TPU v7x, 768 devices: a whole 4x8x12 slice. The times are simulated.
768 devices in a mesh: gx: 96 (over z, x, core), gy: 8 (over y).
Axes of the slice: x: 4, y: 8, z: 12, core: 2. Of those that a mesh axis runs over, the one named last changes fastest.
Arguments:
- recharge: float32 [48, 768, 1024], P(None, 'gx', 'gy'), as said below
- conduct: float32 [48, 768, 1024], P(None, 'gx', 'gy'), may hold values from 0.1 to 10
- top_layer: int32 [768, 1024], P('gx', 'gy'), may hold values from 0 to 24
- fixed_head: int32 [768, 1024], P('gx', 'gy'), may hold values 0 or 1
Outputs:
- head_field: float32 [48, 768, 1024], P(None, 'gx', 'gy')
- residual: float32 [48, 768, 1024], P(None, 'gx', 'gy')
- applied: float32 [48, 768, 1024], P(None, 'gx', 'gy')
Inputs may be any that keep to these rules, and one draw needn't show every extreme that they name: `recharge`: recharge is of order one and its magnitude varies from column to column.
All inputs are finite; a program needn't handle non-finite values. No bound on the sum of `fixed_head` on one device may be relied on, other than what follows from the above.
Results may differ from a plain program's by a relative error of at most 0.0038.
Values sent between devices are 32-bit elements; how exact they have to be, the bound alone decides.
No kernel may reach another device: no remote copies, remote signals or barrier semaphores. Data moves between devices by JAX's collectives and lax.ppermute only.
A program may use at most 64 MiB of HBM per device.

v0:
```python
import jax
import jax.numpy as jnp
from jax import lax
from jax.sharding import PartitionSpec as P

ITERS = 4


store_term = 0.1
boundary_term = 4.0
vertical_ratio = 0.3


def with_halo(block, sides, width):
    for axis, dim in sides:
        count = lax.axis_size(axis)
        forward = [(i, i + 1) for i in range(count - 1)]
        backward = [(target, source) for source, target in forward]
        low = lax.ppermute(
            lax.slice_in_dim(block, block.shape[dim] - width, None, axis=dim), axis, forward
        )
        high = lax.ppermute(lax.slice_in_dim(block, 0, width, axis=dim), axis, backward)
        block = jnp.concatenate([low, block, high], axis=dim)
    return block


def face_coefficients(cond_pad):
    center = cond_pad[1:-1, 1:-1, 1:-1]
    east_c = jnp.sqrt(center * cond_pad[1:-1, 2:, 1:-1])
    west_c = jnp.sqrt(center * cond_pad[1:-1, :-2, 1:-1])
    north_c = jnp.sqrt(center * cond_pad[1:-1, 1:-1, 2:])
    south_c = jnp.sqrt(center * cond_pad[1:-1, 1:-1, :-2])
    upper_c = vertical_ratio * jnp.sqrt(center * cond_pad[2:, 1:-1, 1:-1])
    lower_c = vertical_ratio * jnp.sqrt(center * cond_pad[:-2, 1:-1, 1:-1])
    return (east_c, west_c, north_c, south_c, upper_c, lower_c)


def operate(padded, coeffs, diagonal):
    east_c, west_c, north_c, south_c, upper_c, lower_c = coeffs
    beside = east_c * padded[1:-1, 2:, 1:-1] + west_c * padded[1:-1, :-2, 1:-1]
    beside = beside + north_c * padded[1:-1, 1:-1, 2:] + south_c * padded[1:-1, 1:-1, :-2]
    beside = beside + upper_c * padded[2:, 1:-1, 1:-1] + lower_c * padded[:-2, 1:-1, 1:-1]
    return diagonal * padded[1:-1, 1:-1, 1:-1] - beside


def vertical_pad(field):
    return jnp.pad(field, ((1, 1), (0, 0), (0, 0)))


def vector_pad(field):
    return vertical_pad(with_halo(field, (("gx", 1), ("gy", 2)), 1))


def global_sums(first_sum, second_sum):
    return lax.psum((first_sum, second_sum), ("gx", "gy"))


def local(recharge, conduct, top_layer, fixed_head):
    level = lax.broadcasted_iota(jnp.int32, recharge.shape, 0)
    active = (level >= top_layer[None]).astype(jnp.float32)
    head_cell = ((level == top_layer[None]) & (fixed_head[None] == 1)).astype(jnp.float32)
    active_cond = conduct * active
    cond_rim = with_halo(active_cond, (("gx", 1), ("gy", 2)), 1)
    coeffs = face_coefficients(vertical_pad(cond_rim))
    total = coeffs[0] + coeffs[1] + coeffs[2] + coeffs[3] + coeffs[4] + coeffs[5]
    diagonal = active * (total + store_term + boundary_term * head_cell) + (1.0 - active)
    inverse = 1.0 / diagonal

    def stencil(scaled):
        return operate(vector_pad(scaled), coeffs, diagonal)

    head_field = jnp.zeros_like(recharge)
    residual = recharge * active
    precond = inverse * residual
    applied = stencil(precond)
    dir_image = jnp.zeros_like(recharge)
    dir_scaled = jnp.zeros_like(recharge)
    dir_applied = jnp.zeros_like(recharge)
    direction = jnp.zeros_like(recharge)
    gamma_old = jnp.float32(1.0)
    alpha_old = jnp.float32(1.0)
    for step in range(ITERS):
        inner_pre = precond
        gamma_now, delta_now = global_sums(
            jnp.sum(residual * inner_pre), jnp.sum(applied * inner_pre)
        )
        scaled = inverse * applied
        image = stencil(scaled)
        if step == 0:
            beta_now = jnp.float32(0.0)
            alpha_now = gamma_now / delta_now
        else:
            beta_now = gamma_now / gamma_old
            alpha_now = gamma_now / (delta_now - beta_now * gamma_now / alpha_old)
        dir_image = image + beta_now * dir_image
        dir_scaled = scaled + beta_now * dir_scaled
        dir_applied = applied + beta_now * dir_applied
        direction = precond + beta_now * direction
        head_field = head_field + alpha_now * direction
        residual = residual - alpha_now * dir_applied
        precond = precond - alpha_now * dir_scaled
        applied = applied - alpha_now * dir_image
        gamma_old = gamma_now
        alpha_old = alpha_now
    return (head_field, residual, applied)


def solution(mesh):
    in_specs = (P(None, "gx", "gy"), P(None, "gx", "gy"), P("gx", "gy"), P("gx", "gy"))
    out_specs = (P(None, "gx", "gy"), P(None, "gx", "gy"), P(None, "gx", "gy"))
    return jax.shard_map(local, mesh=mesh, in_specs=in_specs, out_specs=out_specs, check_vma=False)
```

profile of v0, /device:TPU:1, one launch (start us, length us, event | category | flops | bytes accessed | tf_op | source)
XLA Modules:
  0.0 604.2 jit_solution(12478861041649592960)
XLA Ops:
  0.6 0.9 fusion.69
  1.6 12.4 %collective-permute-start = (f32[48,1,128]{2,1,0:T(1,128)S(1)}, f32[48,1,128]{2,1,0:T(1,128)S(1)}, u32[]{:S(2)}, u32[]{:S(2)}) collective-permute-start(f32[48,1,128]{2,1,0:T(1,128)S(1)} %get-tuple-element.61), channel_id=1, source_target_pairs={{8,0},{16,8},{24,16},{32,24},{40,32},{48,40},{56,48},{64,56},{72,6... | collective-permute-start | bytes 73736 | tf_op jit(solution)/shard_map/ppermute | solution.py:22
  14.1 1.9 collective-permute-start.1
  16.0 1.1 collective-permute-done.1
  17.1 0.1 pad_maximum_fusion
  17.2 0.2 fusion.89
  17.4 1.3 collective-permute-start.3
  18.7 1.3 collective-permute-start.2
  20.1 7.2 %collective-permute-done.3 = f32[48,10,1]{2,1,0:T(8,128)S(1)} collective-permute-done((f32[48,10,1]{2,1,0:T(8,128)S(1)}, f32[48,10,1]{2,1,0:T(8,128)S(1)}, u32[]{:S(2)}, u32[]{:S(2)}) %collective-permute-start.3) | collective-permute-done | bytes 1952 | tf_op jit(solution)/shard_map/ppermute | solution.py:19
  27.3 3.9 collective-permute-done.2
  31.2 0.6 select_maximum_fusion.20
  31.8 0.7 fusion.72
  32.6 1.9 collective-permute-start.5
  34.5 2.4 collective-permute-start.4
  36.9 2.7 collective-permute-done.4
  39.7 0.2 fusion.88
  39.9 1.3 collective-permute-start.7
  41.2 1.3 collective-permute-start.6
  42.5 6.4 %collective-permute-done.7 = f32[48,10,1]{2,1,0:T(8,128)S(1)} collective-permute-done((f32[48,10,1]{2,1,0:T(8,128)S(1)}, f32[48,10,1]{2,1,0:T(8,128)S(1)}, u32[]{:S(2)}, u32[]{:S(2)}) %collective-permute-start.7) | collective-permute-done | bytes 1952 | tf_op jit(solution)/shard_map/ppermute | solution.py:19
  48.9 4.1 collective-permute-done.6
  53.0 0.6 select_maximum_fusion.16
  53.6 1.3 multiply_reduce_fusion.6
  54.9 3.2 collective-permute-start.9
  58.1 1.9 collective-permute-start.8
  60.0 3.2 collective-permute-done.8
  63.3 0.9 fusion.87
  64.2 3.5 collective-permute-start.11
  67.7 1.3 collective-permute-start.10
  69.0 122.0 %all-reduce.9 = (f32[]{:T(128)}, f32[]{:T(128)}) all-reduce(f32[]{:T(128)} %get-tuple-element.10, f32[]{:T(128)} %get-tuple-element.9), channel_id=1, replica_groups=mesh['gx'=96,'gy'=8] {'gx','gy'}, use_global_device_ids=true, to_apply=%region_1.2 | all-reduce | flops 2 | bytes 16 | tf_op jit(solution)/shard_map/psum | solution.py:55
  192.4 1.6 select_maximum_fusion.12
  194.0 1.7 fusion.76
  195.7 2.2 collective-permute-start.13
  197.9 2.1 collective-permute-start.12
  200.1 3.0 collective-permute-done.12
  203.1 1.0 fusion.86
  204.1 1.3 collective-permute-start.15
  205.5 1.3 collective-permute-start.14
  206.8 0.7 multiply_reduce_fusion.4
  207.4 113.5 %all-reduce.8 = (f32[]{:T(128)}, f32[]{:T(128)}) all-reduce(f32[]{:T(128)} %get-tuple-element.8, f32[]{:T(128)} %get-tuple-element.7), channel_id=1, replica_groups=mesh['gx'=96,'gy'=8] {'gx','gy'}, use_global_device_ids=true, to_apply=%region_5.6 | all-reduce | flops 2 | bytes 16 | tf_op jit(solution)/shard_map/psum | solution.py:55
  325.5 1.7 select_maximum_fusion.8
  327.2 3.2 multiply_reduce_fusion.2
  330.5 2.2 collective-permute-start.17
  332.7 2.1 collective-permute-start.16
  334.9 3.0 collective-permute-done.16
  337.9 1.0 fusion.85
  338.9 2.4 collective-permute-start.19
  341.3 1.3 collective-permute-start.18
  342.6 114.1 %all-reduce.7 = (f32[]{:T(128)}, f32[]{:T(128)}) all-reduce(f32[]{:T(128)} %get-tuple-element.6, f32[]{:T(128)} %get-tuple-element.5), channel_id=1, replica_groups=mesh['gx'=96,'gy'=8] {'gx','gy'}, use_global_device_ids=true, to_apply=%region_9.10 | all-reduce | flops 2 | bytes 16 | tf_op jit(solution)/shard_map/psum | solution.py:55
  460.5 1.7 select_maximum_fusion.4
  462.3 2.5 fusion.73
  464.9 0.6 fusion.90
  465.5 2.2 collective-permute-start.21
  467.7 2.7 collective-permute-start.20
  470.4 1.4 multiply_reduce_fusion
  471.9 106.5 %all-reduce.6 = (f32[]{:T(128)}, f32[]{:T(128)}) all-reduce(f32[]{:T(128)} %get-tuple-element.4, f32[]{:T(128)} %get-tuple-element.3), channel_id=1, replica_groups=mesh['gx'=96,'gy'=8] {'gx','gy'}, use_global_device_ids=true, to_apply=%region_13.14 | all-reduce | flops 2 | bytes 16 | tf_op jit(solution)/shard_map/psum | solution.py:55
  582.2 0.8 pad_maximum_fusion.5
  583.1 0.2 fusion.84
  583.2 2.9 collective-permute-start.23
  586.1 1.3 collective-permute-start.22
  587.4 0.9 multiply_subtract_fusion
  588.3 6.4 %collective-permute-done.23 = f32[48,10,1]{2,1,0:T(8,128)S(1)} collective-permute-done((f32[48,10,1]{2,1,0:T(8,128)S(1)}, f32[48,10,1]{2,1,0:T(8,128)S(1)}, u32[]{:S(2)}, u32[]{:S(2)}) %collective-permute-start.23) | collective-permute-done | bytes 1952 | tf_op jit(solution)/shard_map/ppermute | solution.py:19
  594.7 5.9 collective-permute-done.22
  600.6 1.3 select_maximum_fusion
  602.0 2.2 fusion.5
  (55 shorter events, 0.6 us)
Async XLA Ops:
  1.6 14.4 %collective-permute-start = (f32[48,1,128]{2,1,0:T(1,128)S(1)}, f32[48,1,128]{2,1,0:T(1,128)S(1)}, u32[]{:S(2)}, u32[]{:S(2)}) collective-permute-start(f32[48,1,128]{2,1,0:T(1,128)S(1)} %get-tuple-element.61), channel_id=1, source_target_pairs={{8,0},{16,8},{24,16},{32,24},{40,32},{48,40},{56,48},{64,56},{72,6... | collective-permute-start | bytes 73736 | tf_op jit(solution)/shard_map/ppermute | solution.py:22
  14.1 3.1 collective-permute-start.1
  16.0 311.2 %copy-start.1 = (f32[48,1,128]{2,1,0:T(1,128)}, f32[48,1,128]{2,1,0:T(1,128)S(1)}, u32[]{:S(2)}) copy-start(f32[48,1,128]{2,1,0:T(1,128)S(1)} %collective-permute-done) | copy-start | bytes 73732
  17.1 310.1 %copy-start.4 = (f32[48,1,128]{2,1,0:T(1,128)}, f32[48,1,128]{2,1,0:T(1,128)S(1)}, u32[]{:S(2)}) copy-start(f32[48,1,128]{2,1,0:T(1,128)S(1)} %collective-permute-done.1) | copy-start | bytes 73732
  17.2 2.8 copy-start.14
  17.4 9.9 %collective-permute-start.3 = (f32[48,10,1]{2,1,0:T(8,128)S(1)}, f32[48,10,1]{2,1,0:T(8,128)S(1)}, u32[]{:S(2)}, u32[]{:S(2)}) collective-permute-start(f32[48,10,1]{2,1,0:T(8,128)S(1)} %get-tuple-element.49), channel_id=1, source_target_pairs={{0,1},{1,2},{2,3},{3,4},{4,5},{5,6},{6,7},{8,9},{9,10},{10,11},{11... | collective-permute-start | bytes 5768 | tf_op jit(solution)/shard_map/ppermute | solution.py:19
  18.7 12.5 %collective-permute-start.2 = (f32[48,10,1]{2,1,0:T(8,128)S(1)}, f32[48,10,1]{2,1,0:T(8,128)S(1)}, u32[]{:S(2)}, u32[]{:S(2)}) collective-permute-start(f32[48,10,1]{2,1,0:T(8,128)S(1)} %get-tuple-element.50), channel_id=1, source_target_pairs={{1,0},{2,1},{3,2},{4,3},{5,4},{6,5},{7,6},{9,8},{10,9},{11,10},{12... | collective-permute-start | bytes 5768 | tf_op jit(solution)/shard_map/ppermute | solution.py:22
  20.1 11.7 %copy-start = (f32[48,8,128]{2,1,0:T(8,128)S(1)}, f32[48,8,128]{2,1,0:T(8,128)}, u32[]{:S(2)}) copy-start(f32[48,8,128]{2,1,0:T(8,128)} %param.4) | copy-start | bytes 589828
  20.1 11.7 %copy-start.11 = (s32[8,128]{1,0:T(8,128)S(1)}, s32[8,128]{1,0:T(8,128)}, u32[]{:S(2)}) copy-start(s32[8,128]{1,0:T(8,128)} %param.6) | copy-start | bytes 12292
  32.6 4.3 collective-permute-start.5
  34.5 5.1 collective-permute-start.4
  39.9 9.0 %collective-permute-start.7 = (f32[48,10,1]{2,1,0:T(8,128)S(1)}, f32[48,10,1]{2,1,0:T(8,128)S(1)}, u32[]{:S(2)}, u32[]{:S(2)}) collective-permute-start(f32[48,10,1]{2,1,0:T(8,128)S(1)} %get-tuple-element.47), channel_id=1, source_target_pairs={{0,1},{1,2},{2,3},{3,4},{4,5},{5,6},{6,7},{8,9},{9,10},{10,11},{11... | collective-permute-start | bytes 5768 | tf_op jit(solution)/shard_map/ppermute | solution.py:19
  41.2 11.8 %collective-permute-start.6 = (f32[48,10,1]{2,1,0:T(8,128)S(1)}, f32[48,10,1]{2,1,0:T(8,128)S(1)}, u32[]{:S(2)}, u32[]{:S(2)}) collective-permute-start(f32[48,10,1]{2,1,0:T(8,128)S(1)} %get-tuple-element.48), channel_id=1, source_target_pairs={{1,0},{2,1},{3,2},{4,3},{5,4},{6,5},{7,6},{9,8},{10,9},{11,10},{12... | collective-permute-start | bytes 5768 | tf_op jit(solution)/shard_map/ppermute | solution.py:22
  54.9 5.1 collective-permute-start.9
  58.1 5.1 collective-permute-start.8
  64.2 128.2 %collective-permute-start.11 = (f32[48,10,1]{2,1,0:T(8,128)}, f32[48,10,1]{2,1,0:T(8,128)S(1)}, u32[]{:S(2)}, u32[]{:S(2)}) collective-permute-start(f32[48,10,1]{2,1,0:T(8,128)} %get-tuple-element.45), channel_id=1, source_target_pairs={{0,1},{1,2},{2,3},{3,4},{4,5},{5,6},{6,7},{8,9},{9,10},{10,11},{11... | collective-permute-start | bytes 5768 | tf_op jit(solution)/shard_map/ppermute | solution.py:19
  67.7 124.7 %collective-permute-start.10 = (f32[48,10,1]{2,1,0:T(8,128)S(1)}, f32[48,10,1]{2,1,0:T(8,128)}, u32[]{:S(2)}, u32[]{:S(2)}) collective-permute-start(f32[48,10,1]{2,1,0:T(8,128)S(1)} %get-tuple-element.46), channel_id=1, source_target_pairs={{1,0},{2,1},{3,2},{4,3},{5,4},{6,5},{7,6},{9,8},{10,9},{11,10},{12... | collective-permute-start | bytes 5768 | tf_op jit(solution)/shard_map/ppermute | solution.py:22
  195.7 4.3 collective-permute-start.13
  197.9 5.1 collective-permute-start.12
  204.1 121.3 %collective-permute-start.15 = (f32[48,10,1]{2,1,0:T(8,128)}, f32[48,10,1]{2,1,0:T(8,128)S(1)}, u32[]{:S(2)}, u32[]{:S(2)}) collective-permute-start(f32[48,10,1]{2,1,0:T(8,128)} %get-tuple-element.43), channel_id=1, source_target_pairs={{0,1},{1,2},{2,3},{3,4},{4,5},{5,6},{6,7},{8,9},{9,10},{10,11},{11... | collective-permute-start | bytes 5768 | tf_op jit(solution)/shard_map/ppermute | solution.py:19
  205.5 120.0 %collective-permute-start.14 = (f32[48,10,1]{2,1,0:T(8,128)}, f32[48,10,1]{2,1,0:T(8,128)}, u32[]{:S(2)}, u32[]{:S(2)}) collective-permute-start(f32[48,10,1]{2,1,0:T(8,128)} %get-tuple-element.44), channel_id=1, source_target_pairs={{1,0},{2,1},{3,2},{4,3},{5,4},{6,5},{7,6},{9,8},{10,9},{11,10},{12... | collective-permute-start | bytes 5768 | tf_op jit(solution)/shard_map/ppermute | solution.py:22
  325.5 1.7 copy-start.7
  330.5 4.3 collective-permute-start.17
  332.7 5.1 collective-permute-start.16
  334.9 125.7 %copy-start.12 = (f32[48,1,128]{2,1,0:T(1,128)}, f32[48,1,128]{2,1,0:T(1,128)S(1)}, u32[]{:S(2)}) copy-start(f32[48,1,128]{2,1,0:T(1,128)S(1)} %collective-permute-done.17) | copy-start | bytes 73732
  337.8 122.7 %copy-start.13 = (f32[48,1,128]{2,1,0:T(1,128)}, f32[48,1,128]{2,1,0:T(1,128)S(1)}, u32[]{:S(2)}) copy-start(f32[48,1,128]{2,1,0:T(1,128)S(1)} %collective-permute-done.16) | copy-start | bytes 73732
  338.9 121.6 %collective-permute-start.19 = (f32[48,10,1]{2,1,0:T(8,128)}, f32[48,10,1]{2,1,0:T(8,128)}, u32[]{:S(2)}, u32[]{:S(2)}) collective-permute-start(f32[48,10,1]{2,1,0:T(8,128)} %get-tuple-element.41), channel_id=1, source_target_pairs={{0,1},{1,2},{2,3},{3,4},{4,5},{5,6},{6,7},{8,9},{9,10},{10,11},{11... | collective-permute-start | bytes 5768 | tf_op jit(solution)/shard_map/ppermute | solution.py:19
  341.3 119.2 %collective-permute-start.18 = (f32[48,10,1]{2,1,0:T(8,128)}, f32[48,10,1]{2,1,0:T(8,128)}, u32[]{:S(2)}, u32[]{:S(2)}) collective-permute-start(f32[48,10,1]{2,1,0:T(8,128)} %get-tuple-element.42), channel_id=1, source_target_pairs={{1,0},{2,1},{3,2},{4,3},{5,4},{6,5},{7,6},{9,8},{10,9},{11,10},{12... | collective-permute-start | bytes 5768 | tf_op jit(solution)/shard_map/ppermute | solution.py:22
  460.5 1.8 copy-start.2
  460.5 1.8 copy-start.5
  460.5 1.8 copy-start.8
  465.5 116.7 %collective-permute-start.21 = (f32[48,1,128]{2,1,0:T(1,128)}, f32[48,1,128]{2,1,0:T(1,128)}, u32[]{:S(2)}, u32[]{:S(2)}) collective-permute-start(f32[48,1,128]{2,1,0:T(1,128)} %get-tuple-element.51), channel_id=1, source_target_pairs={{0,8},{8,16},{16,24},{24,32},{32,40},{40,48},{48,56},{56,64},{64,7... | collective-permute-start | bytes 73736 | tf_op jit(solution)/shard_map/ppermute | solution.py:19
  467.7 114.5 %collective-permute-start.20 = (f32[48,1,128]{2,1,0:T(1,128)}, f32[48,1,128]{2,1,0:T(1,128)}, u32[]{:S(2)}, u32[]{:S(2)}) collective-permute-start(f32[48,1,128]{2,1,0:T(1,128)} %get-tuple-element.52), channel_id=1, source_target_pairs={{8,0},{16,8},{24,16},{32,24},{40,32},{48,40},{56,48},{64,56},{72,6... | collective-permute-start | bytes 73736 | tf_op jit(solution)/shard_map/ppermute | solution.py:22
  583.0 4.4 copy-start.9
  583.2 11.5 %collective-permute-start.23 = (f32[48,10,1]{2,1,0:T(8,128)S(1)}, f32[48,10,1]{2,1,0:T(8,128)S(1)}, u32[]{:S(2)}, u32[]{:S(2)}) collective-permute-start(f32[48,10,1]{2,1,0:T(8,128)S(1)} %get-tuple-element.39), channel_id=1, source_target_pairs={{0,1},{1,2},{2,3},{3,4},{4,5},{5,6},{6,7},{8,9},{9,10},{10,11},{11... | collective-permute-start | bytes 5768 | tf_op jit(solution)/shard_map/ppermute | solution.py:19
  586.1 14.5 %collective-permute-start.22 = (f32[48,10,1]{2,1,0:T(8,128)S(1)}, f32[48,10,1]{2,1,0:T(8,128)S(1)}, u32[]{:S(2)}, u32[]{:S(2)}) collective-permute-start(f32[48,10,1]{2,1,0:T(8,128)S(1)} %get-tuple-element.40), channel_id=1, source_target_pairs={{1,0},{2,1},{3,2},{4,3},{5,4},{6,5},{7,6},{9,8},{10,9},{11,10},{12... | collective-permute-start | bytes 5768 | tf_op jit(solution)/shard_map/ppermute | solution.py:22
  588.3 13.6 %copy-start.3 = (f32[48,1,128]{2,1,0:T(1,128)S(1)}, f32[48,1,128]{2,1,0:T(1,128)}, u32[]{:S(2)}) copy-start(f32[48,1,128]{2,1,0:T(1,128)} %copy-done.1) | copy-start | bytes 73732
  588.3 13.7 %copy-start.6 = (f32[48,1,128]{2,1,0:T(1,128)S(1)}, f32[48,1,128]{2,1,0:T(1,128)}, u32[]{:S(2)}) copy-start(f32[48,1,128]{2,1,0:T(1,128)} %copy-done.4) | copy-start | bytes 73732
  588.3 13.7 %copy-start.10 = (f32[48,8,128]{2,1,0:T(8,128)S(1)}, f32[48,8,128]{2,1,0:T(8,128)}, u32[]{:S(2)}) copy-start(f32[48,8,128]{2,1,0:T(8,128)} %get-tuple-element.21) | copy-start | bytes 589828
where the time goes:
time: 611 us; the launch traced here: 604 us
  blocking collectives  456 us (75%)
  starting transfers between devices  57.7 us (9%)
  waiting for transfers between devices  47 us (8%)
  other arithmetic  24.3 us (4%)
  between operations  14.7 us (2%)
    psum x4, blocking collectives, global_sums(): return lax.psum((first_sum, second_sum), ('gx', 'gy'))  456 us
    ppermute x12, starting transfers between devices, with_halo(): lax.ppermute(lax.slice_in_dim(block, 0, width, axis=dim), axis, backward)  31.4 us
    ppermute x12, starting transfers between devices, with_halo(): lax.ppermute(lax.slice_in_dim(block, block.shape[dim] - width, None, axis...  26.2 us
    ppermute x12, waiting for transfers between devices, with_halo(): lax.ppermute(lax.slice_in_dim(block, 0, width, axis=dim), axis, backward)  25.8 us
    ppermute x12, waiting for transfers between devices, with_halo(): lax.ppermute(lax.slice_in_dim(block, block.shape[dim] - width, None, axis...  21.2 us
  transfers between devices with their start and end apart: 24, of which 11 were waited for; matrix products, arithmetic and copies ran while one was open for 0% of the time, Pallas kernels for 0%

commit v1 on v0

v1 whole, which is shorter than its diff:
```python
import jax
import jax.numpy as jnp
from jax import lax
from jax.experimental import pallas as pl
from jax.experimental.pallas import tpu as pltpu
from jax.sharding import Mesh, PartitionSpec as P

ITERS = 4
LAYERS = 48
ROWS = 8
LANES = 128
SLOTS = 16
PACKED = 7
PLANES = 2 * LAYERS + 1
TALL = 3 * ROWS
MID = 2 * ROWS
BASIS = ITERS + 2

store_term = 0.1
boundary_term = 4.0
vertical_ratio = 0.3

GX = ("z", "x", "c")


def lane_index(rows):
    return lax.broadcasted_iota(jnp.int32, (rows, LANES), 1)


def pack_kernel(recharge, conduct, top_layer, fixed_head, fields, low_edge, high_edge):
    slot = lane_index(ROWS) // 8
    top = top_layer[...]

    def edges(tile, planes):
        low = jnp.zeros((ROWS, LANES), jnp.float32)
        high = jnp.zeros((ROWS, LANES), jnp.float32)
        for m, plane in enumerate(planes):
            turned = plane if m == 0 else pltpu.roll(plane, 8 * m, 1)
            low = jnp.where(slot == m, turned, low)
            high = jnp.where(slot == (m - 1) % SLOTS, turned, high)
        low_edge[tile] = low
        high_edge[tile] = high

    def group(k, _):
        roots, sources = [], []
        for m in range(SLOTS):
            level = k * SLOTS + m
            root = jnp.where(level >= top, jnp.sqrt(conduct[level]), 0.0)
            source = root * recharge[level]
            fields[level] = root
            fields[LAYERS + level] = source
            roots.append(root)
            sources.append(source)
        edges(k, roots)
        edges(LAYERS // SLOTS + k, sources)
        return 0

    lax.fori_loop(0, LAYERS // SLOTS, group, 0)
    fixed = fixed_head[...].astype(jnp.float32)
    fields[2 * LAYERS] = fixed
    edges(PACKED - 1, [fixed])


def beside(center, halo):
    lane = lane_index(center.shape[0])
    c_up, h_up = pltpu.roll(center, LANES - 1, 1), pltpu.roll(halo, LANES - 1, 1)
    c_down, h_down = pltpu.roll(center, 1, 1), pltpu.roll(halo, 1, 1)
    last, first = lane == LANES - 1, lane == 0
    c_sum = jnp.where(last, h_up, c_up) + jnp.where(first, h_down, c_down)
    h_sum = jnp.where(last, c_up, h_up) + jnp.where(first, c_down, h_down)
    return c_sum, h_sum


def around(c_ref, h_ref, base, height, rows):
    c_sum, h_sum = beside(c_ref[pl.ds(base, rows)], h_ref[pl.ds(base, rows)])

    def rest(ref):
        across = ref[pl.ds(base - 1, rows)] + ref[pl.ds(base + 1, rows)]
        vertical = ref[pl.ds(base - height, rows)] + ref[pl.ds(base + height, rows)]
        return across + vertical_ratio * vertical

    return c_sum + rest(c_ref), h_sum + rest(h_ref)


def basis_kernel(own, low, high, basis, inv_root, scale, moments,
                 s_c, s_h, q_c, q_h, f_c, f_h, g_c, g_h, diag, t0_c, t0_h, t_c, t_h):
    lane = lane_index(ROWS)
    rim = (lane < 8) | (lane >= LANES - 8)

    for ref, height in ((s_c, TALL), (s_h, TALL), (t0_c, TALL), (t0_h, TALL)):
        ref[pl.ds(0, height)] = jnp.zeros((height, LANES), jnp.float32)
        ref[pl.ds((LAYERS + 1) * height, height)] = jnp.zeros((height, LANES), jnp.float32)
    for j in range(ITERS):
        for ref in (t_c, t_h):
            ref[j, pl.ds(0, MID)] = jnp.zeros((MID, LANES), jnp.float32)
            ref[j, pl.ds((LAYERS + 1) * MID, MID)] = jnp.zeros((MID, LANES), jnp.float32)

    def halo_lanes(source, tile, m):
        both = jnp.where(lane // 8 == m, source[PLANES + tile], source[PLANES + PACKED + tile])
        turned = both if m == 0 else pltpu.roll(both, LANES - 8 * m, 1)
        return jnp.where(rim, turned, 0.0)

    for part, source in enumerate((low, own, high)):
        def assemble(k, _, source=source, part=part):
            for m in range(SLOTS):
                level = k * SLOTS + m
                row = pl.multiple_of(level * TALL, 8) + part * ROWS
                s_c[pl.ds(row + TALL, ROWS)] = source[level]
                q_c[pl.ds(row, ROWS)] = source[LAYERS + level]
                s_h[pl.ds(row + TALL, ROWS)] = halo_lanes(source, k, m)
                q_h[pl.ds(row, ROWS)] = halo_lanes(source, LAYERS // SLOTS + k, m)
            return 0

        lax.fori_loop(0, LAYERS // SLOTS, assemble, 0)
        f_c[pl.ds(part * ROWS, ROWS)] = boundary_term * source[2 * LAYERS]
        f_h[pl.ds(part * ROWS, ROWS)] = boundary_term * halo_lanes(source, PACKED - 1, 0)

    def first(level, _):
        here = pl.multiple_of(level * TALL, 8)
        base = here + TALL
        sums = around(s_c, s_h, base, TALL, TALL)
        outs = ((s_c, q_c, f_c, g_c, t0_c), (s_h, q_h, f_h, g_h, t0_h))
        for n, (s, q, f, g, t) in enumerate(outs):
            root = s[pl.ds(base, TALL)]
            above = s[pl.ds(base - TALL, TALL)]
            active = root > 0.0
            fixed = jnp.where(above > 0.0, 0.0, f[...])
            d = jnp.where(active, root * sums[n] + (store_term + fixed), 1.0)
            inverse = 1.0 / d
            g[pl.ds(here, TALL)] = root * root * inverse
            t[pl.ds(base, TALL)] = q[pl.ds(here, TALL)] * inverse
            if n == 0:
                diag[level] = d[ROWS:MID]
        return 0

    lax.fori_loop(0, LAYERS, first, 0)

    lead = ROWS // 2

    def second(level, _):
        base = pl.multiple_of((level + 1) * TALL, 8) + lead
        sums = around(t0_c, t0_h, base, TALL, MID)
        to = pl.multiple_of((level + 1) * MID, 8)
        t_c[0, pl.ds(to, MID)] = g_c[pl.ds(base - TALL, MID)] * sums[0]
        t_h[0, pl.ds(to, MID)] = g_h[pl.ds(base - TALL, MID)] * sums[1]
        return 0

    lax.fori_loop(0, LAYERS, second, 0)

    for j in range(1, ITERS):
        def later(level, _, j=j):
            base = pl.multiple_of((level + 1) * MID, 8)
            from_g = pl.multiple_of(level * TALL, 8) + lead
            sums = around(t_c.at[j - 1], t_h.at[j - 1], base, MID, MID)
            if j == 1:
                start = pl.multiple_of((level + 1) * TALL, 8) + lead
                before = t0_c[pl.ds(start, MID)], t0_h[pl.ds(start, MID)]
            else:
                before = t_c[j - 2, pl.ds(base, MID)], t_h[j - 2, pl.ds(base, MID)]
            t_c[j, pl.ds(base, MID)] = 2.0 * g_c[pl.ds(from_g, MID)] * sums[0] - before[0]
            t_h[j, pl.ds(base, MID)] = 2.0 * g_h[pl.ds(from_g, MID)] * sums[1] - before[1]
            return 0

        lax.fori_loop(0, LAYERS, later, 0)

    def last(level, totals):
        base = pl.multiple_of((level + 1) * MID, 8) + lead
        tall = pl.multiple_of(level * TALL, 8) + ROWS
        sums = around(t_c.at[ITERS - 1], t_h.at[ITERS - 1], base, MID, ROWS)
        t = [t0_c[pl.ds(tall + TALL, ROWS)]] + [t_c[j, pl.ds(base, ROWS)] for j in range(ITERS)]
        t.append(2.0 * g_c[pl.ds(tall, ROWS)] * sums[0] - t[ITERS - 1])
        for j in range(BASIS):
            basis[j, level] = t[j]
        root = s_c[pl.ds(tall + TALL, ROWS)]
        inv = jnp.where(root > 0.0, 1.0 / root, 0.0)
        ratio = diag[level] * inv
        inv_root[level] = inv
        scale[level] = ratio
        weight = ratio * inv
        out = []
        for j in range(ITERS):
            weighted = weight * t[j]
            out += [totals[2 * j] + weighted * t[j], totals[2 * j + 1] + weighted * t[j + 1]]
        return tuple(out)

    zero = jnp.zeros((ROWS, LANES), jnp.float32)
    totals = lax.fori_loop(0, LAYERS, last, (zero,) * (2 * ITERS))
    column = lane_index(1)
    row = jnp.zeros((1, LANES), jnp.float32)
    for n, total in enumerate(totals):
        row = jnp.where(column == n, jnp.sum(jnp.sum(total, axis=0, keepdims=True), axis=1, keepdims=True), row)
    moments[...] = row


def added(a, b, factor):
    out = []
    for i in range(max(len(a), len(b))):
        left = a[i] if i < len(a) else None
        right = b[i] if i < len(b) else None
        if right is not None:
            right = factor * right
        out.append(right if left is None else left if right is None else left + right)
    return out


def shifted(a):
    out = [None] * (len(a) + 1)

    def put(i, value):
        out[i] = value if out[i] is None else out[i] + value

    for i, value in enumerate(a):
        if i == 0:
            put(1, value)
        else:
            put(i + 1, 0.5 * value)
            put(i - 1, 0.5 * value)
    return out


def form(a, b, gram):
    total = None
    for i, left in enumerate(a):
        inner = None
        for j, right in enumerate(b):
            if right is None:
                continue
            term = right * gram(i, j)
            inner = term if inner is None else inner + term
        inner = left * inner
        total = inner if total is None else total + inner
    return total


def recursion(moments):
    half = [0.5 * m for m in moments]

    def gram(i, j):
        return moments[i] if j == 0 else moments[j] if i == 0 else half[i + j] + half[abs(i - j)]

    one = jnp.ones_like(moments[0])
    precond, direction, head = [one], [], []
    gamma_old = alpha_old = None
    for step in range(ITERS):
        gamma = form(precond, precond, gram)
        delta = gamma - form(precond, shifted(precond), gram)
        if step == 0:
            direction = precond
            alpha = gamma / delta
        else:
            beta = gamma / gamma_old
            alpha = gamma / (delta - beta * gamma / alpha_old)
            direction = added(precond, direction, beta)
        head = added(head, direction, alpha)
        moved = added(direction, shifted(direction), -1.0)
        precond = added(precond, moved, -alpha)
        gamma_old, alpha_old = gamma, alpha
    return head, precond, added(precond, shifted(precond), -1.0)


def combine_kernel(moments, basis, inv_root, scale, head_field, residual, applied):
    row = jnp.sum(moments[...], axis=0)
    column = lane_index(1)
    raw = []
    for n in range(2 * ITERS):
        value = jnp.sum(jnp.where(column == n, row, 0.0), axis=1, keepdims=True)
        raw.append(jnp.broadcast_to(value, (ROWS, LANES)))
    full = raw[:2]
    for n in range(2, 2 * ITERS):
        full.append(2.0 * raw[n] - raw[n % 2])
    coefficients = recursion(full)

    def write(level, _):
        t = [basis[j, level] for j in range(BASIS)]
        outs = []
        for weights in coefficients:
            total = weights[0] * t[0]
            for j in range(1, len(weights)):
                total = total + weights[j] * t[j]
            outs.append(total)
        factor = scale[level]
        head_field[level] = inv_root[level] * outs[0]
        residual[level] = factor * outs[1]
        applied[level] = factor * outs[2]
        return 0

    lax.fori_loop(0, LAYERS, write, 0)


def f32(*shape):
    return jax.ShapeDtypeStruct(shape, jnp.float32)


def scratch(*shape):
    return pltpu.VMEM(shape, jnp.float32)


def call(kernel, outs, scratches=()):
    whole = pl.BlockSpec(memory_space=pltpu.VMEM)
    return pl.pallas_call(
        kernel,
        out_shape=outs,
        out_specs=[whole] * len(outs),
        scratch_shapes=list(scratches),
        compiler_params=pltpu.CompilerParams(vmem_limit_bytes=32 * 1024 * 1024),
    )


def shift_both(low_going, high_going, axis):
    count = lax.axis_size(axis)
    up = [(i, i + 1) for i in range(count - 1)]
    down = [(target, source) for source, target in up]
    return lax.ppermute(high_going, axis, up), lax.ppermute(low_going, axis, down)


def spread_sum(row, axes):
    count = lax.axis_size(axes)
    got = lax.all_to_all(jnp.broadcast_to(row[None], (count,) + row.shape), axes, 0, 0, tiled=True)
    return got


def local(recharge, conduct, top_layer, fixed_head):
    tile = (ROWS, LANES)
    fields, low_edge, high_edge = call(
        pack_kernel,
        (f32(PLANES + 2 * PACKED, *tile), f32(PACKED, *tile), f32(PACKED, *tile)),
    )(recharge, conduct, top_layer, fixed_head)
    from_low, from_high = shift_both(low_edge, high_edge, "y")
    fields = lax.dynamic_update_slice(fields, jnp.concatenate([from_high, from_low], axis=0), (PLANES, 0, 0))
    low, high = shift_both(fields, fields, GX)

    tall, mid = (LAYERS + 2) * TALL, (LAYERS + 2) * MID
    basis, inv_root, scale, moments = call(
        basis_kernel,
        (f32(BASIS, LAYERS, *tile), f32(LAYERS, *tile), f32(LAYERS, *tile), f32(1, LANES)),
        [scratch(tall, LANES)] * 2 + [scratch(LAYERS * TALL, LANES)] * 2 + [scratch(TALL, LANES)] * 2
        + [scratch(LAYERS * TALL, LANES)] * 2 + [scratch(LAYERS, *tile)] + [scratch(tall, LANES)] * 2
        + [scratch(ITERS, mid, LANES)] * 2,
    )(fields, low, high)

    moments = jnp.sum(spread_sum(moments, ("z", "c")), axis=0)
    moments = spread_sum(moments, ("x", "y"))
    out = f32(LAYERS, *tile)
    return call(combine_kernel, (out, out, out))(moments, basis, inv_root, scale)


def solution(mesh):
    grid = Mesh(mesh.devices.reshape(12, 4, 2, 8), ("z", "x", "c", "y"))
    field, plane = P(None, GX, "y"), P(GX, "y")
    return jax.shard_map(
        local, mesh=grid, in_specs=(field, field, plane, plane), out_specs=(field, field, field), check_vma=False
    )
```

time: 611 us -> 97.4 us (0.16); the launches traced: 604 us -> 97.1 us
  blocking collectives: 456 us -> 39.5 us
  waiting for transfers between devices: 47 us -> 6.31 us
  starting transfers between devices: 57.7 us -> 20.7 us
  Pallas kernels: 0 us -> 26.5 us
  other arithmetic: 24.3 us -> 0.02 us
  between operations: 14.7 us -> 0.71 us
    psum x4 -> x0, blocking collectives: 456 us -> none  [global_sums(): return lax.psum((first_sum, second_sum), ('gx', 'gy'))]
    ppermute x24 -> x4, waiting for transfers between devices: 47 us -> 6.31 us  [the longest x2 6.3 us: shift_both(): lax.ppermute(high_going, axis, up)]
    all_to_all x0 -> x2, blocking collectives: none -> 39.5 us  [spread_sum(): lax.all_to_all(jnp.broadcast_to(row[None], (count,) + row.shape), axes, 0...]
    ppermute x24 -> x4, starting transfers between devices: 57.7 us -> 20.7 us  [the longest x2 14.2 us: shift_both(): lax.ppermute(low_going, axis, down)]
    pallas_call x0 -> x3, Pallas kernels: none -> 26.5 us  [the longest x1 24.6 us: local(): call(basis_kernel, (f32(BASIS, LAYERS, *tile), f32(LAYERS, *tile), f32(LA...]
    concatenate x12 -> x0, other arithmetic: 8.73 us -> none  [with_halo(): block = jnp.concatenate([low, block, high], axis=dim)]
    reduce_sum x4 -> x1, other arithmetic: 6.59 us -> 0.02 us  [local(): moments = jnp.sum(spread_sum(moments, ('z', 'c')), axis=0)]
  transfers between devices with their start and end apart: 24 -> 4, of which waited for: 11 -> 2; matrix products, arithmetic and copies ran while one was open for 0% -> 0% of each run, Pallas kernels for 0% -> 0%
where the time goes in v1:
time: 97.4 us; the launch traced here: 97.1 us
  blocking collectives  39.5 us (41%)
  Pallas kernels  26.5 us (27%)
  starting transfers between devices  20.7 us (21%)
  waiting for transfers between devices  6.31 us (6%)
  local copies, waits for them, and re-layouts  3.26 us (3%)
    all_to_all x2, blocking collectives, spread_sum(): lax.all_to_all(jnp.broadcast_to(row[None], (count,) + row.shape), axes, 0...  39.5 us
    pallas_call x1, Pallas kernels, local(): call(basis_kernel, (f32(BASIS, LAYERS, *tile), f32(LAYERS, *tile), f32(LA...  24.6 us
    ppermute x2, starting transfers between devices, shift_both(): lax.ppermute(low_going, axis, down)  14.2 us
    ppermute x2, starting transfers between devices, shift_both(): lax.ppermute(high_going, axis, up)  6.58 us
    ppermute x2, waiting for transfers between devices, shift_both(): lax.ppermute(high_going, axis, up)  6.3 us
    unnamed x8, local copies, waits for them, and re-layouts  3.22 us
  transfers between devices with their start and end apart: 4, of which 2 were waited for; matrix products, arithmetic and copies ran while one was open for 0% of the time, Pallas kernels for 0%

profile of v1, /device:TPU:1, one launch (start us, length us, event | category | flops | bytes accessed | tf_op | source)
XLA Modules:
  0.0 97.1 jit_solution(12049765107312593863)
XLA Ops:
  0.6 0.0 copy-start
  0.6 0.9 copy-done
  1.6 0.0 copy-start.1
  1.6 0.9 copy-done.1
  2.5 0.0 copy-start.2
  2.5 0.7 copy-done.2
  3.2 0.0 copy-start.3
  3.2 0.7 copy-done.3
  3.9 0.3 shard_map.67
  4.2 1.3 %collective-permute-start = (f32[7,8,128]{2,1,0:T(8,128)S(1)}, f32[7,8,128]{2,1,0:T(8,128)S(1)}, u32[]{:S(2)}, u32[]{:S(2)}) collective-permute-start(f32[7,8,128]{2,1,0:T(8,128)S(1)} %get-tuple-element.11), channel_id=1, source_target_pairs={{1,0},{2,1},{3,2},{4,3},{5,4},{6,5},{7,6},{9,8},{10,9},{11,10},{12... | collective-permute-start | bytes 86024 | tf_op jit(solution)/shard_map/ppermute | solution.py:313
  5.5 4.7 %collective-permute-start.1 = (f32[7,8,128]{2,1,0:T(8,128)S(1)}, f32[7,8,128]{2,1,0:T(8,128)S(1)}, u32[]{:S(2)}, u32[]{:S(2)}) collective-permute-start(f32[7,8,128]{2,1,0:T(8,128)S(1)} %get-tuple-element.12), channel_id=1, source_target_pairs={{0,1},{1,2},{2,3},{3,4},{4,5},{5,6},{6,7},{8,9},{9,10},{10,11},{11... | collective-permute-start | bytes 86024 | tf_op jit(solution)/shard_map/ppermute | solution.py:313
  10.2 0.0 collective-permute-done
  10.2 1.0 collective-permute-done.1
  11.1 12.9 %collective-permute-start.3 = (f32[111,8,128]{2,1,0:T(8,128)S(1)}, f32[111,8,128]{2,1,0:T(8,128)S(1)}, u32[]{:S(2)}, u32[]{:S(2)}) collective-permute-start(f32[111,8,128]{2,1,0:T(8,128)S(1)} %maximum_dynamic-update-slice_fusion.own), channel_id=1, source_target_pairs={{8,0},{16,8},{24,16},{32,24},{40,32},{48,40},{56,48},{64,56},{72,6... | collective-permute-start | bytes 1363976 | tf_op jit(solution)/shard_map/ppermute | solution.py:313
  24.0 1.9 %collective-permute-start.2 = (f32[111,8,128]{2,1,0:T(8,128)S(1)}, f32[111,8,128]{2,1,0:T(8,128)S(1)}, u32[]{:S(2)}, u32[]{:S(2)}) collective-permute-start(f32[111,8,128]{2,1,0:T(8,128)S(1)} %maximum_dynamic-update-slice_fusion.own), channel_id=1, source_target_pairs={{0,8},{8,16},{16,24},{24,32},{32,40},{40,48},{48,56},{56,64},{64,7... | collective-permute-start | bytes 1363976 | tf_op jit(solution)/shard_map/ppermute | solution.py:313
  25.9 0.0 collective-permute-done.3.high
  26.0 5.3 %collective-permute-done.2.low = f32[111,8,128]{2,1,0:T(8,128)S(1)} collective-permute-done((f32[111,8,128]{2,1,0:T(8,128)S(1)}, f32[111,8,128]{2,1,0:T(8,128)S(1)}, u32[]{:S(2)}, u32[]{:S(2)}) %collective-permute-start.2) | collective-permute-done | bytes 454688 | tf_op jit(solution)/shard_map/ppermute | solution.py:313
  31.3 24.6 %shard_map.68 = (f32[6,48,8,128]{3,2,1,0:T(8,128)S(1)}, f32[48,8,128]{2,1,0:T(8,128)S(1)}, f32[48,8,128]{2,1,0:T(8,128)S(1)}, f32[1,128]{1,0:T(1,128)S(1)}) custom-call(f32[111,8,128]{2,1,0:T(8,128)S(1)} %maximum_dynamic-update-slice_fusion.own, f32[111,8,128]{2,1,0:T(8,128)S(1)} %collective-permute-done.2.low, f32[111,8,128]{2,1,0:T(8,128)S(1)} %collective-permute-done.3.high), custom_call_target="tpu_custom_call" | custom-call | tf_op jit(solution)/shard_map/pallas_call | solution.py:333
  56.0 22.2 %all_to_all.10 = f32[24,1,128]{2,1,0:T(1,128)S(1)} all-to-all(f32[24,1,128]{2,1,0:T(1,128)S(1)} %broadcast_in_dim.7), channel_id=1, replica_groups=mesh['z'=12,'x'=4,'c'=2,'y'=8] {'z','c'}, dimensions={0} | all-to-all | bytes 24576 | tf_op jit(solution)/shard_map/all_to_all | solution.py:318
  78.2 17.3 %all_to_all.11.moments = f32[32,1,128]{2,1,0:T(1,128)S(1)} all-to-all(f32[32,1,128]{2,1,0:T(1,128)S(1)} %broadcast_in_dim.16), channel_id=1, replica_groups=mesh['z'=12,'x'=4,'c'=2,'y'=8] {'x','y'}, dimensions={0} | all-to-all | bytes 32768 | tf_op jit(solution)/shard_map/all_to_all | solution.py:318
  95.5 1.5 %shard_map.69 = (f32[48,8,128]{2,1,0:T(8,128)}, f32[48,8,128]{2,1,0:T(8,128)}, f32[48,8,128]{2,1,0:T(8,128)}) custom-call(f32[32,1,128]{2,1,0:T(1,128)S(1)} %all_to_all.11.moments, f32[6,48,8,128]{3,2,1,0:T(8,128)S(1)} %get-tuple-element.14.basis, f32[48,8,128]{2,1,0:T(8,128)S(1)} %get-tuple-element.15.inv_root, f32[48,8,128]{2,1,0:T(8,128)S(1)} %get-tuple-element.16.scale), custom_call_target="tpu_custom_call" | custom-call | tf_op jit(solution)/shard_map/pallas_call | solution.py:344
  (4 shorter events, 0.1 us)
Async XLA Ops:
  0.6 0.9 copy-start
  1.6 0.9 copy-start.1
  2.5 0.7 copy-start.2
  3.2 0.7 copy-start.3
  4.2 6.0 %collective-permute-start = (f32[7,8,128]{2,1,0:T(8,128)S(1)}, f32[7,8,128]{2,1,0:T(8,128)S(1)}, u32[]{:S(2)}, u32[]{:S(2)}) collective-permute-start(f32[7,8,128]{2,1,0:T(8,128)S(1)} %get-tuple-element.11), channel_id=1, source_target_pairs={{1,0},{2,1},{3,2},{4,3},{5,4},{6,5},{7,6},{9,8},{10,9},{11,10},{12... | collective-permute-start | bytes 86024 | tf_op jit(solution)/shard_map/ppermute | solution.py:313
  5.5 5.6 %collective-permute-start.1 = (f32[7,8,128]{2,1,0:T(8,128)S(1)}, f32[7,8,128]{2,1,0:T(8,128)S(1)}, u32[]{:S(2)}, u32[]{:S(2)}) collective-permute-start(f32[7,8,128]{2,1,0:T(8,128)S(1)} %get-tuple-element.12), channel_id=1, source_target_pairs={{0,1},{1,2},{2,3},{3,4},{4,5},{5,6},{6,7},{8,9},{9,10},{10,11},{11... | collective-permute-start | bytes 86024 | tf_op jit(solution)/shard_map/ppermute | solution.py:313
  11.1 14.8 %collective-permute-start.3 = (f32[111,8,128]{2,1,0:T(8,128)S(1)}, f32[111,8,128]{2,1,0:T(8,128)S(1)}, u32[]{:S(2)}, u32[]{:S(2)}) collective-permute-start(f32[111,8,128]{2,1,0:T(8,128)S(1)} %maximum_dynamic-update-slice_fusion.own), channel_id=1, source_target_pairs={{8,0},{16,8},{24,16},{32,24},{40,32},{48,40},{56,48},{64,56},{72,6... | collective-permute-start | bytes 1363976 | tf_op jit(solution)/shard_map/ppermute | solution.py:313
  24.0 7.3 %collective-permute-start.2 = (f32[111,8,128]{2,1,0:T(8,128)S(1)}, f32[111,8,128]{2,1,0:T(8,128)S(1)}, u32[]{:S(2)}, u32[]{:S(2)}) collective-permute-start(f32[111,8,128]{2,1,0:T(8,128)S(1)} %maximum_dynamic-update-slice_fusion.own), channel_id=1, source_target_pairs={{0,8},{8,16},{16,24},{24,32},{32,40},{40,48},{48,56},{56,64},{64,7... | collective-permute-start | bytes 1363976 | tf_op jit(solution)/shard_map/ppermute | solution.py:313

commit v2 on v1

--- a/solution.py
+++ b/solution.py
@@ -82,8 +82,25 @@
     return c_sum + rest(c_ref), h_sum + rest(h_ref)
 
 
+def put(stores):
+    for ref, where, value in stores:
+        ref[where] = value
+
+
+def over_layers(step, unroll):
+    def block(k, _):
+        stores = []
+        for m in range(unroll):
+            stores += step(k * unroll + m)
+        put(stores)
+        return 0
+
+    lax.fori_loop(0, LAYERS // unroll, block, 0)
+
+
 def basis_kernel(own, low, high, basis, inv_root, scale, moments,
-                 s_c, s_h, q_c, q_h, f_c, f_h, g_c, g_h, diag, t0_c, t0_h, t_c, t_h):
+                 s_c, s_h, q_c, q_h, f_c, f_h, g_c, g_h, diag, t0_c, t0_h, *t_refs):
+    t_c, t_h = t_refs[:ITERS], t_refs[ITERS:]
     lane = lane_index(ROWS)
     rim = (lane < 8) | (lane >= LANES - 8)
 
@@ -91,9 +108,9 @@
         ref[pl.ds(0, height)] = jnp.zeros((height, LANES), jnp.float32)
         ref[pl.ds((LAYERS + 1) * height, height)] = jnp.zeros((height, LANES), jnp.float32)
     for j in range(ITERS):
-        for ref in (t_c, t_h):
-            ref[j, pl.ds(0, MID)] = jnp.zeros((MID, LANES), jnp.float32)
-            ref[j, pl.ds((LAYERS + 1) * MID, MID)] = jnp.zeros((MID, LANES), jnp.float32)
+        for ref in (t_c[j], t_h[j]):
+            ref[pl.ds(0, MID)] = jnp.zeros((MID, LANES), jnp.float32)
+            ref[pl.ds((LAYERS + 1) * MID, MID)] = jnp.zeros((MID, LANES), jnp.float32)
 
     def halo_lanes(source, tile, m):
         both = jnp.where(lane // 8 == m, source[PLANES + tile], source[PLANES + PACKED + tile])
@@ -115,10 +132,11 @@
         f_c[pl.ds(part * ROWS, ROWS)] = boundary_term * source[2 * LAYERS]
         f_h[pl.ds(part * ROWS, ROWS)] = boundary_term * halo_lanes(source, PACKED - 1, 0)
 
-    def first(level, _):
+    def first(level):
         here = pl.multiple_of(level * TALL, 8)
         base = here + TALL
         sums = around(s_c, s_h, base, TALL, TALL)
+        stores = []
         outs = ((s_c, q_c, f_c, g_c, t0_c), (s_h, q_h, f_h, g_h, t0_h))
         for n, (s, q, f, g, t) in enumerate(outs):
             root = s[pl.ds(base, TALL)]
@@ -127,64 +145,74 @@
             fixed = jnp.where(above > 0.0, 0.0, f[...])
             d = jnp.where(active, root * sums[n] + (store_term + fixed), 1.0)
             inverse = 1.0 / d
-            g[pl.ds(here, TALL)] = root * root * inverse
-            t[pl.ds(base, TALL)] = q[pl.ds(here, TALL)] * inverse
+            stores.append((g, (pl.ds(here, TALL),), root * root * inverse))
+            stores.append((t, (pl.ds(base, TALL),), q[pl.ds(here, TALL)] * inverse))
             if n == 0:
-                diag[level] = d[ROWS:MID]
-        return 0
-
-    lax.fori_loop(0, LAYERS, first, 0)
+                stores.append((diag, (level,), d[ROWS:MID]))
+        return stores
+
+    over_layers(first, 8)
 
     lead = ROWS // 2
 
-    def second(level, _):
+    def second(level):
         base = pl.multiple_of((level + 1) * TALL, 8) + lead
         sums = around(t0_c, t0_h, base, TALL, MID)
-        to = pl.multiple_of((level + 1) * MID, 8)
-        t_c[0, pl.ds(to, MID)] = g_c[pl.ds(base - TALL, MID)] * sums[0]
-        t_h[0, pl.ds(to, MID)] = g_h[pl.ds(base - TALL, MID)] * sums[1]
-        return 0
-
-    lax.fori_loop(0, LAYERS, second, 0)
+        to = (pl.ds(pl.multiple_of((level + 1) * MID, 8), MID),)
+        return [
+            (t_c[0], to, g_c[pl.ds(base - TALL, MID)] * sums[0]),
+            (t_h[0], to, g_h[pl.ds(base - TALL, MID)] * sums[1]),
+        ]
+
+    over_layers(second, 16)
 
     for j in range(1, ITERS):
-        def later(level, _, j=j):
+        def later(level, j=j):
             base = pl.multiple_of((level + 1) * MID, 8)
             from_g = pl.multiple_of(level * TALL, 8) + lead
-            sums = around(t_c.at[j - 1], t_h.at[j - 1], base, MID, MID)
+            sums = around(t_c[j - 1], t_h[j - 1], base, MID, MID)
             if j == 1:
                 start = pl.multiple_of((level + 1) * TALL, 8) + lead
                 before = t0_c[pl.ds(start, MID)], t0_h[pl.ds(start, MID)]
             else:
-                before = t_c[j - 2, pl.ds(base, MID)], t_h[j - 2, pl.ds(base, MID)]
-            t_c[j, pl.ds(base, MID)] = 2.0 * g_c[pl.ds(from_g, MID)] * sums[0] - before[0]
-            t_h[j, pl.ds(base, MID)] = 2.0 * g_h[pl.ds(from_g, MID)] * sums[1] - before[1]
-            return 0
-
-        lax.fori_loop(0, LAYERS, later, 0)
-
-    def last(level, totals):
+                before = t_c[j - 2][pl.ds(base, MID)], t_h[j - 2][pl.ds(base, MID)]
+            to = (pl.ds(base, MID),)
+            return [
+                (t_c[j], to, 2.0 * g_c[pl.ds(from_g, MID)] * sums[0] - before[0]),
+                (t_h[j], to, 2.0 * g_h[pl.ds(from_g, MID)] * sums[1] - before[1]),
+            ]
+
+        over_layers(later, 16)
+
+    def last(level):
         base = pl.multiple_of((level + 1) * MID, 8) + lead
         tall = pl.multiple_of(level * TALL, 8) + ROWS
-        sums = around(t_c.at[ITERS - 1], t_h.at[ITERS - 1], base, MID, ROWS)
-        t = [t0_c[pl.ds(tall + TALL, ROWS)]] + [t_c[j, pl.ds(base, ROWS)] for j in range(ITERS)]
+        sums = around(t_c[ITERS - 1], t_h[ITERS - 1], base, MID, ROWS)
+        t = [t0_c[pl.ds(tall + TALL, ROWS)]] + [t_c[j][pl.ds(base, ROWS)] for j in range(ITERS)]
         t.append(2.0 * g_c[pl.ds(tall, ROWS)] * sums[0] - t[ITERS - 1])
-        for j in range(BASIS):
-            basis[j, level] = t[j]
         root = s_c[pl.ds(tall + TALL, ROWS)]
         inv = jnp.where(root > 0.0, 1.0 / root, 0.0)
         ratio = diag[level] * inv
-        inv_root[level] = inv
-        scale[level] = ratio
         weight = ratio * inv
-        out = []
+        stores = [(basis, (j, level), t[j]) for j in range(BASIS)]
+        stores += [(inv_root, (level,), inv), (scale, (level,), ratio)]
+        terms = []
         for j in range(ITERS):
             weighted = weight * t[j]
-            out += [totals[2 * j] + weighted * t[j], totals[2 * j + 1] + weighted * t[j + 1]]
-        return tuple(out)
+            terms += [weighted * t[j], weighted * t[j + 1]]
+        return stores, terms
+
+    def last_block(k, totals):
+        stores = []
+        for m in range(8):
+            more, terms = last(k * 8 + m)
+            stores += more
+            totals = tuple(a + b for a, b in zip(totals, terms))
+        put(stores)
+        return totals
 
     zero = jnp.zeros((ROWS, LANES), jnp.float32)
-    totals = lax.fori_loop(0, LAYERS, last, (zero,) * (2 * ITERS))
+    totals = lax.fori_loop(0, LAYERS // 8, last_block, (zero,) * (2 * ITERS))
     column = lane_index(1)
     row = jnp.zeros((1, LANES), jnp.float32)
     for n, total in enumerate(totals):
@@ -319,29 +347,35 @@
     return got
 
 
+def pack(recharge, conduct, top_layer, fixed_head):
+    shapes = (f32(PLANES + 2 * PACKED, ROWS, LANES), f32(PACKED, ROWS, LANES), f32(PACKED, ROWS, LANES))
+    return call(pack_kernel, shapes)(recharge, conduct, top_layer, fixed_head)
+
+
+def make_basis(fields, low, high):
+    field = f32(LAYERS, ROWS, LANES)
+    tall, mid = (LAYERS + 2) * TALL, (LAYERS + 2) * MID
+    plain = LAYERS * TALL
+    scratches = [scratch(tall, LANES)] * 2 + [scratch(plain, LANES)] * 2 + [scratch(TALL, LANES)] * 2
+    scratches += [scratch(plain, LANES)] * 2 + [scratch(LAYERS, ROWS, LANES)] + [scratch(tall, LANES)] * 2
+    scratches += [scratch(mid, LANES)] * (2 * ITERS)
+    outs = (f32(BASIS, LAYERS, ROWS, LANES), field, field, f32(1, LANES))
+    return call(basis_kernel, outs, scratches)(fields, low, high)
+
+
+def combine(moments, basis, inv_root, scale):
+    return call(combine_kernel, (f32(LAYERS, ROWS, LANES),) * 3)(moments, basis, inv_root, scale)
+
+
 def local(recharge, conduct, top_layer, fixed_head):
-    tile = (ROWS, LANES)
-    fields, low_edge, high_edge = call(
-        pack_kernel,
-        (f32(PLANES + 2 * PACKED, *tile), f32(PACKED, *tile), f32(PACKED, *tile)),
-    )(recharge, conduct, top_layer, fixed_head)
+    fields, low_edge, high_edge = pack(recharge, conduct, top_layer, fixed_head)
     from_low, from_high = shift_both(low_edge, high_edge, "y")
     fields = lax.dynamic_update_slice(fields, jnp.concatenate([from_high, from_low], axis=0), (PLANES, 0, 0))
     low, high = shift_both(fields, fields, GX)
-
-    tall, mid = (LAYERS + 2) * TALL, (LAYERS + 2) * MID
-    basis, inv_root, scale, moments = call(
-        basis_kernel,
-        (f32(BASIS, LAYERS, *tile), f32(LAYERS, *tile), f32(LAYERS, *tile), f32(1, LANES)),
-        [scratch(tall, LANES)] * 2 + [scratch(LAYERS * TALL, LANES)] * 2 + [scratch(TALL, LANES)] * 2
-        + [scratch(LAYERS * TALL, LANES)] * 2 + [scratch(LAYERS, *tile)] + [scratch(tall, LANES)] * 2
-        + [scratch(ITERS, mid, LANES)] * 2,
-    )(fields, low, high)
-
+    basis, inv_root, scale, moments = make_basis(fields, low, high)
     moments = jnp.sum(spread_sum(moments, ("z", "c")), axis=0)
     moments = spread_sum(moments, ("x", "y"))
-    out = f32(LAYERS, *tile)
-    return call(combine_kernel, (out, out, out))(moments, basis, inv_root, scale)
+    return combine(moments, basis, inv_root, scale)
 
 
 def solution(mesh):

time: 97.4 us -> 78.3 us (0.80)
  Pallas kernels: 26.5 us -> 7.36 us
    pallas_call x3, Pallas kernels: 26.5 us -> 7.36 us  [the longest x1 5.51 us: make_basis(): return call(basis_kernel, outs, scratches)(fields, low, high)]
where the time goes in v2:
time: 78.3 us; the launch traced here: 77.9 us
  blocking collectives  39.5 us (50%)
  starting transfers between devices  20.7 us (26%)
  Pallas kernels  7.36 us (9%)
  waiting for transfers between devices  6.31 us (8%)
  local copies, waits for them, and re-layouts  3.25 us (4%)
    all_to_all x2, blocking collectives, spread_sum(): lax.all_to_all(jnp.broadcast_to(row[None], (count,) + row.shape), axes, 0...  39.5 us
    ppermute x2, starting transfers between devices, shift_both(): lax.ppermute(low_going, axis, down)  14.2 us
    ppermute x2, starting transfers between devices, shift_both(): lax.ppermute(high_going, axis, up)  6.58 us
    ppermute x2, waiting for transfers between devices, shift_both(): lax.ppermute(high_going, axis, up)  6.3 us
    pallas_call x1, Pallas kernels, make_basis(): return call(basis_kernel, outs, scratches)(fields, low, high)  5.51 us
    unnamed x8, local copies, waits for them, and re-layouts  3.22 us
  transfers between devices with their start and end apart: 4, of which 2 were waited for; matrix products, arithmetic and copies ran while one was open for 0% of the time, Pallas kernels for 0%

profile of v2, /device:TPU:1, one launch (start us, length us, event | category | flops | bytes accessed | tf_op | source)
XLA Modules:
  0.0 77.9 jit_solution(2797266314485525440)
XLA Ops:
  0.6 0.0 copy-start
  0.6 0.9 %copy-done = f32[48,8,128]{2,1,0:T(8,128)S(1)} copy-done((f32[48,8,128]{2,1,0:T(8,128)S(1)}, f32[48,8,128]{2,1,0:T(8,128)}, u32[]{:S(2)}) %copy-start) | copy-done | bytes 196632
  1.6 0.0 copy-start.1
  1.6 0.9 %copy-done.1 = f32[48,8,128]{2,1,0:T(8,128)S(1)} copy-done((f32[48,8,128]{2,1,0:T(8,128)S(1)}, f32[48,8,128]{2,1,0:T(8,128)}, u32[]{:S(2)}) %copy-start.1) | copy-done | bytes 196632
  2.5 0.0 copy-start.2
  2.5 0.7 copy-done.2
  3.2 0.0 copy-start.3
  3.2 0.7 copy-done.3
  3.9 0.3 shard_map.67
  4.2 1.3 %collective-permute-start = (f32[7,8,128]{2,1,0:T(8,128)S(1)}, f32[7,8,128]{2,1,0:T(8,128)S(1)}, u32[]{:S(2)}, u32[]{:S(2)}) collective-permute-start(f32[7,8,128]{2,1,0:T(8,128)S(1)} %get-tuple-element.11), channel_id=1, source_target_pairs={{1,0},{2,1},{3,2},{4,3},{5,4},{6,5},{7,6},{9,8},{10,9},{11,10},{12... | collective-permute-start | bytes 86024 | tf_op jit(solution)/shard_map/ppermute | solution.py:341
  5.5 4.7 %collective-permute-start.1 = (f32[7,8,128]{2,1,0:T(8,128)S(1)}, f32[7,8,128]{2,1,0:T(8,128)S(1)}, u32[]{:S(2)}, u32[]{:S(2)}) collective-permute-start(f32[7,8,128]{2,1,0:T(8,128)S(1)} %get-tuple-element.12), channel_id=1, source_target_pairs={{0,1},{1,2},{2,3},{3,4},{4,5},{5,6},{6,7},{8,9},{9,10},{10,11},{11... | collective-permute-start | bytes 86024 | tf_op jit(solution)/shard_map/ppermute | solution.py:341
  10.2 0.0 collective-permute-done
  10.2 1.0 %collective-permute-done.1 = f32[7,8,128]{2,1,0:T(8,128)S(1)} collective-permute-done((f32[7,8,128]{2,1,0:T(8,128)S(1)}, f32[7,8,128]{2,1,0:T(8,128)S(1)}, u32[]{:S(2)}, u32[]{:S(2)}) %collective-permute-start.1) | collective-permute-done | bytes 28704 | tf_op jit(solution)/shard_map/ppermute | solution.py:341
  11.1 12.9 %collective-permute-start.3 = (f32[111,8,128]{2,1,0:T(8,128)S(1)}, f32[111,8,128]{2,1,0:T(8,128)S(1)}, u32[]{:S(2)}, u32[]{:S(2)}) collective-permute-start(f32[111,8,128]{2,1,0:T(8,128)S(1)} %maximum_dynamic-update-slice_fusion.own), channel_id=1, source_target_pairs={{8,0},{16,8},{24,16},{32,24},{40,32},{48,40},{56,48},{64,56},{72,6... | collective-permute-start | bytes 1363976 | tf_op jit(solution)/shard_map/ppermute | solution.py:341
  24.0 1.9 %collective-permute-start.2 = (f32[111,8,128]{2,1,0:T(8,128)S(1)}, f32[111,8,128]{2,1,0:T(8,128)S(1)}, u32[]{:S(2)}, u32[]{:S(2)}) collective-permute-start(f32[111,8,128]{2,1,0:T(8,128)S(1)} %maximum_dynamic-update-slice_fusion.own), channel_id=1, source_target_pairs={{0,8},{8,16},{16,24},{24,32},{32,40},{40,48},{48,56},{56,64},{64,7... | collective-permute-start | bytes 1363976 | tf_op jit(solution)/shard_map/ppermute | solution.py:341
  25.9 0.0 collective-permute-done.3.high
  26.0 5.3 %collective-permute-done.2.low = f32[111,8,128]{2,1,0:T(8,128)S(1)} collective-permute-done((f32[111,8,128]{2,1,0:T(8,128)S(1)}, f32[111,8,128]{2,1,0:T(8,128)S(1)}, u32[]{:S(2)}, u32[]{:S(2)}) %collective-permute-start.2) | collective-permute-done | bytes 454688 | tf_op jit(solution)/shard_map/ppermute | solution.py:341
  31.3 5.5 %shard_map.68 = (f32[6,48,8,128]{3,2,1,0:T(8,128)S(1)}, f32[48,8,128]{2,1,0:T(8,128)S(1)}, f32[48,8,128]{2,1,0:T(8,128)S(1)}, f32[1,128]{1,0:T(1,128)S(1)}) custom-call(f32[111,8,128]{2,1,0:T(8,128)S(1)} %maximum_dynamic-update-slice_fusion.own, f32[111,8,128]{2,1,0:T(8,128)S(1)} %collective-permute-done.2.low, f32[111,8,128]{2,1,0:T(8,128)S(1)} %collective-permute-done.3.high), custom_call_target="tpu_custom_call" | custom-call | tf_op jit(solution)/shard_map/pallas_call | solution.py:363
  36.8 22.2 %all_to_all.10 = f32[24,1,128]{2,1,0:T(1,128)S(1)} all-to-all(f32[24,1,128]{2,1,0:T(1,128)S(1)} %broadcast_in_dim.7), channel_id=1, replica_groups=mesh['z'=12,'x'=4,'c'=2,'y'=8] {'z','c'}, dimensions={0} | all-to-all | bytes 24576 | tf_op jit(solution)/shard_map/all_to_all | solution.py:346
  59.1 17.3 %all_to_all.11.moments = f32[32,1,128]{2,1,0:T(1,128)S(1)} all-to-all(f32[32,1,128]{2,1,0:T(1,128)S(1)} %broadcast_in_dim.16), channel_id=1, replica_groups=mesh['z'=12,'x'=4,'c'=2,'y'=8] {'x','y'}, dimensions={0} | all-to-all | bytes 32768 | tf_op jit(solution)/shard_map/all_to_all | solution.py:346
  76.4 1.5 %shard_map.69 = (f32[48,8,128]{2,1,0:T(8,128)}, f32[48,8,128]{2,1,0:T(8,128)}, f32[48,8,128]{2,1,0:T(8,128)}) custom-call(f32[32,1,128]{2,1,0:T(1,128)S(1)} %all_to_all.11.moments, f32[6,48,8,128]{3,2,1,0:T(8,128)S(1)} %get-tuple-element.14.basis, f32[48,8,128]{2,1,0:T(8,128)S(1)} %get-tuple-element.15.inv_root, f32[48,8,128]{2,1,0:T(8,128)S(1)} %get-tuple-element.16.scale), custom_call_target="tpu_custom_call" | custom-call | tf_op jit(solution)/shard_map/pallas_call | solution.py:367
  (4 shorter events, 0.1 us)
Async XLA Ops:
  0.6 0.9 %copy-start = (f32[48,8,128]{2,1,0:T(8,128)S(1)}, f32[48,8,128]{2,1,0:T(8,128)}, u32[]{:S(2)}) copy-start(f32[48,8,128]{2,1,0:T(8,128)} %recharge.1) | copy-start | bytes 589828
  1.6 0.9 %copy-start.1 = (f32[48,8,128]{2,1,0:T(8,128)S(1)}, f32[48,8,128]{2,1,0:T(8,128)}, u32[]{:S(2)}) copy-start(f32[48,8,128]{2,1,0:T(8,128)} %conduct.1) | copy-start | bytes 589828
  2.5 0.7 copy-start.2
  3.2 0.7 copy-start.3
  4.2 6.0 %collective-permute-start = (f32[7,8,128]{2,1,0:T(8,128)S(1)}, f32[7,8,128]{2,1,0:T(8,128)S(1)}, u32[]{:S(2)}, u32[]{:S(2)}) collective-permute-start(f32[7,8,128]{2,1,0:T(8,128)S(1)} %get-tuple-element.11), channel_id=1, source_target_pairs={{1,0},{2,1},{3,2},{4,3},{5,4},{6,5},{7,6},{9,8},{10,9},{11,10},{12... | collective-permute-start | bytes 86024 | tf_op jit(solution)/shard_map/ppermute | solution.py:341
  5.5 5.6 %collective-permute-start.1 = (f32[7,8,128]{2,1,0:T(8,128)S(1)}, f32[7,8,128]{2,1,0:T(8,128)S(1)}, u32[]{:S(2)}, u32[]{:S(2)}) collective-permute-start(f32[7,8,128]{2,1,0:T(8,128)S(1)} %get-tuple-element.12), channel_id=1, source_target_pairs={{0,1},{1,2},{2,3},{3,4},{4,5},{5,6},{6,7},{8,9},{9,10},{10,11},{11... | collective-permute-start | bytes 86024 | tf_op jit(solution)/shard_map/ppermute | solution.py:341
  11.1 14.8 %collective-permute-start.3 = (f32[111,8,128]{2,1,0:T(8,128)S(1)}, f32[111,8,128]{2,1,0:T(8,128)S(1)}, u32[]{:S(2)}, u32[]{:S(2)}) collective-permute-start(f32[111,8,128]{2,1,0:T(8,128)S(1)} %maximum_dynamic-update-slice_fusion.own), channel_id=1, source_target_pairs={{8,0},{16,8},{24,16},{32,24},{40,32},{48,40},{56,48},{64,56},{72,6... | collective-permute-start | bytes 1363976 | tf_op jit(solution)/shard_map/ppermute | solution.py:341
  24.0 7.3 %collective-permute-start.2 = (f32[111,8,128]{2,1,0:T(8,128)S(1)}, f32[111,8,128]{2,1,0:T(8,128)S(1)}, u32[]{:S(2)}, u32[]{:S(2)}) collective-permute-start(f32[111,8,128]{2,1,0:T(8,128)S(1)} %maximum_dynamic-update-slice_fusion.own), channel_id=1, source_target_pairs={{0,8},{8,16},{16,24},{24,32},{32,40},{40,48},{48,56},{56,64},{64,7... | collective-permute-start | bytes 1363976 | tf_op jit(solution)/shard_map/ppermute | solution.py:341

commit v3 on v0

v3 whole, which is shorter than its diff:
```python
import jax
import jax.numpy as jnp
from jax import lax
from jax.experimental import pallas as pl
from jax.experimental.pallas import tpu as pltpu
from jax.sharding import Mesh, PartitionSpec as P

ITERS = 4
LAYERS = 48
ROWS = 8
LANES = 128
BASIS = ITERS + 2
DEPTH = BASIS
SPAN = ROWS + 2 * DEPTH
WIDTH = 2 * LAYERS + 8
UNITS = WIDTH // 8
SLOTS = 16
STRIDE = LAYERS + 8
FIRST = SPAN - 2
LEAD = (FIRST - ROWS) // 2

store_term = 0.1
boundary_term = 4.0
vertical_ratio = 0.3

GX = ("z", "x", "c")


def lane_index(rows):
    return lax.broadcasted_iota(jnp.int32, (rows, LANES), 1)


def padded(row):
    return 8 + row * STRIDE


def zero_padding(ref, rows):
    blank = jnp.zeros((8, LANES), jnp.float32)
    for row in range(rows + 1):
        ref[pl.ds(row * STRIDE, 8)] = blank


def rows_in_blocks(count, unroll, step):
    def block(k, _):
        stores = []
        for m in range(unroll):
            stores += step(k * unroll + m)
        for ref, where, value in stores:
            ref[where] = value
        return 0

    lax.fori_loop(0, count // unroll, block, 0)


def prepare_kernel(recharge, conduct, top_layer, fixed_head, main, part, r_buf, c_buf, t_buf, f_buf, sems):
    pairs = ((conduct, c_buf), (top_layer, t_buf), (recharge, r_buf), (fixed_head, f_buf))
    copies = [pltpu.make_async_copy(a, b, sems.at[n]) for n, (a, b) in enumerate(pairs)]
    for copy in copies:
        copy.start()
    for copy in copies:
        copy.wait()
    core = lax.axis_index("c")
    level = lax.broadcasted_iota(jnp.int32, (LAYERS, LANES), 0)
    for row in range(ROWS):
        conductivity = c_buf[pl.ds(row, LAYERS, stride=ROWS)]
        root = jnp.where(level >= t_buf[row:row + 1], jnp.sqrt(conductivity), 0.0)
        main[row, :LAYERS] = root
        main[row, LAYERS:2 * LAYERS] = root * r_buf[pl.ds(row, LAYERS, stride=ROWS)]
        main[row, 2 * LAYERS:] = jnp.broadcast_to(f_buf[row:row + 1].astype(jnp.float32), (8, LANES))
    for row in range(DEPTH):
        part[row] = main[(ROWS - DEPTH) * core + row]


def span_rows(both, far):
    core = lax.axis_index("c")
    near = [(both, (ROWS - DEPTH) * core + n, DEPTH * (1 - core) + n) for n in range(ROWS + DEPTH)]
    return near + [(far, n, (ROWS + DEPTH) * core + n) for n in range(DEPTH)]


def edges_kernel(both, far, low_edge, high_edge):
    slot = lane_index(ROWS) // 8
    for ref, source, row in span_rows(both, far):
        low = jnp.zeros((8, LANES), jnp.float32)
        high = jnp.zeros((8, LANES), jnp.float32)
        for u in range(UNITS):
            turned = ref[source, 8 * u:8 * u + 8]
            if u:
                turned = pltpu.roll(turned, 8 * u, 1)
            low = jnp.where(slot == u, turned, low)
            high = jnp.where(slot == (u - 1) % SLOTS, turned, high)
        low_edge[row] = low
        high_edge[row] = high


def assemble_kernel(both, far, root, source, fixed, near, across):
    zero_padding(root, SPAN)
    for ref, at, row in span_rows(both, far):
        root[pl.ds(pl.multiple_of(padded(row), 8), LAYERS)] = ref[at, :LAYERS]
        source[row] = ref[at, LAYERS:2 * LAYERS]
        fixed[row] = boundary_term * ref[at, 2 * LAYERS:]
    lane = lane_index(LAYERS)
    last, first = lane == LANES - 1, lane == 0

    def sums(i):
        base = pl.multiple_of(padded(i + 1), 8)
        center = root[pl.ds(base, LAYERS)]
        up, down = pltpu.roll(center, LANES - 1, 1), pltpu.roll(center, 1, 1)
        total = jnp.where(last, 0.0, up) + jnp.where(first, 0.0, down) + straight(root, base)
        return [(near, i, total), (across, i, jnp.where(last, up, jnp.where(first, down, 0.0)))]

    rows_in_blocks(FIRST, 3, sums)


def straight(ref, base):
    rows = ref[pl.ds(base - STRIDE, LAYERS)] + ref[pl.ds(base + STRIDE, LAYERS)]
    return rows + vertical_ratio * (ref[pl.ds(base - 1, LAYERS)] + ref[pl.ds(base + 1, LAYERS)])


def basis_kernel(root_c, source_c, fixed_c, near, across, from_low, from_high, basis, inv_root, scale, moments,
                 root_h, source_h, fixed_h, g_c, g_h, diag, *fields):
    t_c, t_h = fields[:ITERS + 1], fields[ITERS + 1:]
    lane = lane_index(8)
    rim = (lane < 8) | (lane >= LANES - 8)
    zero_padding(root_h, SPAN)
    for j in range(ITERS + 1):
        zero_padding(t_c[j], FIRST - 2 * j)
        zero_padding(t_h[j], FIRST - 2 * j)

    def unpack(row):
        high, low = from_high[row], from_low[row]
        start = pl.multiple_of(padded(row), 8)
        stores = []
        for u in range(UNITS):
            tile = jnp.where(lane // 8 == u, high, low)
            if u:
                tile = pltpu.roll(tile, LANES - 8 * u, 1)
            tile = jnp.where(rim, tile, 0.0)
            if u < LAYERS // 8:
                stores.append((root_h, pl.ds(start + 8 * u, 8), tile))
            elif u < 2 * LAYERS // 8:
                stores.append((source_h, (row, pl.ds(8 * u - LAYERS, 8)), tile))
            else:
                stores.append((fixed_h, row, boundary_term * tile))
        return stores

    rows_in_blocks(SPAN, 5, unpack)

    wide = lane_index(LAYERS)
    last, first = wide == LANES - 1, wide == 0

    def start(i):
        base = pl.multiple_of(padded(i + 1), 8)
        to = pl.ds(pl.multiple_of(padded(i), 8), LAYERS)
        halo = root_h[pl.ds(base, LAYERS)]
        up, down = pltpu.roll(halo, LANES - 1, 1), pltpu.roll(halo, 1, 1)
        c_sum = near[i] + jnp.where(last, up, jnp.where(first, down, 0.0))
        h_sum = jnp.where(last, 0.0, up) + jnp.where(first, 0.0, down) + across[i] + straight(root_h, base)
        stores = []
        parts = (
            (root_c, c_sum, source_c, fixed_c, g_c, t_c[0], diag),
            (root_h, h_sum, source_h, fixed_h, g_h, t_h[0], None),
        )
        for roots, total, source, fixed, g, t, keep in parts:
            root = roots[pl.ds(base, LAYERS)]
            above = roots[pl.ds(base - 1, LAYERS)]
            head = jnp.where(above > 0.0, 0.0, fixed[i + 1, :1])
            d = jnp.where(root > 0.0, root * total + (store_term + head), 1.0)
            inverse = 1.0 / d
            stores.append((g, i, root * root * inverse))
            stores.append((t, to, source[i + 1] * inverse))
            if keep is not None:
                stores.append((keep, i, d))
        return stores

    rows_in_blocks(FIRST, 3, start)

    def sums(c_ref, h_ref, base):
        center, halo = c_ref[pl.ds(base, LAYERS)], h_ref[pl.ds(base, LAYERS)]
        c_up, h_up = pltpu.roll(center, LANES - 1, 1), pltpu.roll(halo, LANES - 1, 1)
        c_down, h_down = pltpu.roll(center, 1, 1), pltpu.roll(halo, 1, 1)
        c_sum = jnp.where(last, h_up, c_up) + jnp.where(first, h_down, c_down) + straight(c_ref, base)

        def halo_sum():
            return jnp.where(last, c_up, h_up) + jnp.where(first, c_down, h_down) + straight(h_ref, base)

        return c_sum, halo_sum

    def field(ref, row):
        return ref[pl.ds(pl.multiple_of(padded(row), 8), LAYERS)]

    for j, unroll in zip(range(1, ITERS + 1), (4, 7, 6, 5)):
        def step(i, j=j):
            c_sum, halo_sum = sums(t_c[j - 1], t_h[j - 1], pl.multiple_of(padded(i + 1), 8))
            out = [g_c[i + j] * c_sum, g_h[i + j] * halo_sum()]
            if j > 1:
                out = [2.0 * a - field(t[j - 2], i + 2) for a, t in zip(out, (t_c, t_h))]
            to = pl.ds(pl.multiple_of(padded(i), 8), LAYERS)
            return [(t_c[j], to, out[0]), (t_h[j], to, out[1])]

        rows_in_blocks(FIRST - 2 * j, unroll, step)

    unroll = 2

    def finish(k, totals):
        stores = []
        for m in range(unroll):
            i = k * unroll + m
            c_sum, _ = sums(t_c[ITERS], t_h[ITERS], pl.multiple_of(padded(i + 1), 8))
            t = [field(t_c[j], i + LEAD - j) for j in range(ITERS + 1)]
            t.append(2.0 * g_c[i + LEAD] * c_sum - t[ITERS - 1])
            stores += [(basis, (j, i), t[j]) for j in range(BASIS)]
            root = field(root_c, i + DEPTH)
            inv = jnp.where(root > 0.0, 1.0 / root, 0.0)
            ratio = diag[i + LEAD] * inv
            stores += [(inv_root, i, inv), (scale, i, ratio)]
            weight = ratio * inv
            new = []
            for j in range(ITERS):
                weighted = weight * t[j]
                new += [weighted * t[j], weighted * t[j + 1]]
            totals = tuple(a + b for a, b in zip(totals, new))
        for ref, where, value in stores:
            ref[where] = value
        return totals

    zero = jnp.zeros((LAYERS, LANES), jnp.float32)
    totals = lax.fori_loop(0, ROWS // unroll, finish, (zero,) * (2 * ITERS))
    column = lane_index(1)
    row = jnp.zeros((1, LANES), jnp.float32)
    for n, total in enumerate(totals):
        row = jnp.where(column == n, jnp.sum(jnp.sum(total, axis=0, keepdims=True), axis=1, keepdims=True), row)
    moments[...] = row


def added(a, b, factor):
    out = []
    for i in range(max(len(a), len(b))):
        left = a[i] if i < len(a) else None
        right = b[i] if i < len(b) else None
        if right is not None:
            right = factor * right
        out.append(right if left is None else left if right is None else left + right)
    return out


def shifted(a):
    out = [None] * (len(a) + 1)

    def put(i, value):
        out[i] = value if out[i] is None else out[i] + value

    for i, value in enumerate(a):
        if i == 0:
            put(1, value)
        else:
            put(i + 1, 0.5 * value)
            put(i - 1, 0.5 * value)
    return out


def form(a, b, gram):
    total = None
    for i, left in enumerate(a):
        inner = None
        for j, right in enumerate(b):
            if right is None:
                continue
            term = right * gram(i, j)
            inner = term if inner is None else inner + term
        inner = left * inner
        total = inner if total is None else total + inner
    return total


def recursion(moments):
    half = [0.5 * m for m in moments]

    def gram(i, j):
        return moments[i] if j == 0 else moments[j] if i == 0 else half[i + j] + half[abs(i - j)]

    one = jnp.ones_like(moments[0])
    precond, direction, head = [one], [], []
    gamma_old = alpha_old = None
    for step in range(ITERS):
        gamma = form(precond, precond, gram)
        delta = gamma - form(precond, shifted(precond), gram)
        if step == 0:
            direction = precond
            alpha = gamma / delta
        else:
            beta = gamma / gamma_old
            alpha = gamma / (delta - beta * gamma / alpha_old)
            direction = added(precond, direction, beta)
        head = added(head, direction, alpha)
        moved = added(direction, shifted(direction), -1.0)
        precond = added(precond, moved, -alpha)
        gamma_old, alpha_old = gamma, alpha
    return head, precond, added(precond, shifted(precond), -1.0)


def combine_kernel(moments, basis, inv_root, scale, head_field, residual, applied, h_buf, r_buf, a_buf, sems):
    row = jnp.sum(moments[...], axis=0)
    column = lane_index(1)
    raw = []
    for n in range(2 * ITERS):
        value = jnp.sum(jnp.where(column == n, row, 0.0), axis=1, keepdims=True)
        raw.append(jnp.broadcast_to(value, (8, LANES)))
    full = raw[:2]
    for n in range(2, 2 * ITERS):
        full.append(2.0 * raw[n] - raw[n % 2])
    targets = ((h_buf, head_field, inv_root), (r_buf, residual, scale), (a_buf, applied, scale))
    copies = []
    for n, (weights, (buf, out, factor)) in enumerate(zip(recursion(full), targets)):
        weights = [jnp.concatenate([w] * (LAYERS // 8), axis=0) for w in weights]
        for row in range(ROWS):
            total = weights[0] * basis[0, row]
            for j in range(1, len(weights)):
                total = total + weights[j] * basis[j, row]
            buf[pl.ds(row, LAYERS, stride=ROWS)] = factor[row] * total
        copies.append(pltpu.make_async_copy(buf, out, sems.at[n]))
        copies[-1].start()
    for copy in copies:
        copy.wait()


def f32(*shape):
    return jax.ShapeDtypeStruct(shape, jnp.float32)


def scratch(*shape):
    return pltpu.VMEM(shape, jnp.float32)


VMEM = pl.BlockSpec(memory_space=pltpu.VMEM)
HBM = pl.BlockSpec(memory_space=pltpu.HBM)


def call(kernel, outs, scratches=(), ins=VMEM, out=VMEM):
    def run(*args):
        return pl.pallas_call(
            kernel,
            out_shape=outs,
            in_specs=[ins] * len(args),
            out_specs=[out] * len(outs),
            scratch_shapes=list(scratches),
            compiler_params=pltpu.CompilerParams(vmem_limit_bytes=32 * 1024 * 1024),
        )(*args)

    return run


def prepare(recharge, conduct, top_layer, fixed_head):
    flat = (LAYERS * ROWS, LANES)
    plane = pltpu.VMEM((ROWS, LANES), jnp.int32)
    args = (recharge.reshape(flat), conduct.reshape(flat), top_layer, fixed_head)
    return call(
        prepare_kernel,
        (f32(ROWS, WIDTH, LANES), f32(DEPTH, WIDTH, LANES)),
        [scratch(*flat), scratch(*flat), plane, plane, pltpu.SemaphoreType.DMA((4,))],
        ins=HBM,
    )(*[pltpu.with_memory_space_constraint(a, pltpu.HBM) for a in args])


def edges(both, far):
    return call(edges_kernel, (f32(SPAN, 8, LANES),) * 2)(both, far)


def assemble(both, far):
    field = f32(FIRST, LAYERS, LANES)
    outs = (f32(padded(SPAN), LANES), f32(SPAN, LAYERS, LANES), f32(SPAN, 8, LANES), field, field)
    return call(assemble_kernel, outs)(both, far)


def make_basis(parts, from_low, from_high):
    field = f32(ROWS, LAYERS, LANES)
    layers = scratch(FIRST, LAYERS, LANES)
    scratches = [scratch(padded(SPAN), LANES), scratch(SPAN, LAYERS, LANES), scratch(SPAN, 8, LANES)]
    scratches += [layers] * 3 + [scratch(padded(FIRST - 2 * j), LANES) for j in range(ITERS + 1)] * 2
    outs = (f32(BASIS, ROWS, LAYERS, LANES), field, field, f32(1, LANES))
    return call(basis_kernel, outs, scratches)(*parts, from_low, from_high)


def combine(moments, basis, inv_root, scale):
    flat = (LAYERS * ROWS, LANES)
    outs = call(
        combine_kernel,
        (f32(*flat),) * 3,
        [scratch(*flat)] * 3 + [pltpu.SemaphoreType.DMA((3,))],
        out=HBM,
    )(moments, basis, inv_root, scale)
    return tuple(out.reshape(LAYERS, ROWS, LANES) for out in outs)


def shift_both(low_going, high_going, axis):
    count = lax.axis_size(axis)
    up = [(i, i + 1) for i in range(count - 1)]
    down = [(target, source) for source, target in up]
    return lax.ppermute(high_going, axis, up), lax.ppermute(low_going, axis, down)


def between_chips(array):
    count = lax.axis_size(GX)
    pairs = []
    for i in range(1, count - 1, 2):
        pairs += [(i, i + 1), (i + 1, i)]
    return lax.ppermute(array, GX, pairs)


def spread_sum(row, axes):
    count = lax.axis_size(axes)
    return lax.all_to_all(jnp.broadcast_to(row[None], (count,) + row.shape), axes, 0, 0, tiled=True)


def local(recharge, conduct, top_layer, fixed_head):
    main, part = prepare(recharge, conduct, top_layer, fixed_head)
    far = between_chips(part)
    both = lax.all_gather(main, "c", axis=0, tiled=True)
    low_edge, high_edge = edges(both, far)
    from_low, from_high = shift_both(low_edge, high_edge, "y")
    parts = assemble(both, far)
    basis, inv_root, scale, moments = make_basis(parts, from_low, from_high)
    moments = jnp.sum(spread_sum(moments, ("z", "c")), axis=0)
    moments = spread_sum(moments, ("x", "y"))
    return combine(moments, basis, inv_root, scale)


def solution(mesh):
    grid = Mesh(mesh.devices.reshape(12, 4, 2, 8), ("z", "x", "c", "y"))
    field, plane = P(None, GX, "y"), P(GX, "y")
    return jax.shard_map(
        local, mesh=grid, in_specs=(field, field, plane, plane), out_specs=(field, field, field), check_vma=False
    )
```

time: 611 us -> 71.7 us (0.12); the launches traced: 604 us -> 71.5 us
  blocking collectives: 456 us -> 52 us
  starting transfers between devices: 57.7 us -> 7.09 us
  waiting for transfers between devices: 47 us -> 3.48 us
  other arithmetic: 24.3 us -> 0.02 us
  between operations: 14.7 us -> 0.7 us
  Pallas kernels: 0 us -> 8.11 us
    psum x4 -> x0, blocking collectives: 456 us -> none  [global_sums(): return lax.psum((first_sum, second_sum), ('gx', 'gy'))]
    ppermute x24 -> x3, starting transfers between devices: 57.7 us -> 7.09 us  [the longest x1 4.51 us: between_chips(): return lax.ppermute(array, GX, pairs)]
    ppermute x24 -> x3, waiting for transfers between devices: 47 us -> 3.48 us  [the longest x1 3.48 us: shift_both(): lax.ppermute(low_going, axis, down)]
    all_to_all x0 -> x2, blocking collectives: none -> 43.3 us  [spread_sum(): lax.all_to_all(jnp.broadcast_to(row[None], (count,) + row.shape), axes, 0...]
    all_gather x0 -> x1, blocking collectives: none -> 8.73 us  [local(): both = lax.all_gather(main, 'c', axis=0, tiled=True)]
    concatenate x12 -> x0, other arithmetic: 8.73 us -> none  [with_halo(): block = jnp.concatenate([low, block, high], axis=dim)]
    pallas_call x0 -> x5, Pallas kernels: none -> 8.11 us  [run(): pl.pallas_call(kernel, out_shape=outs, in_specs=[ins] * len(args), out_sp...]
    reduce_sum x4 -> x1, other arithmetic: 6.59 us -> 0.02 us  [local(): moments = jnp.sum(spread_sum(moments, ('z', 'c')), axis=0)]
  transfers between devices with their start and end apart: 24 -> 3, of which waited for: 11 -> 1; matrix products, arithmetic and copies ran while one was open for 0% -> 0% of each run, Pallas kernels for 0% -> 1%
where the time goes in v3:
time: 71.7 us; the launch traced here: 71.5 us
  blocking collectives  52 us (73%)
  Pallas kernels  8.11 us (11%)
  starting transfers between devices  7.09 us (10%)
  waiting for transfers between devices  3.48 us (5%)
    all_to_all x2, blocking collectives, spread_sum(): lax.all_to_all(jnp.broadcast_to(row[None], (count,) + row.shape), axes, 0...  43.3 us
    all_gather x1, blocking collectives, local(): both = lax.all_gather(main, 'c', axis=0, tiled=True)  8.73 us
    pallas_call x5, Pallas kernels, run(): pl.pallas_call(kernel, out_shape=outs, in_specs=[ins] * len(args), out_sp...  8.11 us
    ppermute x1, starting transfers between devices, between_chips(): return lax.ppermute(array, GX, pairs)  4.51 us
    ppermute x1, waiting for transfers between devices, shift_both(): lax.ppermute(low_going, axis, down)  3.48 us
  transfers between devices with their start and end apart: 3, of which 1 were waited for; matrix products, arithmetic and copies ran while one was open for 0% of the time, Pallas kernels for 1%

profile of v3, /device:TPU:1, one launch (start us, length us, event | category | flops | bytes accessed | tf_op | source)
XLA Modules:
  0.0 71.5 jit_solution(17421947219382418490)
XLA Ops:
  0.6 1.2 %shard_map.67 = (f32[8,104,128]{2,1,0:T(8,128)S(1)}, f32[6,104,128]{2,1,0:T(8,128)S(1)}) custom-call(f32[384,128]{1,0:T(8,128)} %bitcast.8, f32[384,128]{1,0:T(8,128)} %bitcast.9, s32[8,128]{1,0:T(8,128)} %top_layer.1, s32[8,128]{1,0:T(8,128)} %fixed_head.1), custom_call_target="tpu_custom_call" | custom-call | tf_op jit(solution)/shard_map/pallas_call | solution.py:340
  1.9 4.5 %collective-permute-start = (f32[6,104,128]{2,1,0:T(8,128)S(1)}, f32[6,104,128]{2,1,0:T(8,128)S(1)}, u32[]{:S(2)}, u32[]{:S(2)}) collective-permute-start(f32[6,104,128]{2,1,0:T(8,128)S(1)} %get-tuple-element.20), channel_id=1, source_target_pairs={{8,16},{16,8},{24,32},{32,24},{40,48},{48,40},{56,64},{64,56},{72,... | collective-permute-start | bytes 958472 | tf_op jit(solution)/shard_map/ppermute | solution.py:406
  6.4 8.7 %all_gather.3.both = f32[16,104,128]{2,1,0:T(8,128)S(1)} all-gather(f32[8,104,128]{2,1,0:T(8,128)S(1)} %get-tuple-element.19), channel_id=1, replica_groups=mesh['z'=12,'x'=4,'c'=2,'y'=8] {'c'}, dimensions={0}, use_global_device_ids=true | all-gather | bytes 1277952 | tf_op jit(solution)/shard_map/all_gather | solution.py:417
  15.1 0.0 collective-permute-done.far
  15.1 0.3 shard_map.69
  15.4 1.3 %collective-permute-start.1 = (f32[20,8,128]{2,1,0:T(8,128)S(1)}, f32[20,8,128]{2,1,0:T(8,128)S(1)}, u32[]{:S(2)}, u32[]{:S(2)}) collective-permute-start(f32[20,8,128]{2,1,0:T(8,128)S(1)} %get-tuple-element.26), channel_id=1, source_target_pairs={{0,1},{1,2},{2,3},{3,4},{4,5},{5,6},{6,7},{8,9},{9,10},{10,11},{11... | collective-permute-start | bytes 245768 | tf_op jit(solution)/shard_map/ppermute | solution.py:398
  16.7 1.3 %collective-permute-start.2 = (f32[20,8,128]{2,1,0:T(8,128)S(1)}, f32[20,8,128]{2,1,0:T(8,128)S(1)}, u32[]{:S(2)}, u32[]{:S(2)}) collective-permute-start(f32[20,8,128]{2,1,0:T(8,128)S(1)} %get-tuple-element.27), channel_id=1, source_target_pairs={{1,0},{2,1},{3,2},{4,3},{5,4},{6,5},{7,6},{9,8},{10,9},{11,10},{12... | collective-permute-start | bytes 245768 | tf_op jit(solution)/shard_map/ppermute | solution.py:398
  18.0 0.8 %shard_map.68 = (f32[1128,128]{1,0:T(8,128)S(1)}, f32[20,48,128]{2,1,0:T(8,128)S(1)}, f32[20,8,128]{2,1,0:T(8,128)S(1)}, f32[18,48,128]{2,1,0:T(8,128)S(1)}, f32[18,48,128]{2,1,0:T(8,128)S(1)}) custom-call(f32[16,104,128]{2,1,0:T(8,128)S(1)} %all_gather.3.both, f32[6,104,128]{2,1,0:T(8,128)S(1)} %collective-permute-done.far), custom_call_target="tpu_custom_call" | custom-call | tf_op jit(solution)/shard_map/pallas_call | solution.py:340
  18.8 0.0 collective-permute-done.1.from_low
  18.8 3.5 %collective-permute-done.2.from_high = f32[20,8,128]{2,1,0:T(8,128)S(1)} collective-permute-done((f32[20,8,128]{2,1,0:T(8,128)S(1)}, f32[20,8,128]{2,1,0:T(8,128)S(1)}, u32[]{:S(2)}, u32[]{:S(2)}) %collective-permute-start.2) | collective-permute-done | bytes 81952 | tf_op jit(solution)/shard_map/ppermute | solution.py:398
  22.3 4.7 %shard_map.70 = (f32[6,8,48,128]{3,2,1,0:T(8,128)S(1)}, f32[8,48,128]{2,1,0:T(8,128)S(1)}, f32[8,48,128]{2,1,0:T(8,128)S(1)}, f32[1,128]{1,0:T(1,128)S(1)}) custom-call(f32[1128,128]{1,0:T(8,128)S(1)} %get-tuple-element.21.root_c, f32[20,48,128]{2,1,0:T(8,128)S(1)} %get-tuple-element.22.source_c, f32[20,8,128]{2,1,0:T(8,128)S(1)} %get-tuple-element.23.fixed_c, ...), custom_call_target="tpu_custom_call" | custom-call | tf_op jit(solution)/shard_map/pallas_call | solution.py:340
  27.0 26.1 %all_to_all.10 = f32[24,1,128]{2,1,0:T(1,128)S(1)} all-to-all(f32[24,1,128]{2,1,0:T(1,128)S(1)} %broadcast_in_dim.7), channel_id=1, replica_groups=mesh['z'=12,'x'=4,'c'=2,'y'=8] {'z','c'}, dimensions={0} | all-to-all | bytes 24576 | tf_op jit(solution)/shard_map/all_to_all | solution.py:411
  53.1 17.3 %all_to_all.11.moments = f32[32,1,128]{2,1,0:T(1,128)S(1)} all-to-all(f32[32,1,128]{2,1,0:T(1,128)S(1)} %broadcast_in_dim.16), channel_id=1, replica_groups=mesh['z'=12,'x'=4,'c'=2,'y'=8] {'x','y'}, dimensions={0} | all-to-all | bytes 32768 | tf_op jit(solution)/shard_map/all_to_all | solution.py:411
  70.3 1.1 %shard_map.71 = (f32[384,128]{1,0:T(8,128)}, f32[384,128]{1,0:T(8,128)}, f32[384,128]{1,0:T(8,128)}) custom-call(f32[32,1,128]{2,1,0:T(1,128)S(1)} %all_to_all.11.moments, f32[6,8,48,128]{3,2,1,0:T(8,128)S(1)} %get-tuple-element.29.basis, f32[8,48,128]{2,1,0:T(8,128)S(1)} %get-tuple-element.30.inv_root, f32[8,48,128]{2,1,0:T(8,128)S(1)} %get-tuple-element.31.scale), custom_call_target="tpu_custom_call" | custom-call | tf_op jit(solution)/shard_map/pallas_call | solution.py:340
  (3 shorter events, 0.0 us)
Async XLA Ops:
  1.9 13.2 %collective-permute-start = (f32[6,104,128]{2,1,0:T(8,128)S(1)}, f32[6,104,128]{2,1,0:T(8,128)S(1)}, u32[]{:S(2)}, u32[]{:S(2)}) collective-permute-start(f32[6,104,128]{2,1,0:T(8,128)S(1)} %get-tuple-element.20), channel_id=1, source_target_pairs={{8,16},{16,8},{24,32},{32,24},{40,48},{48,40},{56,64},{64,56},{72,... | collective-permute-start | bytes 958472 | tf_op jit(solution)/shard_map/ppermute | solution.py:406
  15.4 3.4 %collective-permute-start.1 = (f32[20,8,128]{2,1,0:T(8,128)S(1)}, f32[20,8,128]{2,1,0:T(8,128)S(1)}, u32[]{:S(2)}, u32[]{:S(2)}) collective-permute-start(f32[20,8,128]{2,1,0:T(8,128)S(1)} %get-tuple-element.26), channel_id=1, source_target_pairs={{0,1},{1,2},{2,3},{3,4},{4,5},{5,6},{6,7},{8,9},{9,10},{10,11},{11... | collective-permute-start | bytes 245768 | tf_op jit(solution)/shard_map/ppermute | solution.py:398
  16.7 5.6 %collective-permute-start.2 = (f32[20,8,128]{2,1,0:T(8,128)S(1)}, f32[20,8,128]{2,1,0:T(8,128)S(1)}, u32[]{:S(2)}, u32[]{:S(2)}) collective-permute-start(f32[20,8,128]{2,1,0:T(8,128)S(1)} %get-tuple-element.27), channel_id=1, source_target_pairs={{1,0},{2,1},{3,2},{4,3},{5,4},{6,5},{7,6},{9,8},{10,9},{11,10},{12... | collective-permute-start | bytes 245768 | tf_op jit(solution)/shard_map/ppermute | solution.py:398

commit v4 on v3

v4 whole, which is shorter than its diff:
```python
import jax
import jax.numpy as jnp
from jax import lax
from jax.experimental import pallas as pl
from jax.experimental.pallas import tpu as pltpu
from jax.sharding import Mesh, PartitionSpec as P

ITERS = 4
LAYERS = 48
ROWS = 8
LANES = 128
BASIS = ITERS + 2
DEPTH = BASIS
SPAN = ROWS + 2 * DEPTH
WIDTH = 2 * LAYERS + 8
TILES = LAYERS // 8
FIRST = SPAN - 2
LEAD = (FIRST - ROWS) // 2

EDGE = 7
SIDE = 3 * EDGE
PAIR = 2 * SIDE
FOLD = 3
STRIPS = 7
DENSE = 3 * STRIPS
MERGE = 8

store_term = 0.1
boundary_term = 4.0
vertical_ratio = 0.3

GX = ("z", "x", "c")


def lane_index(rows):
    return lax.broadcasted_iota(jnp.int32, (rows, LANES), 1)


def turn(tile, lanes):
    lanes %= LANES
    return pltpu.roll(tile, lanes, 1) if lanes else tile


def between(lane, low, high):
    return (lane >= low) & (lane < high)


def layer_above(row):
    sublane = lax.broadcasted_iota(jnp.int32, (8, LANES), 0)
    edge = jnp.where(sublane == 0, 0.0, pltpu.roll(row[LAYERS - 8:], 1, 0))
    return jnp.concatenate([edge, row[:LAYERS - 8]], axis=0)


def layer_below(row):
    sublane = lax.broadcasted_iota(jnp.int32, (8, LANES), 0)
    edge = jnp.where(sublane == 7, 0.0, pltpu.roll(row[:8], 7, 0))
    return jnp.concatenate([row[8:], edge], axis=0)


def neighbours(row, before, after):
    sides = turn(row, 1) + turn(row, -1) + before + after
    return sides + vertical_ratio * (layer_above(row) + layer_below(row))


def start_fields(root, source, fixed, total):
    head = jnp.where(layer_above(root) > 0.0, 0.0, boundary_term * fixed)
    diagonal = jnp.where(root > 0.0, root * total + (store_term + head), 1.0)
    inverse = 1.0 / diagonal
    return diagonal, root * root * inverse, source * inverse


def outer_factors(root, diagonal):
    inv = jnp.where(root > 0.0, 1.0 / root, 0.0)
    return inv, diagonal * inv


def products(weight, fields):
    out = []
    for j in range(ITERS):
        weighted = weight * fields[j]
        out += [weighted * fields[j], weighted * fields[j + 1]]
    return out


def as_row(totals):
    column = lane_index(1)
    row = jnp.zeros((1, LANES), jnp.float32)
    for n, total in enumerate(totals):
        row = jnp.where(column == n, jnp.sum(jnp.sum(total, axis=0, keepdims=True), axis=1, keepdims=True), row)
    return row


def rows_in_blocks(count, unroll, step):
    def block(k, _):
        stores = []
        for m in range(unroll):
            stores += step(k * unroll + m)
        for ref, where, value in stores:
            ref[where] = value
        return 0

    lax.fori_loop(0, count // unroll, block, 0)


def prepare_kernel(recharge, conduct, top_layer, fixed_head, main, part, r_buf, c_buf, t_buf, f_buf, sems):
    pairs = ((conduct, c_buf), (top_layer, t_buf), (recharge, r_buf), (fixed_head, f_buf))
    copies = [pltpu.make_async_copy(a, b, sems.at[n]) for n, (a, b) in enumerate(pairs)]
    for copy in copies:
        copy.start()
    for copy in copies:
        copy.wait()
    core = lax.axis_index("c")
    level = TILES * lax.broadcasted_iota(jnp.int32, (8, LANES), 0)
    for row in range(ROWS):
        top = t_buf[row:row + 1]
        for k in range(TILES):
            layers = pl.ds(k * ROWS + row, 8, stride=TILES * ROWS)
            root = jnp.where(level + k >= top, jnp.sqrt(c_buf[layers]), 0.0)
            main[row, 8 * k:8 * k + 8] = root
            main[row, LAYERS + 8 * k:LAYERS + 8 * k + 8] = root * r_buf[layers]
        main[row, 2 * LAYERS:] = jnp.broadcast_to(f_buf[row:row + 1].astype(jnp.float32), (8, LANES))
    for row in range(DEPTH):
        part[row] = main[(ROWS - DEPTH) * core + row]


def units(strip):
    for slot in range(FOLD):
        row = slot * STRIPS + strip
        if row < SPAN:
            for unit in range(2 * TILES + 1):
                group, place = divmod(unit, TILES)
                yield 3 * strip + group, place, slot, row, 8 * unit


def edges_kernel(both, far, span, low_edge, high_edge):
    core = lax.axis_index("c")
    for n in range(ROWS + DEPTH):
        span[DEPTH * (1 - core) + n] = both[(ROWS - DEPTH) * core + n]
    for n in range(DEPTH):
        span[(ROWS + DEPTH) * core + n] = far[n]
    lane = lane_index(8)
    for strip in range(STRIPS):
        low = {3 * strip + g: jnp.zeros((8, LANES), jnp.float32) for g in range(3)}
        high = dict(low)
        for dense, place, slot, row, at in units(strip):
            to = PAIR * slot + EDGE * place
            turned = turn(span[row, at:at + 8], to)
            low[dense] = jnp.where(between(lane, to, to + EDGE), turned, low[dense])
            to = (to - EDGE) % LANES
            high[dense] = jnp.where(between(lane, to, to + EDGE), turned, high[dense])
        for dense in low:
            low_edge[dense] = low[dense]
            high_edge[dense] = high[dense]


def own_kernel(span, basis, inv_root, scale, moments, strip_root, strip_source, strip_fixed, g, diag, *t):
    def start(i):
        row = i + 1
        root = span[row, :LAYERS]
        total = neighbours(root, span[row - 1, :LAYERS], span[row + 1, :LAYERS])
        fixed = span[row, 2 * LAYERS:2 * LAYERS + 1]
        d, g_row, t_row = start_fields(root, span[row, LAYERS:2 * LAYERS], fixed, total)
        return [(diag, i, d), (g, i, g_row), (t[0], i, t_row)]

    rows_in_blocks(FIRST, 3, start)

    for j, unroll in zip(range(1, ITERS + 1), (4, 7, 6, 5)):
        def step(i, j=j):
            new = g[i + j] * neighbours(t[j - 1][i + 1], t[j - 1][i], t[j - 1][i + 2])
            return [(t[j], i, new if j == 1 else 2.0 * new - t[j - 2][i + 2])]

        rows_in_blocks(FIRST - 2 * j, unroll, step)

    wide = lane_index(LAYERS)
    inner = between(wide, MERGE, LANES - MERGE)
    unroll = 2

    def finish(k, totals):
        stores = []
        for m in range(unroll):
            i = k * unroll + m
            fields = [t[j][i + LEAD - j] for j in range(ITERS + 1)]
            sums = neighbours(t[ITERS][i + 1], t[ITERS][i], t[ITERS][i + 2])
            fields.append(2.0 * g[i + LEAD] * sums - fields[ITERS - 1])
            inv, ratio = outer_factors(span[i + DEPTH, :LAYERS], diag[i + LEAD])
            stores += [(basis, (j, i), fields[j]) for j in range(BASIS)]
            stores += [(inv_root, i, inv), (scale, i, ratio)]
            new = products(jnp.where(inner, ratio * inv, 0.0), fields)
            totals = tuple(a + b for a, b in zip(totals, new))
        for ref, where, value in stores:
            ref[where] = value
        return totals

    zero = jnp.zeros((LAYERS, LANES), jnp.float32)
    moments[...] = as_row(lax.fori_loop(0, ROWS // unroll, finish, (zero,) * (2 * ITERS)))

    lane = lane_index(8)
    for strip in range(STRIPS):
        for unit in range(2 * TILES + 1):
            tile = jnp.zeros((8, LANES), jnp.float32)
            for slot in range(FOLD):
                row = slot * STRIPS + strip
                if row < SPAN:
                    source, base = span[row, 8 * unit:8 * unit + 8], PAIR * slot
                    low, high = turn(source, base + EDGE), turn(source, base + PAIR - EDGE)
                    tile = jnp.where(between(lane, base + EDGE, base + SIDE), low, tile)
                    tile = jnp.where(between(lane, base + SIDE, base + PAIR - EDGE), high, tile)
            if unit < TILES:
                strip_root[strip, 8 * unit:8 * unit + 8] = tile
            elif unit < 2 * TILES:
                strip_source[strip, 8 * unit - LAYERS:8 * unit - LAYERS + 8] = tile
            else:
                strip_fixed[strip] = tile


def strips_kernel(own_moments, own_root, own_source, own_fixed, from_low, from_high,
                  basis, inv_root, scale, moments, root, source, g):
    lane = lane_index(8)
    low_lanes = high_lanes = lane < 0
    for slot in range(FOLD):
        base = PAIR * slot
        low_lanes = low_lanes | between(lane, base, base + EDGE)
        high_lanes = high_lanes | between(lane, base + PAIR - EDGE, base + PAIR)

    def with_halo(own, dense, place):
        low = turn(from_low[dense], EDGE - EDGE * place)
        high = turn(from_high[dense], PAIR - EDGE - EDGE * place)
        return jnp.where(low_lanes, low, jnp.where(high_lanes, high, own))

    fixed = []
    for q in range(STRIPS):
        for k in range(TILES):
            tile = pl.ds(8 * k, 8)
            root[q, tile] = with_halo(own_root[q, tile], 3 * q, k)
            source[q, tile] = with_halo(own_source[q, tile], 3 * q + 1, k)
        fixed.append(with_halo(own_fixed[q], 3 * q + 2, 0)[:1])

    def sums(ref, at):
        rows = [ref[(*at, q)] for q in range(STRIPS)]
        before = [turn(rows[-1], PAIR)] + rows[:-1]
        after = rows[1:] + [turn(rows[0], -PAIR)]
        return [neighbours(*three) for three in zip(rows, before, after)]

    wide = lane_index(LAYERS)
    own_lanes = []
    for slot in range(2):
        base = PAIR * slot
        low = between(wide, base + EDGE, base + EDGE + MERGE)
        own_lanes.append(low | between(wide, base + PAIR - EDGE - MERGE, base + PAIR - EDGE))

    weights = []
    for q, total in enumerate(sums(root, ())):
        d, g[q], basis[0, q] = start_fields(root[q], source[q], fixed[q], total)
        inv, ratio = outer_factors(root[q], d)
        inv_root[q] = inv
        scale[q] = ratio
    for j in range(1, BASIS):
        for q, total in enumerate(sums(basis, (j - 1,))):
            new = g[q] * total
            basis[j, q] = new if j == 1 else 2.0 * new - basis[j - 2, q]

    totals = None
    for q in range(STRIPS):
        mine = own_lanes[1] | own_lanes[0] if q == DEPTH else own_lanes[1]
        new = products(jnp.where(mine, scale[q] * inv_root[q], 0.0), [basis[j, q] for j in range(ITERS + 1)])
        totals = new if totals is None else [a + b for a, b in zip(totals, new)]
    moments[...] = own_moments[...] + as_row(totals)


def added(a, b, factor):
    out = []
    for i in range(max(len(a), len(b))):
        left = a[i] if i < len(a) else None
        right = b[i] if i < len(b) else None
        if right is not None:
            right = factor * right
        out.append(right if left is None else left if right is None else left + right)
    return out


def shifted(a):
    out = [None] * (len(a) + 1)

    def put(i, value):
        out[i] = value if out[i] is None else out[i] + value

    for i, value in enumerate(a):
        if i == 0:
            put(1, value)
        else:
            put(i + 1, 0.5 * value)
            put(i - 1, 0.5 * value)
    return out


def form(a, b, gram):
    total = None
    for i, left in enumerate(a):
        inner = None
        for j, right in enumerate(b):
            if right is None:
                continue
            term = right * gram(i, j)
            inner = term if inner is None else inner + term
        inner = left * inner
        total = inner if total is None else total + inner
    return total


def recursion(moments):
    half = [0.5 * m for m in moments]

    def gram(i, j):
        return moments[i] if j == 0 else moments[j] if i == 0 else half[i + j] + half[abs(i - j)]

    one = jnp.ones_like(moments[0])
    precond, direction, head = [one], [], []
    gamma_old = alpha_old = None
    for step in range(ITERS):
        gamma = form(precond, precond, gram)
        delta = gamma - form(precond, shifted(precond), gram)
        if step == 0:
            direction = precond
            alpha = gamma / delta
        else:
            beta = gamma / gamma_old
            alpha = gamma / (delta - beta * gamma / alpha_old)
            direction = added(precond, direction, beta)
        head = added(head, direction, alpha)
        moved = added(direction, shifted(direction), -1.0)
        precond = added(precond, moved, -alpha)
        gamma_old, alpha_old = gamma, alpha
    return head, precond, added(precond, shifted(precond), -1.0)


def combine_kernel(moments, basis, inv_root, scale, strip_basis, strip_inv_root, strip_scale,
                   head_field, residual, applied, h_buf, r_buf, a_buf, sems):
    row = jnp.sum(moments[...], axis=0)
    column = lane_index(1)
    raw = []
    for n in range(2 * ITERS):
        value = jnp.sum(jnp.where(column == n, row, 0.0), axis=1, keepdims=True)
        raw.append(jnp.broadcast_to(value, (8, LANES)))
    full = raw[:2]
    for n in range(2, 2 * ITERS):
        full.append(2.0 * raw[n] - raw[n % 2])
    lane = lane_index(LAYERS)
    low, high = lane < MERGE, lane >= LANES - MERGE
    targets = (
        (h_buf, head_field, inv_root, strip_inv_root),
        (r_buf, residual, scale, strip_scale),
        (a_buf, applied, scale, strip_scale),
    )
    copies = []
    for n, (weights, (buf, out, factor, strip_factor)) in enumerate(zip(recursion(full), targets)):
        weights = [jnp.concatenate([w] * TILES, axis=0) for w in weights]

        def total(fields, factors, at):
            value = weights[0] * fields[0, at]
            for j in range(1, len(weights)):
                value = value + weights[j] * fields[j, at]
            return factors[at] * value

        strips = [total(strip_basis, strip_factor, q) for q in range(STRIPS)]
        for row in range(ROWS):
            slot, q = divmod(row + DEPTH, STRIPS)
            base = PAIR * slot
            value = total(basis, factor, row)
            value = jnp.where(low, turn(strips[q], -base - EDGE), value)
            value = jnp.where(high, turn(strips[q], LANES - (base + PAIR - EDGE)), value)
            for k in range(TILES):
                buf[pl.ds(k * ROWS + row, 8, stride=TILES * ROWS)] = value[8 * k:8 * k + 8]
        copies.append(pltpu.make_async_copy(buf, out, sems.at[n]))
        copies[-1].start()
    for copy in copies:
        copy.wait()


def f32(*shape):
    return jax.ShapeDtypeStruct(shape, jnp.float32)


def scratch(*shape):
    return pltpu.VMEM(shape, jnp.float32)


VMEM = pl.BlockSpec(memory_space=pltpu.VMEM)
HBM = pl.BlockSpec(memory_space=pltpu.HBM)


def call(kernel, outs, scratches=(), ins=VMEM, out=VMEM):
    def run(*args):
        return pl.pallas_call(
            kernel,
            out_shape=outs,
            in_specs=[ins] * len(args),
            out_specs=[out] * len(outs),
            scratch_shapes=list(scratches),
            compiler_params=pltpu.CompilerParams(vmem_limit_bytes=32 * 1024 * 1024),
        )(*args)

    return run


def prepare(recharge, conduct, top_layer, fixed_head):
    flat = (LAYERS * ROWS, LANES)
    plane = pltpu.VMEM((ROWS, LANES), jnp.int32)
    args = (recharge.reshape(flat), conduct.reshape(flat), top_layer, fixed_head)
    return call(
        prepare_kernel,
        (f32(ROWS, WIDTH, LANES), f32(DEPTH, WIDTH, LANES)),
        [scratch(*flat), scratch(*flat), plane, plane, pltpu.SemaphoreType.DMA((4,))],
        ins=HBM,
    )(*[pltpu.with_memory_space_constraint(a, pltpu.HBM) for a in args])


def edges(both, far):
    dense = f32(DENSE, 8, LANES)
    return call(edges_kernel, (f32(SPAN, WIDTH, LANES), dense, dense))(both, far)


def own_columns(span):
    field, strip = f32(ROWS, LAYERS, LANES), f32(STRIPS, LAYERS, LANES)
    outs = (f32(BASIS, ROWS, LAYERS, LANES), field, field, f32(1, LANES), strip, strip, f32(STRIPS, 8, LANES))
    scratches = [scratch(FIRST, LAYERS, LANES)] * 2
    scratches += [scratch(FIRST - 2 * j, LAYERS, LANES) for j in range(ITERS + 1)]
    return call(own_kernel, outs, scratches)(span)


def strip_columns(moments, own, from_low, from_high):
    field = f32(STRIPS, LAYERS, LANES)
    outs = (f32(BASIS, STRIPS, LAYERS, LANES), field, field, f32(1, LANES))
    return call(strips_kernel, outs, [scratch(STRIPS, LAYERS, LANES)] * 3)(moments, *own, from_low, from_high)


def combine(moments, own, strips):
    flat = (LAYERS * ROWS, LANES)
    outs = call(
        combine_kernel,
        (f32(*flat),) * 3,
        [scratch(*flat)] * 3 + [pltpu.SemaphoreType.DMA((3,))],
        out=HBM,
    )(moments, *own, *strips)
    return tuple(out.reshape(LAYERS, ROWS, LANES) for out in outs)


def shift_both(low_going, high_going, axis):
    count = lax.axis_size(axis)
    up = [(i, i + 1) for i in range(count - 1)]
    down = [(target, source) for source, target in up]
    return lax.ppermute(high_going, axis, up), lax.ppermute(low_going, axis, down)


def between_chips(array):
    count = lax.axis_size(GX)
    pairs = []
    for i in range(1, count - 1, 2):
        pairs += [(i, i + 1), (i + 1, i)]
    return lax.ppermute(array, GX, pairs)


def spread_sum(row, axes):
    count = lax.axis_size(axes)
    return lax.all_to_all(jnp.broadcast_to(row[None], (count,) + row.shape), axes, 0, 0, tiled=True)


def local(recharge, conduct, top_layer, fixed_head):
    main, part = prepare(recharge, conduct, top_layer, fixed_head)
    far = between_chips(part)
    both = lax.all_gather(main, "c", axis=0, tiled=True)
    span, low_edge, high_edge = edges(both, far)
    from_low, from_high = shift_both(low_edge, high_edge, "y")
    *own, own_moments, root, source, fixed = own_columns(span)
    *strips, moments = strip_columns(own_moments, (root, source, fixed), from_low, from_high)
    moments = jnp.sum(spread_sum(moments, ("z", "c")), axis=0)
    moments = spread_sum(moments, ("x", "y"))
    return combine(moments, own, strips)


def solution(mesh):
    grid = Mesh(mesh.devices.reshape(12, 4, 2, 8), ("z", "x", "c", "y"))
    field, plane = P(None, GX, "y"), P(GX, "y")
    return jax.shard_map(
        local, mesh=grid, in_specs=(field, field, plane, plane), out_specs=(field, field, field), check_vma=False
    )
```

time: 71.7 us -> 69.9 us (0.975)
  waiting for transfers between devices: 3.48 us -> 1.16 us
  blocking collectives: 52 us -> 53.1 us
    ppermute x1, waiting for transfers between devices: 3.48 us -> 1.16 us  [shift_both(): lax.ppermute(low_going, axis, down)]
    all_to_all x2, blocking collectives: 43.3 us -> 44.3 us  [spread_sum(): lax.all_to_all(jnp.broadcast_to(row[None], (count,) + row.shape), axes, 0...]
  transfers between devices with their start and end apart: 3 -> 3, of which waited for: 1 -> 1; matrix products, arithmetic and copies ran while one was open for 0% -> 0% of each run, Pallas kernels for 1% -> 5%
where the time goes in v4:
time: 69.9 us; the launch traced here: 69.6 us
  blocking collectives  53.1 us (76%)
  Pallas kernels  7.59 us (11%)
  starting transfers between devices  7.09 us (10%)
  waiting for transfers between devices  1.16 us (2%)
  between operations  0.7 us (1%)
    all_to_all x2, blocking collectives, spread_sum(): lax.all_to_all(jnp.broadcast_to(row[None], (count,) + row.shape), axes, 0...  44.3 us
    all_gather x1, blocking collectives, local(): both = lax.all_gather(main, 'c', axis=0, tiled=True)  8.73 us
    pallas_call x5, Pallas kernels, run(): pl.pallas_call(kernel, out_shape=outs, in_specs=[ins] * len(args), out_sp...  7.59 us
    ppermute x1, starting transfers between devices, between_chips(): return lax.ppermute(array, GX, pairs)  4.5 us
  transfers between devices with their start and end apart: 3, of which 1 were waited for; matrix products, arithmetic and copies ran while one was open for 0% of the time, Pallas kernels for 5%

profile of v4, /device:TPU:1, one launch (start us, length us, event | category | flops | bytes accessed | tf_op | source)
XLA Modules:
  0.0 69.6 jit_solution(5203192134060498139)
XLA Ops:
  0.6 1.3 %shard_map.67 = (f32[8,104,128]{2,1,0:T(8,128)S(1)}, f32[6,104,128]{2,1,0:T(8,128)S(1)}) custom-call(f32[384,128]{1,0:T(8,128)} %bitcast.8, f32[384,128]{1,0:T(8,128)} %bitcast.9, s32[8,128]{1,0:T(8,128)} %top_layer.1, s32[8,128]{1,0:T(8,128)} %fixed_head.1), custom_call_target="tpu_custom_call" | custom-call | tf_op jit(solution)/shard_map/pallas_call | solution.py:393
  1.9 4.5 %collective-permute-start = (f32[6,104,128]{2,1,0:T(8,128)S(1)}, f32[6,104,128]{2,1,0:T(8,128)S(1)}, u32[]{:S(2)}, u32[]{:S(2)}) collective-permute-start(f32[6,104,128]{2,1,0:T(8,128)S(1)} %get-tuple-element.23), channel_id=1, source_target_pairs={{8,16},{16,8},{24,32},{32,24},{40,48},{48,40},{56,64},{64,56},{72,... | collective-permute-start | bytes 958472 | tf_op jit(solution)/shard_map/ppermute | solution.py:459
  6.4 8.7 %all_gather.3.both = f32[16,104,128]{2,1,0:T(8,128)S(1)} all-gather(f32[8,104,128]{2,1,0:T(8,128)S(1)} %get-tuple-element.22), channel_id=1, replica_groups=mesh['z'=12,'x'=4,'c'=2,'y'=8] {'c'}, dimensions={0}, use_global_device_ids=true | all-gather | bytes 1277952 | tf_op jit(solution)/shard_map/all_gather | solution.py:470
  15.2 0.0 collective-permute-done.far
  15.2 0.4 shard_map.68
  15.6 1.3 %collective-permute-start.1 = (f32[21,8,128]{2,1,0:T(8,128)S(1)}, f32[21,8,128]{2,1,0:T(8,128)S(1)}, u32[]{:S(2)}, u32[]{:S(2)}) collective-permute-start(f32[21,8,128]{2,1,0:T(8,128)S(1)} %get-tuple-element.29), channel_id=1, source_target_pairs={{0,1},{1,2},{2,3},{3,4},{4,5},{5,6},{6,7},{8,9},{9,10},{10,11},{11... | collective-permute-start | bytes 258056 | tf_op jit(solution)/shard_map/ppermute | solution.py:451
  16.9 1.3 %collective-permute-start.2 = (f32[21,8,128]{2,1,0:T(8,128)S(1)}, f32[21,8,128]{2,1,0:T(8,128)S(1)}, u32[]{:S(2)}, u32[]{:S(2)}) collective-permute-start(f32[21,8,128]{2,1,0:T(8,128)S(1)} %get-tuple-element.30), channel_id=1, source_target_pairs={{1,0},{2,1},{3,2},{4,3},{5,4},{6,5},{7,6},{9,8},{10,9},{11,10},{12... | collective-permute-start | bytes 258056 | tf_op jit(solution)/shard_map/ppermute | solution.py:451
  18.2 3.2 %shard_map.69 = (f32[6,8,48,128]{3,2,1,0:T(8,128)S(1)}, f32[8,48,128]{2,1,0:T(8,128)S(1)}, f32[8,48,128]{2,1,0:T(8,128)S(1)}, f32[1,128]{1,0:T(1,128)S(1)}, f32[...) custom-call(f32[20,104,128]{2,1,0:T(8,128)S(1)} %get-tuple-element.24.span), custom_call_target="tpu_custom_call" | custom-call | tf_op jit(solution)/shard_map/pallas_call | solution.py:393
  21.4 0.0 collective-permute-done.1.from_low
  21.4 1.2 %collective-permute-done.2.from_high = f32[21,8,128]{2,1,0:T(8,128)S(1)} collective-permute-done((f32[21,8,128]{2,1,0:T(8,128)S(1)}, f32[21,8,128]{2,1,0:T(8,128)S(1)}, u32[]{:S(2)}, u32[]{:S(2)}) %collective-permute-start.2) | collective-permute-done | bytes 86048 | tf_op jit(solution)/shard_map/ppermute | solution.py:451
  22.6 1.3 %shard_map.70 = (f32[6,7,48,128]{3,2,1,0:T(8,128)S(1)}, f32[7,48,128]{2,1,0:T(8,128)S(1)}, f32[7,48,128]{2,1,0:T(8,128)S(1)}, f32[1,128]{1,0:T(1,128)S(1)}) custom-call(f32[1,128]{1,0:T(1,128)S(1)} %get-tuple-element.25.own_moments, f32[7,48,128]{2,1,0:T(8,128)S(1)} %get-tuple-element.26.own_root, f32[7,48,128]{2,1,0:T(8,128)S(1)} %get-tuple-element.27.own_source, ...), custom_call_target="tpu_custom_call" | custom-call | tf_op jit(solution)/shard_map/pallas_call | solution.py:393
  23.9 26.0 %all_to_all.10 = f32[24,1,128]{2,1,0:T(1,128)S(1)} all-to-all(f32[24,1,128]{2,1,0:T(1,128)S(1)} %broadcast_in_dim.7), channel_id=1, replica_groups=mesh['z'=12,'x'=4,'c'=2,'y'=8] {'z','c'}, dimensions={0} | all-to-all | bytes 24576 | tf_op jit(solution)/shard_map/all_to_all | solution.py:464
  49.9 18.3 %all_to_all.11.moments = f32[32,1,128]{2,1,0:T(1,128)S(1)} all-to-all(f32[32,1,128]{2,1,0:T(1,128)S(1)} %broadcast_in_dim.16), channel_id=1, replica_groups=mesh['z'=12,'x'=4,'c'=2,'y'=8] {'x','y'}, dimensions={0} | all-to-all | bytes 32768 | tf_op jit(solution)/shard_map/all_to_all | solution.py:464
  68.3 1.4 %shard_map.71 = (f32[384,128]{1,0:T(8,128)}, f32[384,128]{1,0:T(8,128)}, f32[384,128]{1,0:T(8,128)}) custom-call(f32[32,1,128]{2,1,0:T(1,128)S(1)} %all_to_all.11.moments, f32[6,8,48,128]{3,2,1,0:T(8,128)S(1)} %get-tuple-element.32.basis, f32[8,48,128]{2,1,0:T(8,128)S(1)} %get-tuple-element.33.inv_root, f32[8,48,128]{2,1,0:T(8,128)S(1)} %get-tuple-element.34.scale, ...), custom_call_target="tpu_custom_call" | custom-call | tf_op jit(solution)/shard_map/pallas_call | solution.py:393
  (3 shorter events, 0.0 us)
Async XLA Ops:
  1.9 13.2 %collective-permute-start = (f32[6,104,128]{2,1,0:T(8,128)S(1)}, f32[6,104,128]{2,1,0:T(8,128)S(1)}, u32[]{:S(2)}, u32[]{:S(2)}) collective-permute-start(f32[6,104,128]{2,1,0:T(8,128)S(1)} %get-tuple-element.23), channel_id=1, source_target_pairs={{8,16},{16,8},{24,32},{32,24},{40,48},{48,40},{56,64},{64,56},{72,... | collective-permute-start | bytes 958472 | tf_op jit(solution)/shard_map/ppermute | solution.py:459
  15.6 5.8 %collective-permute-start.1 = (f32[21,8,128]{2,1,0:T(8,128)S(1)}, f32[21,8,128]{2,1,0:T(8,128)S(1)}, u32[]{:S(2)}, u32[]{:S(2)}) collective-permute-start(f32[21,8,128]{2,1,0:T(8,128)S(1)} %get-tuple-element.29), channel_id=1, source_target_pairs={{0,1},{1,2},{2,3},{3,4},{4,5},{5,6},{6,7},{8,9},{9,10},{10,11},{11... | collective-permute-start | bytes 258056 | tf_op jit(solution)/shard_map/ppermute | solution.py:451
  16.9 5.6 %collective-permute-start.2 = (f32[21,8,128]{2,1,0:T(8,128)S(1)}, f32[21,8,128]{2,1,0:T(8,128)S(1)}, u32[]{:S(2)}, u32[]{:S(2)}) collective-permute-start(f32[21,8,128]{2,1,0:T(8,128)S(1)} %get-tuple-element.30), channel_id=1, source_target_pairs={{1,0},{2,1},{3,2},{4,3},{5,4},{6,5},{7,6},{9,8},{10,9},{11,10},{12... | collective-permute-start | bytes 258056 | tf_op jit(solution)/shard_map/ppermute | solution.py:451

commit v5 on v4

--- a/solution.py
+++ b/solution.py
@@ -459,9 +459,11 @@
     return lax.ppermute(array, GX, pairs)
 
 
-def spread_sum(row, axes):
+def spread_sum(row, axes, leader):
     count = lax.axis_size(axes)
-    return lax.all_to_all(jnp.broadcast_to(row[None], (count,) + row.shape), axes, 0, 0, tiled=True)
+    group = [(leader + i) % count for i in range(count)]
+    rows = jnp.broadcast_to(row[None], (count,) + row.shape)
+    return lax.all_to_all(rows, axes, 0, 0, axis_index_groups=[group], tiled=True)
 
 
 def local(recharge, conduct, top_layer, fixed_head):
@@ -472,8 +474,8 @@
     from_low, from_high = shift_both(low_edge, high_edge, "y")
     *own, own_moments, root, source, fixed = own_columns(span)
     *strips, moments = strip_columns(own_moments, (root, source, fixed), from_low, from_high)
-    moments = jnp.sum(spread_sum(moments, ("z", "c")), axis=0)
-    moments = spread_sum(moments, ("x", "y"))
+    moments = jnp.sum(spread_sum(moments, ("z", "c"), 8 * 2), axis=0)
+    moments = spread_sum(moments, ("x", "y"), 3 * 8 + 4)
     return combine(moments, own, strips)
 
 

time: 69.9 us -> 63.2 us (0.904)
  blocking collectives: 53.1 us -> 45.9 us
    all_to_all x2, blocking collectives: 44.3 us -> 37.2 us  [spread_sum(): lax.all_to_all(rows, axes, 0, 0, axis_index_groups=[group], tiled=True)]
where the time goes in v5:
time: 63.2 us; the launch traced here: 62.5 us
  blocking collectives  45.9 us (73%)
  Pallas kernels  7.59 us (12%)
  starting transfers between devices  7.09 us (11%)
  waiting for transfers between devices  1.16 us (2%)
  between operations  0.7 us (1%)
    all_to_all x2, blocking collectives, spread_sum(): lax.all_to_all(rows, axes, 0, 0, axis_index_groups=[group], tiled=True)  37.2 us
    all_gather x1, blocking collectives, local(): both = lax.all_gather(main, 'c', axis=0, tiled=True)  8.73 us
    pallas_call x5, Pallas kernels, run(): pl.pallas_call(kernel, out_shape=outs, in_specs=[ins] * len(args), out_sp...  7.59 us
    ppermute x1, starting transfers between devices, between_chips(): return lax.ppermute(array, GX, pairs)  4.5 us
    ppermute x1, starting transfers between devices, shift_both(): lax.ppermute(high_going, axis, up)  1.29 us
    ppermute x1, starting transfers between devices, shift_both(): lax.ppermute(low_going, axis, down)  1.29 us
  transfers between devices with their start and end apart: 3, of which 1 were waited for; matrix products, arithmetic and copies ran while one was open for 0% of the time, Pallas kernels for 5%

profile of v5, /device:TPU:1, one launch (start us, length us, event | category | flops | bytes accessed | tf_op | source)
XLA Modules:
  0.0 62.5 jit_solution(7151767730657012654)
XLA Ops:
  0.6 1.3 %shard_map.67 = (f32[8,104,128]{2,1,0:T(8,128)S(1)}, f32[6,104,128]{2,1,0:T(8,128)S(1)}) custom-call(f32[384,128]{1,0:T(8,128)} %bitcast.8, f32[384,128]{1,0:T(8,128)} %bitcast.9, s32[8,128]{1,0:T(8,128)} %top_layer.1, s32[8,128]{1,0:T(8,128)} %fixed_head.1), custom_call_target="tpu_custom_call" | custom-call | tf_op jit(solution)/shard_map/pallas_call | solution.py:393
  1.9 4.5 %collective-permute-start = (f32[6,104,128]{2,1,0:T(8,128)S(1)}, f32[6,104,128]{2,1,0:T(8,128)S(1)}, u32[]{:S(2)}, u32[]{:S(2)}) collective-permute-start(f32[6,104,128]{2,1,0:T(8,128)S(1)} %get-tuple-element.23), channel_id=1, source_target_pairs={{8,16},{16,8},{24,32},{32,24},{40,48},{48,40},{56,64},{64,56},{72,... | collective-permute-start | bytes 958472 | tf_op jit(solution)/shard_map/ppermute | solution.py:459
  6.4 8.7 %all_gather.3.both = f32[16,104,128]{2,1,0:T(8,128)S(1)} all-gather(f32[8,104,128]{2,1,0:T(8,128)S(1)} %get-tuple-element.22), channel_id=1, replica_groups=mesh['z'=12,'x'=4,'c'=2,'y'=8] {'c'}, dimensions={0}, use_global_device_ids=true | all-gather | bytes 1277952 | tf_op jit(solution)/shard_map/all_gather | solution.py:472
  15.2 0.0 collective-permute-done.far
  15.2 0.4 shard_map.68
  15.6 1.3 %collective-permute-start.1 = (f32[21,8,128]{2,1,0:T(8,128)S(1)}, f32[21,8,128]{2,1,0:T(8,128)S(1)}, u32[]{:S(2)}, u32[]{:S(2)}) collective-permute-start(f32[21,8,128]{2,1,0:T(8,128)S(1)} %get-tuple-element.29), channel_id=1, source_target_pairs={{0,1},{1,2},{2,3},{3,4},{4,5},{5,6},{6,7},{8,9},{9,10},{10,11},{11... | collective-permute-start | bytes 258056 | tf_op jit(solution)/shard_map/ppermute | solution.py:451
  16.9 1.3 %collective-permute-start.2 = (f32[21,8,128]{2,1,0:T(8,128)S(1)}, f32[21,8,128]{2,1,0:T(8,128)S(1)}, u32[]{:S(2)}, u32[]{:S(2)}) collective-permute-start(f32[21,8,128]{2,1,0:T(8,128)S(1)} %get-tuple-element.30), channel_id=1, source_target_pairs={{1,0},{2,1},{3,2},{4,3},{5,4},{6,5},{7,6},{9,8},{10,9},{11,10},{12... | collective-permute-start | bytes 258056 | tf_op jit(solution)/shard_map/ppermute | solution.py:451
  18.2 3.2 %shard_map.69 = (f32[6,8,48,128]{3,2,1,0:T(8,128)S(1)}, f32[8,48,128]{2,1,0:T(8,128)S(1)}, f32[8,48,128]{2,1,0:T(8,128)S(1)}, f32[1,128]{1,0:T(1,128)S(1)}, f32[...) custom-call(f32[20,104,128]{2,1,0:T(8,128)S(1)} %get-tuple-element.24.span), custom_call_target="tpu_custom_call" | custom-call | tf_op jit(solution)/shard_map/pallas_call | solution.py:393
  21.4 0.0 collective-permute-done.1.from_low
  21.4 1.2 %collective-permute-done.2.from_high = f32[21,8,128]{2,1,0:T(8,128)S(1)} collective-permute-done((f32[21,8,128]{2,1,0:T(8,128)S(1)}, f32[21,8,128]{2,1,0:T(8,128)S(1)}, u32[]{:S(2)}, u32[]{:S(2)}) %collective-permute-start.2) | collective-permute-done | bytes 86048 | tf_op jit(solution)/shard_map/ppermute | solution.py:451
  22.6 1.3 %shard_map.70 = (f32[6,7,48,128]{3,2,1,0:T(8,128)S(1)}, f32[7,48,128]{2,1,0:T(8,128)S(1)}, f32[7,48,128]{2,1,0:T(8,128)S(1)}, f32[1,128]{1,0:T(1,128)S(1)}) custom-call(f32[1,128]{1,0:T(1,128)S(1)} %get-tuple-element.25.own_moments, f32[7,48,128]{2,1,0:T(8,128)S(1)} %get-tuple-element.26.own_root, f32[7,48,128]{2,1,0:T(8,128)S(1)} %get-tuple-element.27.own_source, ...), custom_call_target="tpu_custom_call" | custom-call | tf_op jit(solution)/shard_map/pallas_call | solution.py:393
  23.9 23.3 %all_to_all.10 = f32[24,1,128]{2,1,0:T(1,128)S(1)} all-to-all(f32[24,1,128]{2,1,0:T(1,128)S(1)} %broadcast_in_dim.7), channel_id=1, replica_groups={{512,520,576,584,640,648,704,712,0,8,64,72,128,136,192,200,256,264,320,..., dimensions={0} | all-to-all | bytes 24576 | tf_op jit(solution)/shard_map/all_to_all | solution.py:466
  47.2 13.9 %all_to_all.11.moments = f32[32,1,128]{2,1,0:T(1,128)S(1)} all-to-all(f32[32,1,128]{2,1,0:T(1,128)S(1)} %broadcast_in_dim.16), channel_id=1, replica_groups={{52,53,54,55,0,1,2,3,4,5,6,7,16,17,18,19,20,21,22,23,32,33,34,35,36,37,..., dimensions={0} | all-to-all | bytes 32768 | tf_op jit(solution)/shard_map/all_to_all | solution.py:466
  61.1 1.4 %shard_map.71 = (f32[384,128]{1,0:T(8,128)}, f32[384,128]{1,0:T(8,128)}, f32[384,128]{1,0:T(8,128)}) custom-call(f32[32,1,128]{2,1,0:T(1,128)S(1)} %all_to_all.11.moments, f32[6,8,48,128]{3,2,1,0:T(8,128)S(1)} %get-tuple-element.32.basis, f32[8,48,128]{2,1,0:T(8,128)S(1)} %get-tuple-element.33.inv_root, f32[8,48,128]{2,1,0:T(8,128)S(1)} %get-tuple-element.34.scale, ...), custom_call_target="tpu_custom_call" | custom-call | tf_op jit(solution)/shard_map/pallas_call | solution.py:393
  (3 shorter events, 0.0 us)
Async XLA Ops:
  1.9 13.2 %collective-permute-start = (f32[6,104,128]{2,1,0:T(8,128)S(1)}, f32[6,104,128]{2,1,0:T(8,128)S(1)}, u32[]{:S(2)}, u32[]{:S(2)}) collective-permute-start(f32[6,104,128]{2,1,0:T(8,128)S(1)} %get-tuple-element.23), channel_id=1, source_target_pairs={{8,16},{16,8},{24,32},{32,24},{40,48},{48,40},{56,64},{64,56},{72,... | collective-permute-start | bytes 958472 | tf_op jit(solution)/shard_map/ppermute | solution.py:459
  15.6 5.8 %collective-permute-start.1 = (f32[21,8,128]{2,1,0:T(8,128)S(1)}, f32[21,8,128]{2,1,0:T(8,128)S(1)}, u32[]{:S(2)}, u32[]{:S(2)}) collective-permute-start(f32[21,8,128]{2,1,0:T(8,128)S(1)} %get-tuple-element.29), channel_id=1, source_target_pairs={{0,1},{1,2},{2,3},{3,4},{4,5},{5,6},{6,7},{8,9},{9,10},{10,11},{11... | collective-permute-start | bytes 258056 | tf_op jit(solution)/shard_map/ppermute | solution.py:451
  16.9 5.6 %collective-permute-start.2 = (f32[21,8,128]{2,1,0:T(8,128)S(1)}, f32[21,8,128]{2,1,0:T(8,128)S(1)}, u32[]{:S(2)}, u32[]{:S(2)}) collective-permute-start(f32[21,8,128]{2,1,0:T(8,128)S(1)} %get-tuple-element.30), channel_id=1, source_target_pairs={{1,0},{2,1},{3,2},{4,3},{5,4},{6,5},{7,6},{9,8},{10,9},{11,10},{12... | collective-permute-start | bytes 258056 | tf_op jit(solution)/shard_map/ppermute | solution.py:451

commit v6 on v5

--- a/solution.py
+++ b/solution.py
@@ -22,7 +22,8 @@
 PAIR = 2 * SIDE
 FOLD = 3
 STRIPS = 7
-DENSE = 3 * STRIPS
+DENSE = 2 * STRIPS + 1
+FAR = (2 * DEPTH - 1) * LAYERS + 8
 MERGE = 8
 
 store_term = 0.1
@@ -107,29 +108,37 @@
     copies = [pltpu.make_async_copy(a, b, sems.at[n]) for n, (a, b) in enumerate(pairs)]
     for copy in copies:
         copy.start()
-    for copy in copies:
-        copy.wait()
     core = lax.axis_index("c")
     level = TILES * lax.broadcasted_iota(jnp.int32, (8, LANES), 0)
+    tiles = [(row, k, pl.ds(k * ROWS + row, 8, stride=TILES * ROWS)) for row in range(ROWS) for k in range(TILES)]
+    copies[0].wait()
+    copies[1].wait()
+    for row, k, layers in tiles:
+        root = jnp.where(level + k >= t_buf[row:row + 1], jnp.sqrt(c_buf[layers]), 0.0)
+        main[row, 8 * k:8 * k + 8] = root
+    nearest = [jnp.where(core == 0, n, ROWS - 1 - n) for n in range(DEPTH)]
+    for n, row in enumerate(nearest):
+        part[n * LAYERS:(n + 1) * LAYERS] = main[row, :LAYERS]
+    copies[2].wait()
+    copies[3].wait()
+    for row, k, layers in tiles:
+        main[row, LAYERS + 8 * k:LAYERS + 8 * k + 8] = main[row, 8 * k:8 * k + 8] * r_buf[layers]
+    for n, row in enumerate(nearest[:-1]):
+        part[(DEPTH + n) * LAYERS:(DEPTH + n + 1) * LAYERS] = main[row, LAYERS:2 * LAYERS]
+    fixed = f_buf[...].astype(jnp.float32)
+    part[FAR - 8:] = fixed
     for row in range(ROWS):
-        top = t_buf[row:row + 1]
-        for k in range(TILES):
-            layers = pl.ds(k * ROWS + row, 8, stride=TILES * ROWS)
-            root = jnp.where(level + k >= top, jnp.sqrt(c_buf[layers]), 0.0)
-            main[row, 8 * k:8 * k + 8] = root
-            main[row, LAYERS + 8 * k:LAYERS + 8 * k + 8] = root * r_buf[layers]
-        main[row, 2 * LAYERS:] = jnp.broadcast_to(f_buf[row:row + 1].astype(jnp.float32), (8, LANES))
-    for row in range(DEPTH):
-        part[row] = main[(ROWS - DEPTH) * core + row]
+        main[row, 2 * LAYERS:] = jnp.broadcast_to(fixed[row:row + 1], (8, LANES))
 
 
 def units(strip):
     for slot in range(FOLD):
         row = slot * STRIPS + strip
         if row < SPAN:
-            for unit in range(2 * TILES + 1):
+            for unit in range(2 * TILES):
                 group, place = divmod(unit, TILES)
-                yield 3 * strip + group, place, slot, row, 8 * unit
+                yield 2 * strip + group, place, slot, row, 8 * unit
+            yield DENSE - 1, 0, slot, row, 2 * LAYERS
 
 
 def edges_kernel(both, far, span, low_edge, high_edge):
@@ -137,20 +146,33 @@
     for n in range(ROWS + DEPTH):
         span[DEPTH * (1 - core) + n] = both[(ROWS - DEPTH) * core + n]
     for n in range(DEPTH):
-        span[(ROWS + DEPTH) * core + n] = far[n]
+        row = jnp.where(core == 0, DEPTH - 1 - n, ROWS + DEPTH + n)
+        span[row, :LAYERS] = far[n * LAYERS:(n + 1) * LAYERS]
+        if n < DEPTH - 1:
+            span[row, LAYERS:2 * LAYERS] = far[(DEPTH + n) * LAYERS:(DEPTH + n + 1) * LAYERS]
+        else:
+            span[row, LAYERS:2 * LAYERS] = jnp.zeros((LAYERS, LANES), jnp.float32)
+        fixed = far[pl.ds(FAR - 8 + jnp.where(core == 0, ROWS - 1 - n, n), 1)]
+        span[row, 2 * LAYERS:] = jnp.broadcast_to(fixed, (8, LANES))
     lane = lane_index(8)
+    sublane = lax.broadcasted_iota(jnp.int32, (8, LANES), 0)
+    blank = jnp.zeros((8, LANES), jnp.float32)
+    low, high = [blank] * DENSE, [blank] * DENSE
     for strip in range(STRIPS):
-        low = {3 * strip + g: jnp.zeros((8, LANES), jnp.float32) for g in range(3)}
-        high = dict(low)
         for dense, place, slot, row, at in units(strip):
             to = PAIR * slot + EDGE * place
             turned = turn(span[row, at:at + 8], to)
-            low[dense] = jnp.where(between(lane, to, to + EDGE), turned, low[dense])
-            to = (to - EDGE) % LANES
-            high[dense] = jnp.where(between(lane, to, to + EDGE), turned, high[dense])
-        for dense in low:
+            back = (to - EDGE) % LANES
+            take_low, take_high = between(lane, to, to + EDGE), between(lane, back, back + EDGE)
+            if dense == DENSE - 1:
+                take_low, take_high = take_low & (sublane == strip), take_high & (sublane == strip)
+            low[dense] = jnp.where(take_low, turned, low[dense])
+            high[dense] = jnp.where(take_high, turned, high[dense])
+        for dense in (2 * strip, 2 * strip + 1):
             low_edge[dense] = low[dense]
             high_edge[dense] = high[dense]
+    low_edge[DENSE - 1] = low[-1]
+    high_edge[DENSE - 1] = high[-1]
 
 
 def own_kernel(span, basis, inv_root, scale, moments, strip_root, strip_source, strip_fixed, g, diag, *t):
@@ -195,6 +217,8 @@
     moments[...] = as_row(lax.fori_loop(0, ROWS // unroll, finish, (zero,) * (2 * ITERS)))
 
     lane = lane_index(8)
+    sublane = lax.broadcasted_iota(jnp.int32, (8, LANES), 0)
+    heads = jnp.zeros((8, LANES), jnp.float32)
     for strip in range(STRIPS):
         for unit in range(2 * TILES + 1):
             tile = jnp.zeros((8, LANES), jnp.float32)
@@ -210,7 +234,8 @@
             elif unit < 2 * TILES:
                 strip_source[strip, 8 * unit - LAYERS:8 * unit - LAYERS + 8] = tile
             else:
-                strip_fixed[strip] = tile
+                heads = jnp.where(sublane == strip, tile, heads)
+    strip_fixed[...] = heads
 
 
 def strips_kernel(own_moments, own_root, own_source, own_fixed, from_low, from_high,
@@ -222,18 +247,17 @@
         low_lanes = low_lanes | between(lane, base, base + EDGE)
         high_lanes = high_lanes | between(lane, base + PAIR - EDGE, base + PAIR)
 
-    def with_halo(own, dense, place):
+    def with_halo(own, dense, place=0):
         low = turn(from_low[dense], EDGE - EDGE * place)
         high = turn(from_high[dense], PAIR - EDGE - EDGE * place)
         return jnp.where(low_lanes, low, jnp.where(high_lanes, high, own))
 
-    fixed = []
+    fixed = with_halo(own_fixed[...], DENSE - 1)
     for q in range(STRIPS):
         for k in range(TILES):
             tile = pl.ds(8 * k, 8)
-            root[q, tile] = with_halo(own_root[q, tile], 3 * q, k)
-            source[q, tile] = with_halo(own_source[q, tile], 3 * q + 1, k)
-        fixed.append(with_halo(own_fixed[q], 3 * q + 2, 0)[:1])
+            root[q, tile] = with_halo(own_root[q, tile], 2 * q, k)
+            source[q, tile] = with_halo(own_source[q, tile], 2 * q + 1, k)
 
     def sums(ref, at):
         rows = [ref[(*at, q)] for q in range(STRIPS)]
@@ -250,7 +274,7 @@
 
     weights = []
     for q, total in enumerate(sums(root, ())):
-        d, g[q], basis[0, q] = start_fields(root[q], source[q], fixed[q], total)
+        d, g[q], basis[0, q] = start_fields(root[q], source[q], fixed[q:q + 1], total)
         inv, ratio = outer_factors(root[q], d)
         inv_root[q] = inv
         scale[q] = ratio
@@ -408,7 +432,7 @@
     args = (recharge.reshape(flat), conduct.reshape(flat), top_layer, fixed_head)
     return call(
         prepare_kernel,
-        (f32(ROWS, WIDTH, LANES), f32(DEPTH, WIDTH, LANES)),
+        (f32(ROWS, WIDTH, LANES), f32(FAR, LANES)),
         [scratch(*flat), scratch(*flat), plane, plane, pltpu.SemaphoreType.DMA((4,))],
         ins=HBM,
     )(*[pltpu.with_memory_space_constraint(a, pltpu.HBM) for a in args])
@@ -421,7 +445,7 @@
 
 def own_columns(span):
     field, strip = f32(ROWS, LAYERS, LANES), f32(STRIPS, LAYERS, LANES)
-    outs = (f32(BASIS, ROWS, LAYERS, LANES), field, field, f32(1, LANES), strip, strip, f32(STRIPS, 8, LANES))
+    outs = (f32(BASIS, ROWS, LAYERS, LANES), field, field, f32(1, LANES), strip, strip, f32(8, LANES))
     scratches = [scratch(FIRST, LAYERS, LANES)] * 2
     scratches += [scratch(FIRST - 2 * j, LAYERS, LANES) for j in range(ITERS + 1)]
     return call(own_kernel, outs, scratches)(span)
@@ -474,8 +498,8 @@
     from_low, from_high = shift_both(low_edge, high_edge, "y")
     *own, own_moments, root, source, fixed = own_columns(span)
     *strips, moments = strip_columns(own_moments, (root, source, fixed), from_low, from_high)
-    moments = jnp.sum(spread_sum(moments, ("z", "c"), 8 * 2), axis=0)
-    moments = spread_sum(moments, ("x", "y"), 3 * 8 + 4)
+    moments = jnp.sum(spread_sum(moments, ("z", "c"), 7 * 2 + 1), axis=0)
+    moments = spread_sum(moments, ("x", "y"), 2 * 8 + 4)
     return combine(moments, own, strips)
 
 

time: 63.2 us -> 61.5 us (0.973)
  blocking collectives: 45.9 us -> 45 us
  waiting for transfers between devices: 1.16 us -> 0.49 us
    all_to_all x2, blocking collectives: 37.2 us -> 36.2 us  [spread_sum(): lax.all_to_all(rows, axes, 0, 0, axis_index_groups=[group], tiled=True)]
    ppermute x1, waiting for transfers between devices: 1.16 us -> 0.48 us  [shift_both(): lax.ppermute(low_going, axis, down)]
where the time goes in v6:
time: 61.5 us; the launch traced here: 60.7 us
  blocking collectives  45 us (73%)
  Pallas kernels  7.46 us (12%)
  starting transfers between devices  7.08 us (12%)
  between operations  0.7 us (1%)
    all_to_all x2, blocking collectives, spread_sum(): lax.all_to_all(rows, axes, 0, 0, axis_index_groups=[group], tiled=True)  36.2 us
    all_gather x1, blocking collectives, local(): both = lax.all_gather(main, 'c', axis=0, tiled=True)  8.73 us
    pallas_call x5, Pallas kernels, run(): pl.pallas_call(kernel, out_shape=outs, in_specs=[ins] * len(args), out_sp...  7.46 us
    ppermute x1, starting transfers between devices, between_chips(): return lax.ppermute(array, GX, pairs)  4.5 us
    ppermute x1, starting transfers between devices, shift_both(): lax.ppermute(high_going, axis, up)  1.29 us
    ppermute x1, starting transfers between devices, shift_both(): lax.ppermute(low_going, axis, down)  1.29 us
  transfers between devices with their start and end apart: 3, of which 1 were waited for; matrix products, arithmetic and copies ran while one was open for 0% of the time, Pallas kernels for 5%

profile of v6, /device:TPU:1, one launch (start us, length us, event | category | flops | bytes accessed | tf_op | source)
XLA Modules:
  0.0 60.7 jit_solution(17565715776444476760)
XLA Ops:
  0.6 1.2 %shard_map.67 = (f32[8,104,128]{2,1,0:T(8,128)S(1)}, f32[536,128]{1,0:T(8,128)S(1)}) custom-call(f32[384,128]{1,0:T(8,128)} %bitcast.8, f32[384,128]{1,0:T(8,128)} %bitcast.9, s32[8,128]{1,0:T(8,128)} %top_layer.1, s32[8,128]{1,0:T(8,128)} %fixed_head.1), custom_call_target="tpu_custom_call" | custom-call | tf_op jit(solution)/shard_map/pallas_call | solution.py:417
  1.8 4.5 %collective-permute-start = (f32[536,128]{1,0:T(8,128)S(1)}, f32[536,128]{1,0:T(8,128)S(1)}, u32[]{:S(2)}, u32[]{:S(2)}) collective-permute-start(f32[536,128]{1,0:T(8,128)S(1)} %get-tuple-element.23), channel_id=1, source_target_pairs={{8,16},{16,8},{24,32},{32,24},{40,48},{48,40},{56,64},{64,56},{72,... | collective-permute-start | bytes 823304 | tf_op jit(solution)/shard_map/ppermute | solution.py:483
  6.3 8.7 %all_gather.3.both = f32[16,104,128]{2,1,0:T(8,128)S(1)} all-gather(f32[8,104,128]{2,1,0:T(8,128)S(1)} %get-tuple-element.22), channel_id=1, replica_groups=mesh['z'=12,'x'=4,'c'=2,'y'=8] {'c'}, dimensions={0}, use_global_device_ids=true | all-gather | bytes 1277952 | tf_op jit(solution)/shard_map/all_gather | solution.py:496
  15.1 0.0 collective-permute-done.far
  15.1 0.4 shard_map.68
  15.5 1.3 %collective-permute-start.1 = (f32[15,8,128]{2,1,0:T(8,128)S(1)}, f32[15,8,128]{2,1,0:T(8,128)S(1)}, u32[]{:S(2)}, u32[]{:S(2)}) collective-permute-start(f32[15,8,128]{2,1,0:T(8,128)S(1)} %get-tuple-element.29), channel_id=1, source_target_pairs={{0,1},{1,2},{2,3},{3,4},{4,5},{5,6},{6,7},{8,9},{9,10},{10,11},{11... | collective-permute-start | bytes 184328 | tf_op jit(solution)/shard_map/ppermute | solution.py:475
  16.8 1.3 %collective-permute-start.2 = (f32[15,8,128]{2,1,0:T(8,128)S(1)}, f32[15,8,128]{2,1,0:T(8,128)S(1)}, u32[]{:S(2)}, u32[]{:S(2)}) collective-permute-start(f32[15,8,128]{2,1,0:T(8,128)S(1)} %get-tuple-element.30), channel_id=1, source_target_pairs={{1,0},{2,1},{3,2},{4,3},{5,4},{6,5},{7,6},{9,8},{10,9},{11,10},{12... | collective-permute-start | bytes 184328 | tf_op jit(solution)/shard_map/ppermute | solution.py:475
  18.1 3.2 %shard_map.69 = (f32[6,8,48,128]{3,2,1,0:T(8,128)S(1)}, f32[8,48,128]{2,1,0:T(8,128)S(1)}, f32[8,48,128]{2,1,0:T(8,128)S(1)}, f32[1,128]{1,0:T(1,128)S(1)}, f32[...) custom-call(f32[20,104,128]{2,1,0:T(8,128)S(1)} %get-tuple-element.24.span), custom_call_target="tpu_custom_call" | custom-call | tf_op jit(solution)/shard_map/pallas_call | solution.py:417
  21.3 0.0 collective-permute-done.1.from_low
  21.3 0.5 collective-permute-done.2.from_high
  21.8 1.3 %shard_map.70 = (f32[6,7,48,128]{3,2,1,0:T(8,128)S(1)}, f32[7,48,128]{2,1,0:T(8,128)S(1)}, f32[7,48,128]{2,1,0:T(8,128)S(1)}, f32[1,128]{1,0:T(1,128)S(1)}) custom-call(f32[1,128]{1,0:T(1,128)S(1)} %get-tuple-element.25.own_moments, f32[7,48,128]{2,1,0:T(8,128)S(1)} %get-tuple-element.26.own_root, f32[7,48,128]{2,1,0:T(8,128)S(1)} %get-tuple-element.27.own_source, ...), custom_call_target="tpu_custom_call" | custom-call | tf_op jit(solution)/shard_map/pallas_call | solution.py:417
  23.1 22.9 %all_to_all.10 = f32[24,1,128]{2,1,0:T(1,128)S(1)} all-to-all(f32[24,1,128]{2,1,0:T(1,128)S(1)} %broadcast_in_dim.7), channel_id=1, replica_groups={{456,512,520,576,584,640,648,704,712,0,8,64,72,128,136,192,200,256,264,..., dimensions={0} | all-to-all | bytes 24576 | tf_op jit(solution)/shard_map/all_to_all | solution.py:490
  46.0 13.3 %all_to_all.11.moments = f32[32,1,128]{2,1,0:T(1,128)S(1)} all-to-all(f32[32,1,128]{2,1,0:T(1,128)S(1)} %broadcast_in_dim.16), channel_id=1, replica_groups={{36,37,38,39,48,49,50,51,52,53,54,55,0,1,2,3,4,5,6,7,16,17,18,19,20,21,..., dimensions={0} | all-to-all | bytes 32768 | tf_op jit(solution)/shard_map/all_to_all | solution.py:490
  59.4 1.4 %shard_map.71 = (f32[384,128]{1,0:T(8,128)}, f32[384,128]{1,0:T(8,128)}, f32[384,128]{1,0:T(8,128)}) custom-call(f32[32,1,128]{2,1,0:T(1,128)S(1)} %all_to_all.11.moments, f32[6,8,48,128]{3,2,1,0:T(8,128)S(1)} %get-tuple-element.32.basis, f32[8,48,128]{2,1,0:T(8,128)S(1)} %get-tuple-element.33.inv_root, f32[8,48,128]{2,1,0:T(8,128)S(1)} %get-tuple-element.34.scale, ...), custom_call_target="tpu_custom_call" | custom-call | tf_op jit(solution)/shard_map/pallas_call | solution.py:417
  (3 shorter events, 0.0 us)
Async XLA Ops:
  1.8 13.2 %collective-permute-start = (f32[536,128]{1,0:T(8,128)S(1)}, f32[536,128]{1,0:T(8,128)S(1)}, u32[]{:S(2)}, u32[]{:S(2)}) collective-permute-start(f32[536,128]{1,0:T(8,128)S(1)} %get-tuple-element.23), channel_id=1, source_target_pairs={{8,16},{16,8},{24,32},{32,24},{40,48},{48,40},{56,64},{64,56},{72,... | collective-permute-start | bytes 823304 | tf_op jit(solution)/shard_map/ppermute | solution.py:483
  15.5 5.8 %collective-permute-start.1 = (f32[15,8,128]{2,1,0:T(8,128)S(1)}, f32[15,8,128]{2,1,0:T(8,128)S(1)}, u32[]{:S(2)}, u32[]{:S(2)}) collective-permute-start(f32[15,8,128]{2,1,0:T(8,128)S(1)} %get-tuple-element.29), channel_id=1, source_target_pairs={{0,1},{1,2},{2,3},{3,4},{4,5},{5,6},{6,7},{8,9},{9,10},{10,11},{11... | collective-permute-start | bytes 184328 | tf_op jit(solution)/shard_map/ppermute | solution.py:475
  16.8 5.0 %collective-permute-start.2 = (f32[15,8,128]{2,1,0:T(8,128)S(1)}, f32[15,8,128]{2,1,0:T(8,128)S(1)}, u32[]{:S(2)}, u32[]{:S(2)}) collective-permute-start(f32[15,8,128]{2,1,0:T(8,128)S(1)} %get-tuple-element.30), channel_id=1, source_target_pairs={{1,0},{2,1},{3,2},{4,3},{5,4},{6,5},{7,6},{9,8},{10,9},{11,10},{12... | collective-permute-start | bytes 184328 | tf_op jit(solution)/shard_map/ppermute | solution.py:475

commit v7 on v6

--- a/solution.py
+++ b/solution.py
@@ -141,7 +141,13 @@
             yield DENSE - 1, 0, slot, row, 2 * LAYERS
 
 
-def edges_kernel(both, far, span, low_edge, high_edge):
+def edges_kernel(both, far, span, first_edge, second_edge):
+    even = lax.rem(lax.axis_index("y"), 2) == 0
+
+    def put(dense, low, high):
+        first_edge[dense] = jnp.where(even, high, low)
+        second_edge[dense] = jnp.where(even, low, high)
+
     core = lax.axis_index("c")
     for n in range(ROWS + DEPTH):
         span[DEPTH * (1 - core) + n] = both[(ROWS - DEPTH) * core + n]
@@ -169,10 +175,8 @@
             low[dense] = jnp.where(take_low, turned, low[dense])
             high[dense] = jnp.where(take_high, turned, high[dense])
         for dense in (2 * strip, 2 * strip + 1):
-            low_edge[dense] = low[dense]
-            high_edge[dense] = high[dense]
-    low_edge[DENSE - 1] = low[-1]
-    high_edge[DENSE - 1] = high[-1]
+            put(dense, low[dense], high[dense])
+    put(DENSE - 1, low[-1], high[-1])
 
 
 def own_kernel(span, basis, inv_root, scale, moments, strip_root, strip_source, strip_fixed, g, diag, *t):
@@ -238,7 +242,7 @@
     strip_fixed[...] = heads
 
 
-def strips_kernel(own_moments, own_root, own_source, own_fixed, from_low, from_high,
+def strips_kernel(own_moments, own_root, own_source, own_fixed, first_edge, second_edge,
                   basis, inv_root, scale, moments, root, source, g):
     lane = lane_index(8)
     low_lanes = high_lanes = lane < 0
@@ -247,17 +251,24 @@
         low_lanes = low_lanes | between(lane, base, base + EDGE)
         high_lanes = high_lanes | between(lane, base + PAIR - EDGE, base + PAIR)
 
-    def with_halo(own, dense, place=0):
-        low = turn(from_low[dense], EDGE - EDGE * place)
-        high = turn(from_high[dense], PAIR - EDGE - EDGE * place)
+    even = lax.rem(lax.axis_index("y"), 2) == 0
+
+    def from_sides(dense):
+        first, second = first_edge[dense], second_edge[dense]
+        return jnp.where(even, second, first), jnp.where(even, first, second)
+
+    def with_halo(own, sides, place=0):
+        low = turn(sides[0], EDGE - EDGE * place)
+        high = turn(sides[1], PAIR - EDGE - EDGE * place)
         return jnp.where(low_lanes, low, jnp.where(high_lanes, high, own))
 
-    fixed = with_halo(own_fixed[...], DENSE - 1)
+    fixed = with_halo(own_fixed[...], from_sides(DENSE - 1))
     for q in range(STRIPS):
+        root_sides, source_sides = from_sides(2 * q), from_sides(2 * q + 1)
         for k in range(TILES):
             tile = pl.ds(8 * k, 8)
-            root[q, tile] = with_halo(own_root[q, tile], 2 * q, k)
-            source[q, tile] = with_halo(own_source[q, tile], 2 * q + 1, k)
+            root[q, tile] = with_halo(own_root[q, tile], root_sides, k)
+            source[q, tile] = with_halo(own_source[q, tile], source_sides, k)
 
     def sums(ref, at):
         rows = [ref[(*at, q)] for q in range(STRIPS)]
@@ -451,10 +462,10 @@
     return call(own_kernel, outs, scratches)(span)
 
 
-def strip_columns(moments, own, from_low, from_high):
+def strip_columns(moments, own, first_edge, second_edge):
     field = f32(STRIPS, LAYERS, LANES)
     outs = (f32(BASIS, STRIPS, LAYERS, LANES), field, field, f32(1, LANES))
-    return call(strips_kernel, outs, [scratch(STRIPS, LAYERS, LANES)] * 3)(moments, *own, from_low, from_high)
+    return call(strips_kernel, outs, [scratch(STRIPS, LAYERS, LANES)] * 3)(moments, *own, first_edge, second_edge)
 
 
 def combine(moments, own, strips):
@@ -468,19 +479,11 @@
     return tuple(out.reshape(LAYERS, ROWS, LANES) for out in outs)
 
 
-def shift_both(low_going, high_going, axis):
-    count = lax.axis_size(axis)
-    up = [(i, i + 1) for i in range(count - 1)]
-    down = [(target, source) for source, target in up]
-    return lax.ppermute(high_going, axis, up), lax.ppermute(low_going, axis, down)
-
-
-def between_chips(array):
-    count = lax.axis_size(GX)
+def swap(array, axis, start):
     pairs = []
-    for i in range(1, count - 1, 2):
+    for i in range(start, lax.axis_size(axis) - 1, 2):
         pairs += [(i, i + 1), (i + 1, i)]
-    return lax.ppermute(array, GX, pairs)
+    return lax.ppermute(array, axis, pairs)
 
 
 def spread_sum(row, axes, leader):
@@ -492,12 +495,13 @@
 
 def local(recharge, conduct, top_layer, fixed_head):
     main, part = prepare(recharge, conduct, top_layer, fixed_head)
-    far = between_chips(part)
+    far = swap(part, GX, 1)
     both = lax.all_gather(main, "c", axis=0, tiled=True)
-    span, low_edge, high_edge = edges(both, far)
-    from_low, from_high = shift_both(low_edge, high_edge, "y")
+    span, first_edge, second_edge = edges(both, far)
+    first_edge = swap(first_edge, "y", 0)
+    second_edge = swap(second_edge, "y", 1)
     *own, own_moments, root, source, fixed = own_columns(span)
-    *strips, moments = strip_columns(own_moments, (root, source, fixed), from_low, from_high)
+    *strips, moments = strip_columns(own_moments, (root, source, fixed), first_edge, second_edge)
     moments = jnp.sum(spread_sum(moments, ("z", "c"), 7 * 2 + 1), axis=0)
     moments = spread_sum(moments, ("x", "y"), 2 * 8 + 4)
     return combine(moments, own, strips)

time: 61.5 us -> 60 us (0.976)
  blocking collectives: 45 us -> 43.9 us
    all_to_all x2, blocking collectives: 36.2 us -> 35.2 us  [spread_sum(): lax.all_to_all(rows, axes, 0, 0, axis_index_groups=[group], tiled=True)]
  transfers between devices with their start and end apart: 3 -> 3, of which waited for: 1 -> 0; matrix products, arithmetic and copies ran while one was open for 0% -> 0% of each run, Pallas kernels for 5% -> 5%
where the time goes in v7:
time: 60 us; the launch traced here: 59.2 us
  blocking collectives  43.9 us (73%)
  Pallas kernels  7.47 us (12%)
  starting transfers between devices  7.08 us (12%)
  between operations  0.71 us (1%)
    all_to_all x2, blocking collectives, spread_sum(): lax.all_to_all(rows, axes, 0, 0, axis_index_groups=[group], tiled=True)  35.2 us
    all_gather x1, blocking collectives, local(): both = lax.all_gather(main, 'c', axis=0, tiled=True)  8.73 us
    pallas_call x5, Pallas kernels, run(): pl.pallas_call(kernel, out_shape=outs, in_specs=[ins] * len(args), out_sp...  7.47 us
    ppermute x3, starting transfers between devices, swap(): return lax.ppermute(array, axis, pairs)  7.08 us
  transfers between devices with their start and end apart: 3, of which 0 were waited for; matrix products, arithmetic and copies ran while one was open for 0% of the time, Pallas kernels for 5%

profile of v7, /device:TPU:1, one launch (start us, length us, event | category | flops | bytes accessed | tf_op | source)
XLA Modules:
  0.0 59.2 jit_solution(6289064124375638832)
XLA Ops:
  0.6 1.2 %shard_map.67 = (f32[8,104,128]{2,1,0:T(8,128)S(1)}, f32[536,128]{1,0:T(8,128)S(1)}) custom-call(f32[384,128]{1,0:T(8,128)} %bitcast.8, f32[384,128]{1,0:T(8,128)} %bitcast.9, s32[8,128]{1,0:T(8,128)} %top_layer.1, s32[8,128]{1,0:T(8,128)} %fixed_head.1), custom_call_target="tpu_custom_call" | custom-call | tf_op jit(solution)/shard_map/pallas_call | solution.py:428
  1.8 4.5 %collective-permute-start = (f32[536,128]{1,0:T(8,128)S(1)}, f32[536,128]{1,0:T(8,128)S(1)}, u32[]{:S(2)}, u32[]{:S(2)}) collective-permute-start(f32[536,128]{1,0:T(8,128)S(1)} %get-tuple-element.23), channel_id=1, source_target_pairs={{8,16},{16,8},{24,32},{32,24},{40,48},{48,40},{56,64},{64,56},{72,... | collective-permute-start | bytes 823304 | tf_op jit(solution)/shard_map/ppermute | solution.py:486
  6.3 8.7 %all_gather.3.both = f32[16,104,128]{2,1,0:T(8,128)S(1)} all-gather(f32[8,104,128]{2,1,0:T(8,128)S(1)} %get-tuple-element.22), channel_id=1, replica_groups=mesh['z'=12,'x'=4,'c'=2,'y'=8] {'c'}, dimensions={0}, use_global_device_ids=true | all-gather | bytes 1277952 | tf_op jit(solution)/shard_map/all_gather | solution.py:499
  15.1 0.0 collective-permute-done.far
  15.1 0.4 shard_map.68
  15.5 1.9 %collective-permute-start.1 = (f32[15,8,128]{2,1,0:T(8,128)S(1)}, f32[15,8,128]{2,1,0:T(8,128)S(1)}, u32[]{:S(2)}, u32[]{:S(2)}) collective-permute-start(f32[15,8,128]{2,1,0:T(8,128)S(1)} %get-tuple-element.29), channel_id=1, source_target_pairs={{0,1},{1,0},{2,3},{3,2},{4,5},{5,4},{6,7},{7,6},{8,9},{9,8},{10,11... | collective-permute-start | bytes 184328 | tf_op jit(solution)/shard_map/ppermute | solution.py:486
  17.4 0.7 %collective-permute-start.2 = (f32[15,8,128]{2,1,0:T(8,128)S(1)}, f32[15,8,128]{2,1,0:T(8,128)S(1)}, u32[]{:S(2)}, u32[]{:S(2)}) collective-permute-start(f32[15,8,128]{2,1,0:T(8,128)S(1)} %get-tuple-element.30), channel_id=1, source_target_pairs={{1,2},{2,1},{3,4},{4,3},{5,6},{6,5},{9,10},{10,9},{11,12},{12,11},... | collective-permute-start | bytes 184328 | tf_op jit(solution)/shard_map/ppermute | solution.py:486
  18.1 3.2 %shard_map.69 = (f32[6,8,48,128]{3,2,1,0:T(8,128)S(1)}, f32[8,48,128]{2,1,0:T(8,128)S(1)}, f32[8,48,128]{2,1,0:T(8,128)S(1)}, f32[1,128]{1,0:T(1,128)S(1)}, f32[...) custom-call(f32[20,104,128]{2,1,0:T(8,128)S(1)} %get-tuple-element.24.span), custom_call_target="tpu_custom_call" | custom-call | tf_op jit(solution)/shard_map/pallas_call | solution.py:428
  21.3 0.0 collective-permute-done.1.first_edge
  21.3 0.0 collective-permute-done.2.second_edge
  21.3 1.3 %shard_map.70 = (f32[6,7,48,128]{3,2,1,0:T(8,128)S(1)}, f32[7,48,128]{2,1,0:T(8,128)S(1)}, f32[7,48,128]{2,1,0:T(8,128)S(1)}, f32[1,128]{1,0:T(1,128)S(1)}) custom-call(f32[1,128]{1,0:T(1,128)S(1)} %get-tuple-element.25.own_moments, f32[7,48,128]{2,1,0:T(8,128)S(1)} %get-tuple-element.26.own_root, f32[7,48,128]{2,1,0:T(8,128)S(1)} %get-tuple-element.27.own_source, ...), custom_call_target="tpu_custom_call" | custom-call | tf_op jit(solution)/shard_map/pallas_call | solution.py:428
  22.6 21.2 %all_to_all.10 = f32[24,1,128]{2,1,0:T(1,128)S(1)} all-to-all(f32[24,1,128]{2,1,0:T(1,128)S(1)} %broadcast_in_dim.7), channel_id=1, replica_groups={{456,512,520,576,584,640,648,704,712,0,8,64,72,128,136,192,200,256,264,..., dimensions={0} | all-to-all | bytes 24576 | tf_op jit(solution)/shard_map/all_to_all | solution.py:493
  43.8 14.0 %all_to_all.11.moments = f32[32,1,128]{2,1,0:T(1,128)S(1)} all-to-all(f32[32,1,128]{2,1,0:T(1,128)S(1)} %broadcast_in_dim.16), channel_id=1, replica_groups={{36,37,38,39,48,49,50,51,52,53,54,55,0,1,2,3,4,5,6,7,16,17,18,19,20,21,..., dimensions={0} | all-to-all | bytes 32768 | tf_op jit(solution)/shard_map/all_to_all | solution.py:493
  57.8 1.4 %shard_map.71 = (f32[384,128]{1,0:T(8,128)}, f32[384,128]{1,0:T(8,128)}, f32[384,128]{1,0:T(8,128)}) custom-call(f32[32,1,128]{2,1,0:T(1,128)S(1)} %all_to_all.11.moments, f32[6,8,48,128]{3,2,1,0:T(8,128)S(1)} %get-tuple-element.32.basis, f32[8,48,128]{2,1,0:T(8,128)S(1)} %get-tuple-element.33.inv_root, f32[8,48,128]{2,1,0:T(8,128)S(1)} %get-tuple-element.34.scale, ...), custom_call_target="tpu_custom_call" | custom-call | tf_op jit(solution)/shard_map/pallas_call | solution.py:428
  (3 shorter events, 0.0 us)
Async XLA Ops:
  1.8 13.2 %collective-permute-start = (f32[536,128]{1,0:T(8,128)S(1)}, f32[536,128]{1,0:T(8,128)S(1)}, u32[]{:S(2)}, u32[]{:S(2)}) collective-permute-start(f32[536,128]{1,0:T(8,128)S(1)} %get-tuple-element.23), channel_id=1, source_target_pairs={{8,16},{16,8},{24,32},{32,24},{40,48},{48,40},{56,64},{64,56},{72,... | collective-permute-start | bytes 823304 | tf_op jit(solution)/shard_map/ppermute | solution.py:486
  15.5 5.8 %collective-permute-start.1 = (f32[15,8,128]{2,1,0:T(8,128)S(1)}, f32[15,8,128]{2,1,0:T(8,128)S(1)}, u32[]{:S(2)}, u32[]{:S(2)}) collective-permute-start(f32[15,8,128]{2,1,0:T(8,128)S(1)} %get-tuple-element.29), channel_id=1, source_target_pairs={{0,1},{1,0},{2,3},{3,2},{4,5},{5,4},{6,7},{7,6},{8,9},{9,8},{10,11... | collective-permute-start | bytes 184328 | tf_op jit(solution)/shard_map/ppermute | solution.py:486
  17.4 3.9 %collective-permute-start.2 = (f32[15,8,128]{2,1,0:T(8,128)S(1)}, f32[15,8,128]{2,1,0:T(8,128)S(1)}, u32[]{:S(2)}, u32[]{:S(2)}) collective-permute-start(f32[15,8,128]{2,1,0:T(8,128)S(1)} %get-tuple-element.30), channel_id=1, source_target_pairs={{1,2},{2,1},{3,4},{4,3},{5,6},{6,5},{9,10},{10,9},{11,12},{12,11},... | collective-permute-start | bytes 184328 | tf_op jit(solution)/shard_map/ppermute | solution.py:486

commit v8 on v7

--- a/solution.py
+++ b/solution.py
@@ -131,55 +131,114 @@
         main[row, 2 * LAYERS:] = jnp.broadcast_to(fixed[row:row + 1], (8, LANES))
 
 
-def units(strip):
-    for slot in range(FOLD):
-        row = slot * STRIPS + strip
-        if row < SPAN:
-            for unit in range(2 * TILES):
-                group, place = divmod(unit, TILES)
-                yield 2 * strip + group, place, slot, row, 8 * unit
-            yield DENSE - 1, 0, slot, row, 2 * LAYERS
-
-
-def edges_kernel(both, far, span, first_edge, second_edge):
-    even = lax.rem(lax.axis_index("y"), 2) == 0
-
-    def put(dense, low, high):
-        first_edge[dense] = jnp.where(even, high, low)
-        second_edge[dense] = jnp.where(even, low, high)
-
+def on_each_core(body):
     core = lax.axis_index("c")
-    for n in range(ROWS + DEPTH):
-        span[DEPTH * (1 - core) + n] = both[(ROWS - DEPTH) * core + n]
-    for n in range(DEPTH):
-        row = jnp.where(core == 0, DEPTH - 1 - n, ROWS + DEPTH + n)
-        span[row, :LAYERS] = far[n * LAYERS:(n + 1) * LAYERS]
-        if n < DEPTH - 1:
-            span[row, LAYERS:2 * LAYERS] = far[(DEPTH + n) * LAYERS:(DEPTH + n + 1) * LAYERS]
-        else:
-            span[row, LAYERS:2 * LAYERS] = jnp.zeros((LAYERS, LANES), jnp.float32)
-        fixed = far[pl.ds(FAR - 8 + jnp.where(core == 0, ROWS - 1 - n, n), 1)]
-        span[row, 2 * LAYERS:] = jnp.broadcast_to(fixed, (8, LANES))
+    for which in range(2):
+        @pl.when(core == which)
+        def _(which=which):
+            near = range(DEPTH, SPAN) if which == 0 else range(SPAN - DEPTH)
+            body(which, near, [row for row in range(SPAN) if row not in near])
+
+
+def add_units(low, high, row, read):
     lane = lane_index(8)
     sublane = lax.broadcasted_iota(jnp.int32, (8, LANES), 0)
-    blank = jnp.zeros((8, LANES), jnp.float32)
-    low, high = [blank] * DENSE, [blank] * DENSE
-    for strip in range(STRIPS):
-        for dense, place, slot, row, at in units(strip):
-            to = PAIR * slot + EDGE * place
-            turned = turn(span[row, at:at + 8], to)
-            back = (to - EDGE) % LANES
-            take_low, take_high = between(lane, to, to + EDGE), between(lane, back, back + EDGE)
-            if dense == DENSE - 1:
-                take_low, take_high = take_low & (sublane == strip), take_high & (sublane == strip)
-            low[dense] = jnp.where(take_low, turned, low[dense])
-            high[dense] = jnp.where(take_high, turned, high[dense])
-        for dense in (2 * strip, 2 * strip + 1):
-            put(dense, low[dense], high[dense])
-    put(DENSE - 1, low[-1], high[-1])
-
-
-def own_kernel(span, basis, inv_root, scale, moments, strip_root, strip_source, strip_fixed, g, diag, *t):
+    slot, strip = divmod(row, STRIPS)
+    for unit in range(2 * TILES + 1):
+        group, place = divmod(unit, TILES)
+        dense, to = 2 * strip + group, PAIR * slot + EDGE * place
+        if unit == 2 * TILES:
+            dense, to = DENSE - 1, PAIR * slot
+        back = (to - EDGE) % LANES
+        take_low, take_high = between(lane, to, to + EDGE), between(lane, back, back + EDGE)
+        if dense == DENSE - 1:
+            take_low, take_high = take_low & (sublane == strip), take_high & (sublane == strip)
+        turned = turn(read(8 * unit), to)
+        for tiles, take in ((low, take_low), (high, take_high)):
+            tiles[dense] = jnp.where(take, turned, 0.0 if tiles[dense] is None else tiles[dense])
+
+
+def add_own(tiles, row, read):
+    lane = lane_index(8)
+    sublane = lax.broadcasted_iota(jnp.int32, (8, LANES), 0)
+    slot, strip = divmod(row, STRIPS)
+    base = PAIR * slot
+    for unit in range(2 * TILES + 1):
+        source = read(8 * unit)
+        key = (strip, unit) if unit < 2 * TILES else None
+        take_low = between(lane, base + EDGE, base + SIDE)
+        take_high = between(lane, base + SIDE, base + PAIR - EDGE)
+        if key is None:
+            take_low, take_high = take_low & (sublane == strip), take_high & (sublane == strip)
+        tile = jnp.where(take_low, turn(source, base + EDGE), tiles.get(key, 0.0))
+        tiles[key] = jnp.where(take_high, turn(source, base + PAIR - EDGE), tile)
+
+
+def strip_place(refs, key):
+    root, source, fixed = refs
+    if key is None:
+        return fixed, ...
+    strip, unit = key
+    ref = root if unit < TILES else source
+    return ref, (strip, pl.ds(8 * (unit % TILES), 8))
+
+
+def near_kernel(both, low_edge, high_edge, *strip_refs):
+    def body(which, near, _):
+        shift = -DEPTH if which == 0 else ROWS - DEPTH
+        low, high, strips = [None] * DENSE, [None] * DENSE, {}
+        for row in near:
+            def read(at, row=row):
+                return both[row + shift, at:at + 8]
+
+            add_units(low, high, row, read)
+            add_own(strips, row, read)
+        for n in range(DENSE):
+            low_edge[n] = low[n]
+            high_edge[n] = high[n]
+        for key, tile in strips.items():
+            ref, at = strip_place(strip_refs, key)
+            ref[at] = tile
+
+    on_each_core(body)
+
+
+def far_row(far, which, row):
+    n = DEPTH - 1 - row if which == 0 else row - ROWS - DEPTH
+    at = FAR - 8 + (ROWS - 1 - n if which == 0 else n)
+    root = far[n * LAYERS:(n + 1) * LAYERS]
+    if n < DEPTH - 1:
+        source = far[(DEPTH + n) * LAYERS:(DEPTH + n + 1) * LAYERS]
+    else:
+        source = jnp.zeros((LAYERS, LANES), jnp.float32)
+    return jnp.concatenate([root, source, jnp.broadcast_to(far[at:at + 1], (8, LANES))], axis=0)
+
+
+def edges_kernel(near_low, near_high, far, first_edge, second_edge):
+    even = lax.rem(lax.axis_index("y"), 2) == 0
+
+    def body(which, _, rows):
+        low, high = [near_low[n] for n in range(DENSE)], [near_high[n] for n in range(DENSE)]
+        for row in rows:
+            values = far_row(far, which, row)
+            add_units(low, high, row, lambda at, values=values: values[at:at + 8])
+        for n in range(DENSE):
+            first_edge[n] = jnp.where(even, high[n], low[n])
+            second_edge[n] = jnp.where(even, low[n], high[n])
+
+    on_each_core(body)
+
+
+def own_kernel(both, far, near_root, near_source, near_fixed, basis, inv_root, scale, moments,
+               strip_root, strip_source, strip_fixed, span, g, diag, *t):
+    def fill(which, near, rows):
+        for row in near:
+            span[row] = both[row - DEPTH if which == 0 else row + ROWS - DEPTH]
+        for row in rows:
+            span[row] = far_row(far, which, row)
+
+    on_each_core(fill)
+
     def start(i):
         row = i + 1
         root = span[row, :LAYERS]
@@ -220,26 +279,24 @@
     zero = jnp.zeros((LAYERS, LANES), jnp.float32)
     moments[...] = as_row(lax.fori_loop(0, ROWS // unroll, finish, (zero,) * (2 * ITERS)))
 
-    lane = lane_index(8)
-    sublane = lax.broadcasted_iota(jnp.int32, (8, LANES), 0)
-    heads = jnp.zeros((8, LANES), jnp.float32)
-    for strip in range(STRIPS):
-        for unit in range(2 * TILES + 1):
-            tile = jnp.zeros((8, LANES), jnp.float32)
-            for slot in range(FOLD):
-                row = slot * STRIPS + strip
-                if row < SPAN:
-                    source, base = span[row, 8 * unit:8 * unit + 8], PAIR * slot
-                    low, high = turn(source, base + EDGE), turn(source, base + PAIR - EDGE)
-                    tile = jnp.where(between(lane, base + EDGE, base + SIDE), low, tile)
-                    tile = jnp.where(between(lane, base + SIDE, base + PAIR - EDGE), high, tile)
-            if unit < TILES:
-                strip_root[strip, 8 * unit:8 * unit + 8] = tile
-            elif unit < 2 * TILES:
-                strip_source[strip, 8 * unit - LAYERS:8 * unit - LAYERS + 8] = tile
-            else:
-                heads = jnp.where(sublane == strip, tile, heads)
-    strip_fixed[...] = heads
+    strip_root[...] = near_root[...]
+    strip_source[...] = near_source[...]
+    strip_fixed[...] = near_fixed[...]
+    refs = (strip_root, strip_source, strip_fixed)
+
+    def body(which, _, rows):
+        keys = [(row % STRIPS, unit) for row in rows for unit in range(2 * TILES)] + [None]
+        tiles = {}
+        for key in keys:
+            ref, at = strip_place(refs, key)
+            tiles[key] = ref[at]
+        for row in rows:
+            add_own(tiles, row, lambda at, row=row: span[row, at:at + 8])
+        for key, tile in tiles.items():
+            ref, at = strip_place(refs, key)
+            ref[at] = tile
+
+    on_each_core(body)
 
 
 def strips_kernel(own_moments, own_root, own_source, own_fixed, first_edge, second_edge,
@@ -449,17 +506,21 @@
     )(*[pltpu.with_memory_space_constraint(a, pltpu.HBM) for a in args])
 
 
-def edges(both, far):
-    dense = f32(DENSE, 8, LANES)
-    return call(edges_kernel, (f32(SPAN, WIDTH, LANES), dense, dense))(both, far)
-
-
-def own_columns(span):
+def near_rows(both):
+    dense, strip = f32(DENSE, 8, LANES), f32(STRIPS, LAYERS, LANES)
+    return call(near_kernel, (dense, dense, strip, strip, f32(8, LANES)))(both)
+
+
+def edges(near, far):
+    return call(edges_kernel, (f32(DENSE, 8, LANES),) * 2)(*near, far)
+
+
+def own_columns(both, far, near):
     field, strip = f32(ROWS, LAYERS, LANES), f32(STRIPS, LAYERS, LANES)
     outs = (f32(BASIS, ROWS, LAYERS, LANES), field, field, f32(1, LANES), strip, strip, f32(8, LANES))
-    scratches = [scratch(FIRST, LAYERS, LANES)] * 2
+    scratches = [scratch(SPAN, WIDTH, LANES)] + [scratch(FIRST, LAYERS, LANES)] * 2
     scratches += [scratch(FIRST - 2 * j, LAYERS, LANES) for j in range(ITERS + 1)]
-    return call(own_kernel, outs, scratches)(span)
+    return call(own_kernel, outs, scratches)(both, far, *near)
 
 
 def strip_columns(moments, own, first_edge, second_edge):
@@ -497,10 +558,11 @@
     main, part = prepare(recharge, conduct, top_layer, fixed_head)
     far = swap(part, GX, 1)
     both = lax.all_gather(main, "c", axis=0, tiled=True)
-    span, first_edge, second_edge = edges(both, far)
+    near = near_rows(both)
+    first_edge, second_edge = edges(near[:2], far)
     first_edge = swap(first_edge, "y", 0)
     second_edge = swap(second_edge, "y", 1)
-    *own, own_moments, root, source, fixed = own_columns(span)
+    *own, own_moments, root, source, fixed = own_columns(both, far, near[2:])
     *strips, moments = strip_columns(own_moments, (root, source, fixed), first_edge, second_edge)
     moments = jnp.sum(spread_sum(moments, ("z", "c"), 7 * 2 + 1), axis=0)
     moments = spread_sum(moments, ("x", "y"), 2 * 8 + 4)

time: 60 us -> 59.4 us (0.990)
  blocking collectives: 43.9 us -> 43.2 us
    all_to_all x2, blocking collectives: 35.2 us -> 34.5 us  [spread_sum(): lax.all_to_all(rows, axes, 0, 0, axis_index_groups=[group], tiled=True)]
    pallas_call x5 -> x6, Pallas kernels: 7.47 us -> 7.56 us  [run(): pl.pallas_call(kernel, out_shape=outs, in_specs=[ins] * len(args), out_sp...]
  transfers between devices with their start and end apart: 3 -> 3, of which waited for: 0 -> 0; matrix products, arithmetic and copies ran while one was open for 0% -> 0% of each run, Pallas kernels for 5% -> 6%
where the time goes in v8:
time: 59.4 us; the launch traced here: 58.6 us
  blocking collectives  43.2 us (73%)
  Pallas kernels  7.56 us (13%)
  starting transfers between devices  7.08 us (12%)
  between operations  0.72 us (1%)
    all_to_all x2, blocking collectives, spread_sum(): lax.all_to_all(rows, axes, 0, 0, axis_index_groups=[group], tiled=True)  34.5 us
    all_gather x1, blocking collectives, local(): both = lax.all_gather(main, 'c', axis=0, tiled=True)  8.73 us
    pallas_call x6, Pallas kernels, run(): pl.pallas_call(kernel, out_shape=outs, in_specs=[ins] * len(args), out_sp...  7.56 us
    ppermute x3, starting transfers between devices, swap(): return lax.ppermute(array, axis, pairs)  7.08 us
  transfers between devices with their start and end apart: 3, of which 0 were waited for; matrix products, arithmetic and copies ran while one was open for 0% of the time, Pallas kernels for 6%

profile of v8, /device:TPU:1, one launch (start us, length us, event | category | flops | bytes accessed | tf_op | source)
XLA Modules:
  0.0 58.6 jit_solution(13848009568101780771)
XLA Ops:
  0.6 1.2 %shard_map.67 = (f32[8,104,128]{2,1,0:T(8,128)S(1)}, f32[536,128]{1,0:T(8,128)S(1)}) custom-call(f32[384,128]{1,0:T(8,128)} %bitcast.8, f32[384,128]{1,0:T(8,128)} %bitcast.9, s32[8,128]{1,0:T(8,128)} %top_layer.1, s32[8,128]{1,0:T(8,128)} %fixed_head.1), custom_call_target="tpu_custom_call" | custom-call | tf_op jit(solution)/shard_map/pallas_call | solution.py:485
  1.8 4.5 %collective-permute-start = (f32[536,128]{1,0:T(8,128)S(1)}, f32[536,128]{1,0:T(8,128)S(1)}, u32[]{:S(2)}, u32[]{:S(2)}) collective-permute-start(f32[536,128]{1,0:T(8,128)S(1)} %get-tuple-element.27), channel_id=1, source_target_pairs={{8,16},{16,8},{24,32},{32,24},{40,48},{48,40},{56,64},{64,56},{72,... | collective-permute-start | bytes 823304 | tf_op jit(solution)/shard_map/ppermute | solution.py:547
  6.3 8.7 %all_gather.3.both = f32[16,104,128]{2,1,0:T(8,128)S(1)} all-gather(f32[8,104,128]{2,1,0:T(8,128)S(1)} %get-tuple-element.26), channel_id=1, replica_groups=mesh['z'=12,'x'=4,'c'=2,'y'=8] {'c'}, dimensions={0}, use_global_device_ids=true | all-gather | bytes 1277952 | tf_op jit(solution)/shard_map/all_gather | solution.py:560
  15.1 0.6 shard_map.68
  15.6 0.0 collective-permute-done.far
  15.6 0.2 shard_map.70
  15.8 1.9 %collective-permute-start.1 = (f32[15,8,128]{2,1,0:T(8,128)S(1)}, f32[15,8,128]{2,1,0:T(8,128)S(1)}, u32[]{:S(2)}, u32[]{:S(2)}) collective-permute-start(f32[15,8,128]{2,1,0:T(8,128)S(1)} %get-tuple-element.37), channel_id=1, source_target_pairs={{0,1},{1,0},{2,3},{3,2},{4,5},{5,4},{6,7},{7,6},{8,9},{9,8},{10,11... | collective-permute-start | bytes 184328 | tf_op jit(solution)/shard_map/ppermute | solution.py:547
  17.7 0.7 %collective-permute-start.2 = (f32[15,8,128]{2,1,0:T(8,128)S(1)}, f32[15,8,128]{2,1,0:T(8,128)S(1)}, u32[]{:S(2)}, u32[]{:S(2)}) collective-permute-start(f32[15,8,128]{2,1,0:T(8,128)S(1)} %get-tuple-element.38), channel_id=1, source_target_pairs={{1,2},{2,1},{3,4},{4,3},{5,6},{6,5},{9,10},{10,9},{11,12},{12,11},... | collective-permute-start | bytes 184328 | tf_op jit(solution)/shard_map/ppermute | solution.py:547
  18.4 2.9 %shard_map.69 = (f32[6,8,48,128]{3,2,1,0:T(8,128)S(1)}, f32[8,48,128]{2,1,0:T(8,128)S(1)}, f32[8,48,128]{2,1,0:T(8,128)S(1)}, f32[1,128]{1,0:T(1,128)S(1)}, f32[...) custom-call(f32[16,104,128]{2,1,0:T(8,128)S(1)} %all_gather.3.both, ...), custom_call_target="tpu_custom_call" | custom-call | tf_op jit(solution)/shard_map/pallas_call | solution.py:485
  21.4 0.0 collective-permute-done.1.first_edge
  21.4 0.0 collective-permute-done.2.second_edge
  21.4 1.3 %shard_map.71 = (f32[6,7,48,128]{3,2,1,0:T(8,128)S(1)}, f32[7,48,128]{2,1,0:T(8,128)S(1)}, f32[7,48,128]{2,1,0:T(8,128)S(1)}, f32[1,128]{1,0:T(1,128)S(1)}) custom-call(f32[1,128]{1,0:T(1,128)S(1)} %get-tuple-element.31.own_moments, f32[7,48,128]{2,1,0:T(8,128)S(1)} %get-tuple-element.32.own_root, f32[7,48,128]{2,1,0:T(8,128)S(1)} %get-tuple-element.33.own_source, ...), custom_call_target="tpu_custom_call" | custom-call | tf_op jit(solution)/shard_map/pallas_call | solution.py:485
  22.7 20.5 %all_to_all.10 = f32[24,1,128]{2,1,0:T(1,128)S(1)} all-to-all(f32[24,1,128]{2,1,0:T(1,128)S(1)} %broadcast_in_dim.7), channel_id=1, replica_groups={{456,512,520,576,584,640,648,704,712,0,8,64,72,128,136,192,200,256,264,..., dimensions={0} | all-to-all | bytes 24576 | tf_op jit(solution)/shard_map/all_to_all | solution.py:554
  43.2 14.0 %all_to_all.11.moments = f32[32,1,128]{2,1,0:T(1,128)S(1)} all-to-all(f32[32,1,128]{2,1,0:T(1,128)S(1)} %broadcast_in_dim.16), channel_id=1, replica_groups={{36,37,38,39,48,49,50,51,52,53,54,55,0,1,2,3,4,5,6,7,16,17,18,19,20,21,..., dimensions={0} | all-to-all | bytes 32768 | tf_op jit(solution)/shard_map/all_to_all | solution.py:554
  57.3 1.4 %shard_map.72 = (f32[384,128]{1,0:T(8,128)}, f32[384,128]{1,0:T(8,128)}, f32[384,128]{1,0:T(8,128)}) custom-call(f32[32,1,128]{2,1,0:T(1,128)S(1)} %all_to_all.11.moments, f32[6,8,48,128]{3,2,1,0:T(8,128)S(1)} %get-tuple-element.40.basis, f32[8,48,128]{2,1,0:T(8,128)S(1)} %get-tuple-element.41.inv_root, f32[8,48,128]{2,1,0:T(8,128)S(1)} %get-tuple-element.42.scale, ...), custom_call_target="tpu_custom_call" | custom-call | tf_op jit(solution)/shard_map/pallas_call | solution.py:485
  (3 shorter events, 0.0 us)
Async XLA Ops:
  1.8 13.8 %collective-permute-start = (f32[536,128]{1,0:T(8,128)S(1)}, f32[536,128]{1,0:T(8,128)S(1)}, u32[]{:S(2)}, u32[]{:S(2)}) collective-permute-start(f32[536,128]{1,0:T(8,128)S(1)} %get-tuple-element.27), channel_id=1, source_target_pairs={{8,16},{16,8},{24,32},{32,24},{40,48},{48,40},{56,64},{64,56},{72,... | collective-permute-start | bytes 823304 | tf_op jit(solution)/shard_map/ppermute | solution.py:547
  15.8 5.6 %collective-permute-start.1 = (f32[15,8,128]{2,1,0:T(8,128)S(1)}, f32[15,8,128]{2,1,0:T(8,128)S(1)}, u32[]{:S(2)}, u32[]{:S(2)}) collective-permute-start(f32[15,8,128]{2,1,0:T(8,128)S(1)} %get-tuple-element.37), channel_id=1, source_target_pairs={{0,1},{1,0},{2,3},{3,2},{4,5},{5,4},{6,7},{7,6},{8,9},{9,8},{10,11... | collective-permute-start | bytes 184328 | tf_op jit(solution)/shard_map/ppermute | solution.py:547
  17.7 3.6 %collective-permute-start.2 = (f32[15,8,128]{2,1,0:T(8,128)S(1)}, f32[15,8,128]{2,1,0:T(8,128)S(1)}, u32[]{:S(2)}, u32[]{:S(2)}) collective-permute-start(f32[15,8,128]{2,1,0:T(8,128)S(1)} %get-tuple-element.38), channel_id=1, source_target_pairs={{1,2},{2,1},{3,4},{4,3},{5,6},{6,5},{9,10},{10,9},{11,12},{12,11},... | collective-permute-start | bytes 184328 | tf_op jit(solution)/shard_map/ppermute | solution.py:547

commit v9 on v8

--- a/solution.py
+++ b/solution.py
@@ -564,7 +564,7 @@
     second_edge = swap(second_edge, "y", 1)
     *own, own_moments, root, source, fixed = own_columns(both, far, near[2:])
     *strips, moments = strip_columns(own_moments, (root, source, fixed), first_edge, second_edge)
-    moments = jnp.sum(spread_sum(moments, ("z", "c"), 7 * 2 + 1), axis=0)
+    moments = jnp.sum(spread_sum(moments, ("z", "c"), 8 * 2), axis=0)
     moments = spread_sum(moments, ("x", "y"), 2 * 8 + 4)
     return combine(moments, own, strips)
 

time: 59.4 us -> 59.7 us (level)
  no operation moved by 1% of the time
where the time goes in v9:
time: 59.7 us; the launch traced here: 58.9 us
  blocking collectives  43.5 us (73%)
  Pallas kernels  7.56 us (13%)
  starting transfers between devices  7.08 us (12%)
  between operations  0.72 us (1%)
    all_to_all x2, blocking collectives, spread_sum(): lax.all_to_all(rows, axes, 0, 0, axis_index_groups=[group], tiled=True)  34.8 us
    all_gather x1, blocking collectives, local(): both = lax.all_gather(main, 'c', axis=0, tiled=True)  8.73 us
    pallas_call x6, Pallas kernels, run(): pl.pallas_call(kernel, out_shape=outs, in_specs=[ins] * len(args), out_sp...  7.56 us
    ppermute x3, starting transfers between devices, swap(): return lax.ppermute(array, axis, pairs)  7.08 us
  transfers between devices with their start and end apart: 3, of which 0 were waited for; matrix products, arithmetic and copies ran while one was open for 0% of the time, Pallas kernels for 6%

profile of v9, /device:TPU:1, one launch (start us, length us, event | category | flops | bytes accessed | tf_op | source)
XLA Modules:
  0.0 58.9 jit_solution(2677601637499934238)
XLA Ops:
  0.6 1.2 %shard_map.67 = (f32[8,104,128]{2,1,0:T(8,128)S(1)}, f32[536,128]{1,0:T(8,128)S(1)}) custom-call(f32[384,128]{1,0:T(8,128)} %bitcast.8, f32[384,128]{1,0:T(8,128)} %bitcast.9, s32[8,128]{1,0:T(8,128)} %top_layer.1, s32[8,128]{1,0:T(8,128)} %fixed_head.1), custom_call_target="tpu_custom_call" | custom-call | tf_op jit(solution)/shard_map/pallas_call | solution.py:485
  1.8 4.5 %collective-permute-start = (f32[536,128]{1,0:T(8,128)S(1)}, f32[536,128]{1,0:T(8,128)S(1)}, u32[]{:S(2)}, u32[]{:S(2)}) collective-permute-start(f32[536,128]{1,0:T(8,128)S(1)} %get-tuple-element.27), channel_id=1, source_target_pairs={{8,16},{16,8},{24,32},{32,24},{40,48},{48,40},{56,64},{64,56},{72,... | collective-permute-start | bytes 823304 | tf_op jit(solution)/shard_map/ppermute | solution.py:547
  6.3 8.7 %all_gather.3.both = f32[16,104,128]{2,1,0:T(8,128)S(1)} all-gather(f32[8,104,128]{2,1,0:T(8,128)S(1)} %get-tuple-element.26), channel_id=1, replica_groups=mesh['z'=12,'x'=4,'c'=2,'y'=8] {'c'}, dimensions={0}, use_global_device_ids=true | all-gather | bytes 1277952 | tf_op jit(solution)/shard_map/all_gather | solution.py:560
  15.1 0.6 shard_map.68
  15.6 0.0 collective-permute-done.far
  15.6 0.2 shard_map.70
  15.8 1.9 %collective-permute-start.1 = (f32[15,8,128]{2,1,0:T(8,128)S(1)}, f32[15,8,128]{2,1,0:T(8,128)S(1)}, u32[]{:S(2)}, u32[]{:S(2)}) collective-permute-start(f32[15,8,128]{2,1,0:T(8,128)S(1)} %get-tuple-element.37), channel_id=1, source_target_pairs={{0,1},{1,0},{2,3},{3,2},{4,5},{5,4},{6,7},{7,6},{8,9},{9,8},{10,11... | collective-permute-start | bytes 184328 | tf_op jit(solution)/shard_map/ppermute | solution.py:547
  17.7 0.7 %collective-permute-start.2 = (f32[15,8,128]{2,1,0:T(8,128)S(1)}, f32[15,8,128]{2,1,0:T(8,128)S(1)}, u32[]{:S(2)}, u32[]{:S(2)}) collective-permute-start(f32[15,8,128]{2,1,0:T(8,128)S(1)} %get-tuple-element.38), channel_id=1, source_target_pairs={{1,2},{2,1},{3,4},{4,3},{5,6},{6,5},{9,10},{10,9},{11,12},{12,11},... | collective-permute-start | bytes 184328 | tf_op jit(solution)/shard_map/ppermute | solution.py:547
  18.4 2.9 %shard_map.69 = (f32[6,8,48,128]{3,2,1,0:T(8,128)S(1)}, f32[8,48,128]{2,1,0:T(8,128)S(1)}, f32[8,48,128]{2,1,0:T(8,128)S(1)}, f32[1,128]{1,0:T(1,128)S(1)}, f32[...) custom-call(f32[16,104,128]{2,1,0:T(8,128)S(1)} %all_gather.3.both, ...), custom_call_target="tpu_custom_call" | custom-call | tf_op jit(solution)/shard_map/pallas_call | solution.py:485
  21.4 0.0 collective-permute-done.1.first_edge
  21.4 0.0 collective-permute-done.2.second_edge
  21.4 1.3 %shard_map.71 = (f32[6,7,48,128]{3,2,1,0:T(8,128)S(1)}, f32[7,48,128]{2,1,0:T(8,128)S(1)}, f32[7,48,128]{2,1,0:T(8,128)S(1)}, f32[1,128]{1,0:T(1,128)S(1)}) custom-call(f32[1,128]{1,0:T(1,128)S(1)} %get-tuple-element.31.own_moments, f32[7,48,128]{2,1,0:T(8,128)S(1)} %get-tuple-element.32.own_root, f32[7,48,128]{2,1,0:T(8,128)S(1)} %get-tuple-element.33.own_source, ...), custom_call_target="tpu_custom_call" | custom-call | tf_op jit(solution)/shard_map/pallas_call | solution.py:485
  22.7 20.8 %all_to_all.10 = f32[24,1,128]{2,1,0:T(1,128)S(1)} all-to-all(f32[24,1,128]{2,1,0:T(1,128)S(1)} %broadcast_in_dim.7), channel_id=1, replica_groups={{512,520,576,584,640,648,704,712,0,8,64,72,128,136,192,200,256,264,320,..., dimensions={0} | all-to-all | bytes 24576 | tf_op jit(solution)/shard_map/all_to_all | solution.py:554
  43.5 14.0 %all_to_all.11.moments = f32[32,1,128]{2,1,0:T(1,128)S(1)} all-to-all(f32[32,1,128]{2,1,0:T(1,128)S(1)} %broadcast_in_dim.16), channel_id=1, replica_groups={{36,37,38,39,48,49,50,51,52,53,54,55,0,1,2,3,4,5,6,7,16,17,18,19,20,21,..., dimensions={0} | all-to-all | bytes 32768 | tf_op jit(solution)/shard_map/all_to_all | solution.py:554
  57.5 1.4 %shard_map.72 = (f32[384,128]{1,0:T(8,128)}, f32[384,128]{1,0:T(8,128)}, f32[384,128]{1,0:T(8,128)}) custom-call(f32[32,1,128]{2,1,0:T(1,128)S(1)} %all_to_all.11.moments, f32[6,8,48,128]{3,2,1,0:T(8,128)S(1)} %get-tuple-element.40.basis, f32[8,48,128]{2,1,0:T(8,128)S(1)} %get-tuple-element.41.inv_root, f32[8,48,128]{2,1,0:T(8,128)S(1)} %get-tuple-element.42.scale, ...), custom_call_target="tpu_custom_call" | custom-call | tf_op jit(solution)/shard_map/pallas_call | solution.py:485
  (3 shorter events, 0.0 us)
Async XLA Ops:
  1.8 13.8 %collective-permute-start = (f32[536,128]{1,0:T(8,128)S(1)}, f32[536,128]{1,0:T(8,128)S(1)}, u32[]{:S(2)}, u32[]{:S(2)}) collective-permute-start(f32[536,128]{1,0:T(8,128)S(1)} %get-tuple-element.27), channel_id=1, source_target_pairs={{8,16},{16,8},{24,32},{32,24},{40,48},{48,40},{56,64},{64,56},{72,... | collective-permute-start | bytes 823304 | tf_op jit(solution)/shard_map/ppermute | solution.py:547
  15.8 5.6 %collective-permute-start.1 = (f32[15,8,128]{2,1,0:T(8,128)S(1)}, f32[15,8,128]{2,1,0:T(8,128)S(1)}, u32[]{:S(2)}, u32[]{:S(2)}) collective-permute-start(f32[15,8,128]{2,1,0:T(8,128)S(1)} %get-tuple-element.37), channel_id=1, source_target_pairs={{0,1},{1,0},{2,3},{3,2},{4,5},{5,4},{6,7},{7,6},{8,9},{9,8},{10,11... | collective-permute-start | bytes 184328 | tf_op jit(solution)/shard_map/ppermute | solution.py:547
  17.7 3.6 %collective-permute-start.2 = (f32[15,8,128]{2,1,0:T(8,128)S(1)}, f32[15,8,128]{2,1,0:T(8,128)S(1)}, u32[]{:S(2)}, u32[]{:S(2)}) collective-permute-start(f32[15,8,128]{2,1,0:T(8,128)S(1)} %get-tuple-element.38), channel_id=1, source_target_pairs={{1,2},{2,1},{3,4},{4,3},{5,6},{6,5},{9,10},{10,9},{11,12},{12,11},... | collective-permute-start | bytes 184328 | tf_op jit(solution)/shard_map/ppermute | solution.py:547
